TPU v7x, 32 devices: a whole 2x2x4 slice. The times are simulated.
32 devices in a mesh: groups: 2 (over y), ep: 8 (over z, x), tp: 2 (over core).
Axes of the slice: x: 2, y: 2, z: 4, core: 2. Of those that a mesh axis runs over, the one named last changes fastest.
Arguments:
- hidden: bfloat16 [2, 128, 3584], P(None, ('groups', 'ep')), parts along dimension 1, may hold values from -6 to 6
- norm_gain: bfloat16 [3584], replicated, may hold values from 0.25 to 1.75
- expert_ids: int32 [2, 128, 1], P(None, ('groups', 'ep')), parts along dimension 1, may hold values from 0 to 1, as said below
- shares: float32 [2, 128, 1], P(None, ('groups', 'ep')), parts along dimension 1, may hold values from 0.1 to 1
- slot_index: int32 [2, 128, 1], P(None, ('groups', 'ep')), parts along dimension 1, may hold values from -1 to 3, as said below
- w_gate: bfloat16 [3584, 2048], P(None, ('ep', 'tp')), may hold values from -0.09375 to 0.09375
- w_up: bfloat16 [3584, 2048], P(None, ('ep', 'tp')), may hold values from -0.09375 to 0.09375
- w_down: bfloat16 [2048, 3584], P(('ep', 'tp')), may hold values from -0.1875 to 0.1875
Outputs:
- mixed: bfloat16 [2, 128, 3584], P(None, ('groups', 'ep'), 'tp'), parts along dimension 1
There are 2 independent parts, one for each index of `groups`. A program takes and returns all parts, laid end to end along the dimension named above; an argument that names none is the same for every part. Nothing has to cross between parts.
Inputs may be any that keep to these rules, and one draw needn't show every extreme that they name: `expert_ids`: each row names 1 expert. `slot_index`: -1 marks a dropped choice. Within one micro-batch and one aligned block of 8 rows, the choices naming one expert take slots 0, 1, 2, ... in row order, and a choice is dropped exactly when 4 earlier rows of its block name the same expert.
All inputs are finite; a program needn't handle non-finite values.
Results may differ from a plain program's by a relative error of at most 0.0055.
Values may be sent and summed in bfloat16 or wider, within the bound.
No kernel may reach another device: no remote copies, remote signals or barrier semaphores. Data moves between devices by JAX's collectives and lax.ppermute only.
A program may use at most 64 MiB of HBM per device.

v0:
```python
import jax
import jax.numpy as jnp
from jax import lax
from jax.sharding import PartitionSpec as P

FF = 1024
SLICE = 128


def slot_places(chosen, placed, node_size, capacity, ep_count, member):
    target = chosen * node_size + member
    return jnp.where(placed >= 0, target * capacity + placed, ep_count * capacity)


def fill_buffer(source_rows, place_list, ep_count, capacity):
    row_count = source_rows.shape[0]
    row_ids = jnp.broadcast_to(jnp.arange(row_count, dtype=jnp.int32)[:, None], place_list[0].shape)
    row_table = jnp.full((ep_count * capacity + 1,), row_count, jnp.int32)
    for place in place_list:
        row_table = row_table.at[place.reshape(-1)].set(row_ids.reshape(-1))
    padded = jnp.concatenate(
        [source_rows, jnp.zeros((1, source_rows.shape[1]), source_rows.dtype)], 0
    )
    return padded[row_table[: ep_count * capacity]].reshape(
        ep_count, capacity, source_rows.shape[1]
    )


def combine(returned, place_list, weights, ep_count, capacity):
    model_width = returned.shape[2]
    flat_rows = jnp.concatenate(
        [
            returned.reshape(ep_count * capacity, model_width),
            jnp.zeros((1, model_width), returned.dtype),
        ],
        0,
    )
    routed_sum = jnp.zeros((weights.shape[0], model_width), jnp.float32)
    for place in place_list:
        picked = flat_rows[place].astype(jnp.float32)
        routed_sum = routed_sum + jnp.einsum("rk,rkd->rd", weights, picked)
    return routed_sum


def per_device(hidden, norm_gain, expert_ids, shares, slot_index, w_gate, w_up, w_down):
    micro_count, row_count, model_width = hidden.shape
    top_count = expert_ids.shape[2]
    ep_count = lax.axis_size("ep")
    share_count = lax.axis_size("tp")
    node_size = FF // SLICE // share_count
    capacity = row_count * top_count // (ep_count // node_size)
    half_width = model_width // share_count
    core_index = lax.axis_index("tp")
    offset = core_index * half_width
    values = hidden.astype(jnp.float32)
    scale = lax.rsqrt(jnp.mean(values * values, axis=-1, keepdims=True) + 1e-06)
    normed = (values * scale * norm_gain.astype(jnp.float32)).astype(jnp.bfloat16)
    places = [
        [
            slot_places(
                expert_ids[micro_batch],
                slot_index[micro_batch],
                node_size,
                capacity,
                ep_count,
                member,
            )
            for member in range(node_size)
        ]
        for micro_batch in range(micro_count)
    ]
    buffers = [
        fill_buffer(normed[micro_batch], places[micro_batch], ep_count, capacity)
        for micro_batch in range(micro_count)
    ]

    def expert_block(received):
        flat_rows = received.reshape(-1, model_width)
        gate_val = jnp.dot(flat_rows, w_gate, preferred_element_type=jnp.float32)
        up_val = jnp.dot(flat_rows, w_up, preferred_element_type=jnp.float32)
        active = (jax.nn.silu(gate_val) * up_val).astype(jnp.bfloat16)
        partial_value = jnp.dot(active, w_down, preferred_element_type=jnp.float32).astype(
            jnp.bfloat16
        )
        partial_value = partial_value.reshape(ep_count, -1, model_width)
        return lax.all_to_all(partial_value, "ep", split_axis=0, concat_axis=0, tiled=True)

    def route_rows(buffer):
        return expert_block(lax.all_to_all(buffer, "ep", split_axis=0, concat_axis=0, tiled=True))

    returned = [route_rows(buffer) for buffer in buffers]
    routed = jnp.stack(
        [
            combine(
                returned[micro_batch], places[micro_batch], shares[micro_batch], ep_count, capacity
            )
            for micro_batch in range(micro_count)
        ]
    )
    residual = lax.dynamic_slice_in_dim(values, offset, half_width, 2)
    summed = lax.psum_scatter(
        routed.astype(jnp.bfloat16), "tp", scatter_dimension=2, tiled=True
    ).astype(jnp.float32)
    return (residual + summed).astype(jnp.bfloat16)


def solution(mesh):
    in_specs = (
        P(None, ("groups", "ep"), None),
        P(),
        P(None, ("groups", "ep"), None),
        P(None, ("groups", "ep"), None),
        P(None, ("groups", "ep"), None),
        P(None, ("ep", "tp")),
        P(None, ("ep", "tp")),
        P(("ep", "tp"), None),
    )
    out_specs = P(None, ("groups", "ep"), "tp")
    return jax.shard_map(
        per_device, mesh=mesh, in_specs=in_specs, out_specs=out_specs, check_vma=False
    )
```

profile of v0, /device:TPU:0, one launch (start us, length us, event | category | flops | bytes accessed | tf_op | source)
XLA Modules:
  0.0 80.4 jit_solution(8202133449257738316)
XLA Ops:
  6.5 1.4 %fusion.25 = (s32[8]{0:T(128)S(1)}, s32[1,8,1]{1,2,0:T(1,128)S(1)}, s32[8]{0:T(128)}, s32[1,8,1]{1,2,0:T(1,128)S(1)}, s32[8]{0:T(128)}, /*index=5*/s32[1,8,1]{1,...) fusion(s32[2,8,1]{1,2,0:T(1,128)} %param.10, ...), kind=kLoop, calls=%fused_computation.84 | loop fusion | flops 464 | bytes 640 | tf_op jit(solution)/shard_map/select_n | solution.py:40
  11.0 0.7 gather_fusion
  11.7 0.7 reshape.941
  12.4 7.3 %all-to-all-start = ((bf16[8,4,3584]{2,1,0:T(4,128)(2,1)}), bf16[8,4,3584]{2,1,0:T(4,128)(2,1)S(1)}, u32[]{:S(2)}, u32[]{:S(2)}) async-start(bf16[8,4,3584]{2,1,0:T(4,128)(2,1)} %reshape.941), calls=%async_computation | async-start | bytes 458752 | tf_op jit(solution)/shard_map/all_to_all | solution.py:89
  22.2 0.7 gather_fusion.5
  22.9 0.7 reshape.946
  24.8 3.3 %all-to-all-done = bf16[8,4,3584]{2,1,0:T(4,128)(2,1)S(1)} async-done(((bf16[8,4,3584]{2,1,0:T(4,128)(2,1)}), bf16[8,4,3584]{2,1,0:T(4,128)(2,1)S(1)}, u32[]{:S(2)}, u32[]{:S(2)}) %all-to-all-start) | async-done | bytes 229408 | tf_op jit(solution)/shard_map/all_to_all | solution.py:89
  28.1 3.4 %all-to-all-start.2 = ((bf16[8,4,3584]{2,1,0:T(4,128)(2,1)}), bf16[8,4,3584]{2,1,0:T(4,128)(2,1)S(1)}, u32[]{:S(2)}, u32[]{:S(2)}) async-start(bf16[8,4,3584]{2,1,0:T(4,128)(2,1)} %reshape.946), calls=%async_computation.2 | async-start | bytes 458752 | tf_op jit(solution)/shard_map/all_to_all | solution.py:89
  31.6 0.9 %fusion.40 = f32[32,128]{1,0:T(8,128)} fusion(bf16[32,3584]{1,0:T(8,128)(2,1)S(1)} %reshape.942, bf16[3584,128]{1,0:T(8,128)(2,1)S(1)} %copy-done.2), kind=kOutput, calls=%fused_computation.113 | convolution fusion | flops 29360128 | bytes 1163264 | tf_op jit(solution)/shard_map/dot_general | solution.py:79
  32.7 1.2 %convolution_convert_fusion.1 = bf16[32,3584]{1,0:T(8,128)(2,1)S(1)} fusion(bf16[128,3584]{1,0:T(8,128)(2,1)S(1)} %copy-done, bf16[32,3584]{1,0:T(8,128)(2,1)S(1)} %reshape.942, bf16[3584,128]{1,0:T(8,128)(2,1)S(1)} %copy-done.1, f32[32,128]{1,0:T(8,128)} %fusion.40), kind=kOutput, calls=%fused_computation.19 | convolution fusion | flops 58859520 | bytes 2310144 | tf_op jit(solution)/shard_map/dot_general | solution.py:82
  33.9 0.8 reshape.943
  34.6 4.9 %all-to-all-done.2 = bf16[8,4,3584]{2,1,0:T(4,128)(2,1)S(1)} async-done(((bf16[8,4,3584]{2,1,0:T(4,128)(2,1)}), bf16[8,4,3584]{2,1,0:T(4,128)(2,1)S(1)}, u32[]{:S(2)}, u32[]{:S(2)}) %all-to-all-start.2) | async-done | bytes 229408 | tf_op jit(solution)/shard_map/all_to_all | solution.py:89
  39.6 3.4 %all-to-all-start.1 = ((bf16[8,4,3584]{2,1,0:T(4,128)(2,1)}), bf16[8,4,3584]{2,1,0:T(4,128)(2,1)S(1)}, u32[]{:S(2)}, u32[]{:S(2)}) async-start(bf16[8,4,3584]{2,1,0:T(4,128)(2,1)} %reshape.943), calls=%async_computation.1 | async-start | bytes 458752 | tf_op jit(solution)/shard_map/all_to_all | solution.py:86
  43.8 0.8 reshape.948
  44.6 6.4 %all-to-all-done.1 = bf16[8,4,3584]{2,1,0:T(4,128)(2,1)S(1)} async-done(((bf16[8,4,3584]{2,1,0:T(4,128)(2,1)}), bf16[8,4,3584]{2,1,0:T(4,128)(2,1)S(1)}, u32[]{:S(2)}, u32[]{:S(2)}) %all-to-all-start.1) | async-done | bytes 229408 | tf_op jit(solution)/shard_map/all_to_all | solution.py:86
  51.0 3.4 %all-to-all-start.3 = ((bf16[8,4,3584]{2,1,0:T(4,128)(2,1)}), bf16[8,4,3584]{2,1,0:T(4,128)(2,1)S(1)}, u32[]{:S(2)}, u32[]{:S(2)}) async-start(bf16[8,4,3584]{2,1,0:T(4,128)(2,1)} %reshape.948), calls=%async_computation.3 | async-start | bytes 458752 | tf_op jit(solution)/shard_map/all_to_all | solution.py:86
  55.8 0.7 copy-done.9
  56.6 0.7 gather_fusion.1
  57.3 0.7 gather_fusion.2
  58.0 0.7 gather_fusion.3
  58.7 0.7 gather_fusion.4
  59.4 3.0 %all-to-all-done.3 = bf16[8,4,3584]{2,1,0:T(4,128)(2,1)S(1)} async-done(((bf16[8,4,3584]{2,1,0:T(4,128)(2,1)}), bf16[8,4,3584]{2,1,0:T(4,128)(2,1)S(1)}, u32[]{:S(2)}, u32[]{:S(2)}) %all-to-all-start.3) | async-done | bytes 229408 | tf_op jit(solution)/shard_map/all_to_all | solution.py:86
  65.7 6.4 %reduce-scatter.2.cloned.1.call-done = bf16[2,8,1792]{2,1,0:T(8,128)(2,1)} async-done(((bf16[2,8,3584]{2,1,0:T(8,128)(2,1)}), bf16[2,8,1792]{2,1,0:T(8,128)(2,1)}) %reduce-scatter.2.cloned.1.call-update) | async-done | bytes 57360 | tf_op jit(solution)/shard_map/reduce_scatter | solution.py:101
  72.2 1.5 %add_convert_fusion = bf16[2,8,1792]{2,1,0:T(8,128)(2,1)} fusion(bf16[2,8,1792]{2,1,0:T(8,128)(2,1)} %reduce-scatter.2.cloned.1.call-done, f32[2,8,3584]{2,1,0:T(8,128)S(1)} %convert_element_type.36, s32[]{:T(128)S(6)} %select_n.370), kind=kLoop, calls=%fused_computation.31 | loop fusion | flops 86016 | bytes 229380 | tf_op jit(solution)/shard_map/convert_element_type | solution.py:104
  (73 shorter events, 12.3 us)
Async XLA Ops:
  6.5 25.9 %copy-start = (bf16[128,3584]{1,0:T(8,128)(2,1)S(1)}, bf16[128,3584]{1,0:T(8,128)(2,1)}, u32[]{:S(2)}) copy-start(bf16[128,3584]{1,0:T(8,128)(2,1)} %param.15) | copy-start | bytes 2752516
  9.8 0.7 copy-start.4
  9.8 0.9 %copy-start.3 = (bf16[2,8,3584]{2,1,0:T(8,128)(2,1)S(1)}, bf16[2,8,3584]{2,1,0:T(8,128)(2,1)}, u32[]{:S(2)}) copy-start(bf16[2,8,3584]{2,1,0:T(8,128)(2,1)} %param.8) | copy-start | bytes 344068
  12.4 15.7 %all-to-all-start = ((bf16[8,4,3584]{2,1,0:T(4,128)(2,1)}), bf16[8,4,3584]{2,1,0:T(4,128)(2,1)S(1)}, u32[]{:S(2)}, u32[]{:S(2)}) async-start(bf16[8,4,3584]{2,1,0:T(4,128)(2,1)} %reshape.941), calls=%async_computation | async-start | bytes 458752 | tf_op jit(solution)/shard_map/all_to_all | solution.py:89
  22.9 8.7 %copy-start.2 = (bf16[3584,128]{1,0:T(8,128)(2,1)S(1)}, bf16[3584,128]{1,0:T(8,128)(2,1)}, u32[]{:S(2)}) copy-start(bf16[3584,128]{1,0:T(8,128)(2,1)} %param.13) | copy-start | bytes 2752516
  28.1 11.5 %all-to-all-start.2 = ((bf16[8,4,3584]{2,1,0:T(4,128)(2,1)}), bf16[8,4,3584]{2,1,0:T(4,128)(2,1)S(1)}, u32[]{:S(2)}, u32[]{:S(2)}) async-start(bf16[8,4,3584]{2,1,0:T(4,128)(2,1)} %reshape.946), calls=%async_computation.2 | async-start | bytes 458752 | tf_op jit(solution)/shard_map/all_to_all | solution.py:89
  31.5 1.2 %copy-start.1 = (bf16[3584,128]{1,0:T(8,128)(2,1)S(1)}, bf16[3584,128]{1,0:T(8,128)(2,1)}, u32[]{:S(2)}) copy-start(bf16[3584,128]{1,0:T(8,128)(2,1)} %param.14) | copy-start | bytes 2752516
  39.6 11.4 %all-to-all-start.1 = ((bf16[8,4,3584]{2,1,0:T(4,128)(2,1)}), bf16[8,4,3584]{2,1,0:T(4,128)(2,1)S(1)}, u32[]{:S(2)}, u32[]{:S(2)}) async-start(bf16[8,4,3584]{2,1,0:T(4,128)(2,1)} %reshape.943), calls=%async_computation.1 | async-start | bytes 458752 | tf_op jit(solution)/shard_map/all_to_all | solution.py:86
  51.0 11.4 %all-to-all-start.3 = ((bf16[8,4,3584]{2,1,0:T(4,128)(2,1)}), bf16[8,4,3584]{2,1,0:T(4,128)(2,1)S(1)}, u32[]{:S(2)}, u32[]{:S(2)}) async-start(bf16[8,4,3584]{2,1,0:T(4,128)(2,1)} %reshape.948), calls=%async_computation.3 | async-start | bytes 458752 | tf_op jit(solution)/shard_map/all_to_all | solution.py:86
  54.4 17.7 %reduce-scatter.2.cloned.1.call-start = ((), (), s32[]{:S(2)}) async-start(), calls=%async_computation.5 | async-start | bytes 172032 | tf_op jit(solution)/shard_map/reduce_scatter | solution.py:101
  54.5 0.6 copy-start.7
  54.5 0.7 copy-start.8
  55.1 0.6 copy-start.5
  55.1 0.6 copy-start.6
  55.8 0.7 copy-start.9
Sparse Core Ops, SparseCore 0:
  65.8 6.2 reduce-scatter.1
where the time goes:
time: 81.2 us; the launch traced here: 80.4 us
  waiting for transfers between devices  24.1 us (30%)
  starting transfers between devices  17.5 us (22%)
  local copies, waits for them, and re-layouts  17.1 us (21%)
  between operations  13.8 us (17%)
  other arithmetic  5.13 us (6%)
  matrix products  2.8 us (3%)
    all_to_all x2, starting transfers between devices, route_rows(): lax.all_to_all(buffer, 'ep', split_axis=0, concat_axis=0, tiled=True)  10.7 us
    all_to_all x2, waiting for transfers between devices, expert_block(): lax.all_to_all(partial_value, 'ep', split_axis=0, concat_axis=0, tiled=True)  9.44 us
    all_to_all x2, waiting for transfers between devices, route_rows(): lax.all_to_all(buffer, 'ep', split_axis=0, concat_axis=0, tiled=True)  8.22 us
    all_to_all x2, starting transfers between devices, expert_block(): lax.all_to_all(partial_value, 'ep', split_axis=0, concat_axis=0, tiled=True)  6.8 us
    reduce_scatter x1, waiting for transfers between devices, per_device(): lax.psum_scatter(routed.astype(jnp.bfloat16), 'tp', scatter_dimension=2,...  6.41 us
    gather x8, local copies, waits for them, and re-layouts, combine(): picked = flat_rows[place].astype(jnp.float32)  5.18 us
    scatter x8, local copies, waits for them, and re-layouts, fill_buffer(): row_table = row_table.at[place.reshape(-1)].set(row_ids.reshape(-1))  4.78 us
    unnamed x20, local copies, waits for them, and re-layouts  2.47 us
  transfers between devices with their start and end apart: 5, of which 5 were waited for; matrix products, arithmetic and copies ran while one was open for 15% of the time, Pallas kernels for 0%

commit v1 on v0

v1 whole, which is shorter than its diff:
```python
import functools

import jax
import jax.numpy as jnp
from jax import lax
from jax.experimental import pallas as pl
from jax.experimental.pallas import tpu as pltpu
from jax.sharding import PartitionSpec as P

FF = 1024
SLICE = 128


def hits(ids, placed, node, nodes, first, slots, micro_batch, capacity):
    per_node = slots[1]
    row_count = ids.shape[1]
    slot = lax.broadcasted_iota(jnp.int32, (slots[0] * per_node, row_count), 0) + first * per_node
    offset = ids - node
    offset = jnp.where(offset < 0, offset + nodes, offset)
    place = offset * per_node + micro_batch * capacity + placed
    place = jnp.where(placed >= 0, place, -1)
    return [slot == place[k : k + 1, :] for k in range(ids.shape[0])]


def dispatch_kernel(sizes, hidden_ref, gain_ref, ids_ref, placed_ref, own_ref, rest_ref):
    nodes, node_size, capacity, half, cut = sizes
    micro_count = hidden_ref.shape[0]
    per_node = micro_count * capacity
    node = lax.axis_index("ep") // node_size
    gain = gain_ref[...].astype(jnp.float32)
    own = rest = 0.0
    for m in range(micro_count):
        values = hidden_ref[m].astype(jnp.float32)
        scale = lax.rsqrt(jnp.mean(values * values, axis=-1, keepdims=True) + 1e-06)
        normed = (values * scale * gain).astype(jnp.bfloat16)

        def select(first, count):
            chosen = hits(
                ids_ref[m], placed_ref[m], node, nodes, first, (count, per_node), m, capacity
            )
            flags = functools.reduce(jnp.logical_or, chosen)
            return jnp.dot(
                jnp.where(flags, 1.0, 0.0).astype(jnp.bfloat16),
                normed,
                preferred_element_type=jnp.float32,
            )

        own = own + select(0, 1)
        rest = rest + select(1, nodes - 1)
    own_ref[...] = own.astype(jnp.bfloat16)
    rest_ref[...] = rest.astype(jnp.bfloat16)


def expert_kernel(sizes, *refs):
    node_size, half = sizes
    pieces = refs[: 2 * node_size]
    gate_ref, up_ref, down_ref, keep_ref, send_ref = refs[2 * node_size :]
    core = lax.axis_index("tp")
    rows = jnp.concatenate([ref[...].astype(jnp.float32) for ref in pieces], 0).astype(jnp.bfloat16)
    gate_val = jnp.dot(rows, gate_ref[...], preferred_element_type=jnp.float32)
    up_val = jnp.dot(rows, up_ref[...], preferred_element_type=jnp.float32)
    active = (gate_val / (1.0 + jnp.exp(-gate_val)) * up_val).astype(jnp.bfloat16)

    def down(which):
        columns = pl.ds(pl.multiple_of(which * half, 128), half)
        return jnp.dot(active, down_ref[:, columns], preferred_element_type=jnp.float32)

    send_ref[...] = down(1 - core).astype(jnp.bfloat16).reshape(send_ref.shape)
    keep_ref[...] = down(core).reshape(keep_ref.shape)


def add_cores_kernel(sizes, keep_ref, got_ref, *out_refs):
    node_size, per_node = sizes
    for k in range(node_size):
        total = keep_ref[k] + got_ref[k].astype(jnp.float32)
        own_ref, rest_ref = out_refs[2 * k : 2 * k + 2]
        own_ref[...] = total[:per_node].astype(own_ref.dtype)
        rest_ref[...] = total[per_node:].astype(rest_ref.dtype)


def add_members_kernel(*refs):
    total = refs[0][...]
    for ref in refs[1:-1]:
        total = total + ref[...].astype(jnp.float32)
    refs[-1][...] = total.astype(jnp.bfloat16)


def combine_kernel(sizes, hidden_ref, ids_ref, placed_ref, shares_ref, *refs):
    nodes, node_size, capacity, half = sizes
    own_refs, rest_ref, out_ref = refs[:node_size], refs[node_size], refs[node_size + 1]
    micro_count = hidden_ref.shape[0]
    per_node = micro_count * capacity
    node = lax.axis_index("ep") // node_size
    core = lax.axis_index("tp")
    own = own_refs[0][...]
    for ref in own_refs[1:]:
        own = own + ref[...].astype(jnp.float32)
    rest = rest_ref[...].astype(jnp.float32)
    columns = pl.ds(pl.multiple_of(core * half, 128), half)
    for m in range(micro_count):
        total = hidden_ref[m, :, columns].astype(jnp.float32)
        for first, count, block in ((0, 1, own), (1, nodes - 1, rest)):
            chosen = hits(
                ids_ref[m], placed_ref[m], node, nodes, first, (count, per_node), m, capacity
            )
            weights = sum(
                jnp.where(flags, shares_ref[m][k : k + 1, :], 0.0) for k, flags in enumerate(chosen)
            )
            total = total + lax.dot_general(
                weights,
                block,
                (((0,), (0,)), ((), ())),
                precision=lax.Precision.HIGHEST,
                preferred_element_type=jnp.float32,
            )
        out_ref[m] = total.astype(jnp.bfloat16)


def per_device(hidden, norm_gain, expert_ids, shares, slot_index, w_gate, w_up, w_down):
    micro_count, row_count, model_width = hidden.shape
    ep_count = lax.axis_size("ep")
    share_count = lax.axis_size("tp")
    node_size = FF // SLICE // share_count
    nodes = ep_count // node_size
    capacity = row_count * expert_ids.shape[2] // nodes
    half = model_width // share_count
    per_node = micro_count * capacity
    rest_rows = (nodes - 1) * per_node
    ids, placed, weights = (jnp.swapaxes(a, 1, 2) for a in (expert_ids, slot_index, shares))
    params = pltpu.CompilerParams(
        vmem_limit_bytes=(16 if nodes * per_node <= 32 else 56) * 1024 * 1024
    )
    bf16, f32 = jnp.bfloat16, jnp.float32

    def call(kernel, outs, *args):
        return pl.pallas_call(
            kernel,
            out_shape=[jax.ShapeDtypeStruct(shape, kind) for shape, kind in outs],
            compiler_params=params,
        )(*args)

    def to_member(array, k):
        pairs = [(j, j // node_size * node_size + (j % node_size ^ k)) for j in range(ep_count)]
        return lax.ppermute(array, "ep", pairs)

    def to_nodes(array, sign):
        blocks = []
        for n in range(1, nodes):
            block = array if nodes == 2 else array[(n - 1) * per_node : n * per_node]
            pairs = [(j, (j + sign * n * node_size) % ep_count) for j in range(ep_count)]
            blocks.append(lax.ppermute(block, "ep", pairs))
        return blocks[0] if nodes == 2 else jnp.concatenate(blocks, 0)

    own, rest = call(
        functools.partial(dispatch_kernel, (nodes, node_size, capacity, half, False)),
        [((per_node, model_width), bf16), ((rest_rows, model_width), bf16)],
        hidden,
        norm_gain[None],
        ids,
        placed,
    )
    inbox = to_nodes(rest, 1)
    owns = [own] + [to_member(own, k) for k in range(1, node_size)]
    rests = [inbox] + [to_member(inbox, k) for k in range(1, node_size)]
    pieces = [piece for pair in zip(owns, rests) for piece in pair]
    blocks = (node_size, nodes * per_node, half)
    keep, send = call(
        functools.partial(expert_kernel, (node_size, half)),
        [(blocks, f32), (blocks, bf16)],
        *pieces,
        w_gate,
        w_up,
        w_down,
    )
    got = lax.ppermute(send, "tp", [(i, (i + 1) % share_count) for i in range(share_count)])
    sums = call(
        functools.partial(add_cores_kernel, (node_size, per_node)),
        [
            ((count, half), kind)
            for kind in [f32] + [bf16] * (node_size - 1)
            for count in (per_node, rest_rows)
        ],
        keep,
        got,
    )
    away = [sums[1]] + [to_member(sums[2 * k + 1], k) for k in range(1, node_size)]
    home = [sums[0]] + [to_member(sums[2 * k], k) for k in range(1, node_size)]
    (outbox,) = call(add_members_kernel, [((rest_rows, half), bf16)], *away)
    returned = to_nodes(outbox, -1)
    (mixed,) = call(
        functools.partial(combine_kernel, (nodes, node_size, capacity, half)),
        [((micro_count, row_count, half), bf16)],
        hidden,
        ids,
        placed,
        weights,
        *home,
        returned,
    )
    return mixed


def solution(mesh):
    in_specs = (
        P(None, ("groups", "ep"), None),
        P(),
        P(None, ("groups", "ep"), None),
        P(None, ("groups", "ep"), None),
        P(None, ("groups", "ep"), None),
        P(None, ("ep", "tp")),
        P(None, ("ep", "tp")),
        P(("ep", "tp"), None),
    )
    out_specs = P(None, ("groups", "ep"), "tp")
    return jax.shard_map(
        per_device, mesh=mesh, in_specs=in_specs, out_specs=out_specs, check_vma=False
    )
```

time: 81.2 us -> 37.6 us (0.46)
  waiting for transfers between devices: 24.1 us -> 8.13 us
  between operations: 13.8 us -> 0.07 us
  local copies, waits for them, and re-layouts: 17.1 us -> 6.5 us
  other arithmetic: 5.13 us -> 0 us
  starting transfers between devices: 17.5 us -> 20.3 us
  matrix products: 2.8 us -> 0 us
  Pallas kernels: 0 us -> 2.26 us
    ppermute x0 -> x15, starting transfers between devices: none -> 20.3 us  [the longest x12 14.1 us: to_member(): return lax.ppermute(array, 'ep', pairs)]
    all_to_all x4 -> x0, waiting for transfers between devices: 17.7 us -> none  [the longest x2 9.44 us: expert_block(): lax.all_to_all(partial_value, 'ep', split_axis=0, concat_axis=0, tiled=True)]
    all_to_all x4 -> x0, starting transfers between devices: 17.5 us -> none  [the longest x2 10.7 us: route_rows(): lax.all_to_all(buffer, 'ep', split_axis=0, concat_axis=0, tiled=True)]
    ppermute x0 -> x15, waiting for transfers between devices: none -> 8.13 us  [the longest x12 4.96 us: to_member(): return lax.ppermute(array, 'ep', pairs)]
    gather x10 -> x0, local copies, waits for them, and re-layouts: 6.55 us -> none  [the longest x8 5.18 us: combine(): picked = flat_rows[place].astype(jnp.float32)]
    reduce_scatter x1 -> x0, waiting for transfers between devices: 6.41 us -> none  [per_device(): lax.psum_scatter(routed.astype(jnp.bfloat16), 'tp', scatter_dimension=2,...]
    scatter x8 -> x0, local copies, waits for them, and re-layouts: 4.78 us -> none  [fill_buffer(): row_table = row_table.at[place.reshape(-1)].set(row_ids.reshape(-1))]
    unnamed x20 -> x16, local copies, waits for them, and re-layouts: 2.47 us -> 5.8 us
  transfers between devices with their start and end apart: 5 -> 15, of which waited for: 5 -> 8; matrix products, arithmetic and copies ran while one was open for 15% -> 0% of each run, Pallas kernels for 0% -> 0%
where the time goes in v1:
time: 37.6 us; the launch traced here: 37.3 us
  starting transfers between devices  20.3 us (54%)
  waiting for transfers between devices  8.13 us (22%)
  local copies, waits for them, and re-layouts  6.5 us (17%)
  Pallas kernels  2.26 us (6%)
    ppermute x12, starting transfers between devices, to_member(): return lax.ppermute(array, 'ep', pairs)  14.1 us
    ppermute x2, starting transfers between devices, to_nodes(): blocks.append(lax.ppermute(block, 'ep', pairs))  6.14 us
    unnamed x16, local copies, waits for them, and re-layouts  5.8 us
    ppermute x12, waiting for transfers between devices, to_member(): return lax.ppermute(array, 'ep', pairs)  4.96 us
    pallas_call x5, Pallas kernels, call(): pl.pallas_call(kernel, out_shape=[jax.ShapeDtypeStruct(shape, kind) for s...  2.26 us
    ppermute x2, waiting for transfers between devices, to_nodes(): blocks.append(lax.ppermute(block, 'ep', pairs))  1.7 us
    ppermute x1, waiting for transfers between devices, per_device(): lax.ppermute(send, 'tp', [(i, (i + 1) % share_count) for i in range(share...  1.48 us
  transfers between devices with their start and end apart: 15, of which 8 were waited for; matrix products, arithmetic and copies ran while one was open for 0% of the time, Pallas kernels for 0%

profile of v1, /device:TPU:0, one launch (start us, length us, event | category | flops | bytes accessed | tf_op | source)
XLA Modules:
  0.0 37.3 jit_solution(7927843070390331592)
XLA Ops:
  0.0 0.7 %broadcast_in_dim.3.gain_ref = bf16[1,3584]{1,0:T(2,128)(2,1)S(1)} reshape(bf16[3584]{0:T(1024)(128)(2,1)} %param.9) | data formatting | bytes 14336 | tf_op jit(solution)/shard_map/broadcast_in_dim | solution.py:158
  0.7 0.7 %copy-done.6 = s32[2,8,1]{1,2,0:T(1,128)S(1)} copy-done((s32[2,8,1]{1,2,0:T(1,128)S(1)}, s32[2,8,1]{1,2,0:T(1,128)}, u32[]{:S(2)}) %copy-start.6) | copy-done | bytes 88
  1.4 0.9 %copy-done.3 = bf16[2,8,3584]{2,1,0:T(8,128)(2,1)S(1)} copy-done((bf16[2,8,3584]{2,1,0:T(8,128)(2,1)S(1)}, bf16[2,8,3584]{2,1,0:T(8,128)(2,1)}, u32[]{:S(2)}) %copy-start.3) | copy-done | bytes 114712
  2.7 4.1 %collective-permute-start = (bf16[8,3584]{1,0:T(8,128)(2,1)S(1)}, bf16[8,3584]{1,0:T(8,128)(2,1)S(1)}, u32[]{:S(2)}, u32[]{:S(2)}) collective-permute-start(bf16[8,3584]{1,0:T(8,128)(2,1)S(1)} %get-tuple-element.18), channel_id=1, source_target_pairs={{0,8},{2,10},{4,12},{6,14},{8,0},{10,2},{12,4},{14,6},{1,9},{3,11}... | collective-permute-start | bytes 172040 | tf_op jit(solution)/shard_map/ppermute | solution.py:151
  6.8 2.5 %collective-permute-start.5 = (bf16[8,3584]{1,0:T(8,128)(2,1)S(1)}, bf16[8,3584]{1,0:T(8,128)(2,1)S(1)}, u32[]{:S(2)}, u32[]{:S(2)}) collective-permute-start(bf16[8,3584]{1,0:T(8,128)(2,1)S(1)} %get-tuple-element.17.refs_0_), channel_id=1, source_target_pairs={{0,6},{2,4},{4,2},{6,0},{8,14},{10,12},{12,10},{14,8},{1,7},{3,5},... | collective-permute-start | bytes 172040 | tf_op jit(solution)/shard_map/ppermute | solution.py:144
  10.3 2.5 %collective-permute-start.6 = (bf16[8,3584]{1,0:T(8,128)(2,1)S(1)}, bf16[8,3584]{1,0:T(8,128)(2,1)S(1)}, u32[]{:S(2)}, u32[]{:S(2)}) collective-permute-start(bf16[8,3584]{1,0:T(8,128)(2,1)S(1)} %collective-permute-done.refs_1_), channel_id=1, source_target_pairs={{0,6},{2,4},{4,2},{6,0},{8,14},{10,12},{12,10},{14,8},{1,7},{3,5},... | collective-permute-start | bytes 172040 | tf_op jit(solution)/shard_map/ppermute | solution.py:144
  13.9 1.4 %collective-permute-done.6.refs_7_ = bf16[8,3584]{1,0:T(8,128)(2,1)S(1)} collective-permute-done((bf16[8,3584]{1,0:T(8,128)(2,1)S(1)}, bf16[8,3584]{1,0:T(8,128)(2,1)S(1)}, u32[]{:S(2)}, u32[]{:S(2)}) %collective-permute-start.6) | collective-permute-done | bytes 57376 | tf_op jit(solution)/shard_map/ppermute | solution.py:144
  15.3 1.6 %collective-permute-done.4.refs_5_ = bf16[8,3584]{1,0:T(8,128)(2,1)S(1)} collective-permute-done((bf16[8,3584]{1,0:T(8,128)(2,1)S(1)}, bf16[8,3584]{1,0:T(8,128)(2,1)S(1)}, u32[]{:S(2)}, u32[]{:S(2)}) %collective-permute-start.4) | collective-permute-done | bytes 57376 | tf_op jit(solution)/shard_map/ppermute | solution.py:144
  17.4 1.2 %copy-done = bf16[3584,128]{1,0:T(8,128)(2,1)S(1)} copy-done((bf16[3584,128]{1,0:T(8,128)(2,1)S(1)}, bf16[3584,128]{1,0:T(8,128)(2,1)}, u32[]{:S(2)}) %copy-start) | copy-done | bytes 917528
  18.6 1.2 %copy-done.1 = bf16[3584,128]{1,0:T(8,128)(2,1)S(1)} copy-done((bf16[3584,128]{1,0:T(8,128)(2,1)S(1)}, bf16[3584,128]{1,0:T(8,128)(2,1)}, u32[]{:S(2)}) %copy-start.1) | copy-done | bytes 917528
  19.8 1.2 %copy-done.2 = bf16[128,3584]{1,0:T(8,128)(2,1)S(1)} copy-done((bf16[128,3584]{1,0:T(8,128)(2,1)S(1)}, bf16[128,3584]{1,0:T(8,128)(2,1)}, u32[]{:S(2)}) %copy-start.2) | copy-done | bytes 917528
  20.9 0.7 %shard_map.83 = (f32[4,16,1792]{2,1,0:T(8,128)S(1)}, bf16[4,16,1792]{2,1,0:T(8,128)(2,1)S(1)}) custom-call(bf16[8,3584]{1,0:T(8,128)(2,1)S(1)} %get-tuple-element.17.refs_0_, bf16[8,3584]{1,0:T(8,128)(2,1)S(1)} %collective-permute-done.refs_1_, bf16[8,3584]{1,0:T(8,128)(2,1)S(1)} %collective-permute-done.1.refs_2_, ...), custom_call_target="tpu_custom_call" | custom-call | tf_op jit(solution)/shard_map/pallas_call | solution.py:136
  21.7 1.5 %collective-permute-done.7.got_ref = bf16[4,16,1792]{2,1,0:T(8,128)(2,1)S(1)} collective-permute-done((bf16[4,16,1792]{2,1,0:T(8,128)(2,1)S(1)}, bf16[4,16,1792]{2,1,0:T(8,128)(2,1)S(1)}, u32[]{:S(2)}, u32[]{:S(2)}) %collective-permute-start.7) | collective-permute-done | bytes 229408 | tf_op jit(solution)/shard_map/ppermute | solution.py:175
  23.2 0.7 %collective-permute-start.11 = (bf16[8,1792]{1,0:T(8,128)(2,1)S(1)}, bf16[8,1792]{1,0:T(8,128)(2,1)S(1)}, u32[]{:S(2)}, u32[]{:S(2)}) collective-permute-start(bf16[8,1792]{1,0:T(8,128)(2,1)S(1)} %get-tuple-element.26), channel_id=1, source_target_pairs={{0,2},{2,0},{4,6},{6,4},{8,10},{10,8},{12,14},{14,12},{1,3},{3,1},... | collective-permute-start | bytes 86024 | tf_op jit(solution)/shard_map/ppermute | solution.py:144
  23.9 1.5 %collective-permute-start.12 = (bf16[8,1792]{1,0:T(8,128)(2,1)S(1)}, bf16[8,1792]{1,0:T(8,128)(2,1)S(1)}, u32[]{:S(2)}, u32[]{:S(2)}) collective-permute-start(bf16[8,1792]{1,0:T(8,128)(2,1)S(1)} %get-tuple-element.27), channel_id=1, source_target_pairs={{0,4},{2,6},{4,0},{6,2},{8,12},{10,14},{12,8},{14,10},{1,5},{3,7},... | collective-permute-start | bytes 86024 | tf_op jit(solution)/shard_map/ppermute | solution.py:144
  25.4 1.4 %collective-permute-start.13 = (bf16[8,1792]{1,0:T(8,128)(2,1)S(1)}, bf16[8,1792]{1,0:T(8,128)(2,1)S(1)}, u32[]{:S(2)}, u32[]{:S(2)}) collective-permute-start(bf16[8,1792]{1,0:T(8,128)(2,1)S(1)} %get-tuple-element.28), channel_id=1, source_target_pairs={{0,6},{2,4},{4,2},{6,0},{8,14},{10,12},{12,10},{14,8},{1,7},{3,5},... | collective-permute-start | bytes 86024 | tf_op jit(solution)/shard_map/ppermute | solution.py:144
  26.8 0.6 %collective-permute-start.8 = (bf16[8,1792]{1,0:T(8,128)(2,1)S(1)}, bf16[8,1792]{1,0:T(8,128)(2,1)S(1)}, u32[]{:S(2)}, u32[]{:S(2)}) collective-permute-start(bf16[8,1792]{1,0:T(8,128)(2,1)S(1)} %get-tuple-element.22), channel_id=1, source_target_pairs={{0,2},{2,0},{4,6},{6,4},{8,10},{10,8},{12,14},{14,12},{1,3},{3,1},... | collective-permute-start | bytes 86024 | tf_op jit(solution)/shard_map/ppermute | solution.py:144
  27.4 1.5 %collective-permute-start.9 = (bf16[8,1792]{1,0:T(8,128)(2,1)S(1)}, bf16[8,1792]{1,0:T(8,128)(2,1)S(1)}, u32[]{:S(2)}, u32[]{:S(2)}) collective-permute-start(bf16[8,1792]{1,0:T(8,128)(2,1)S(1)} %get-tuple-element.23), channel_id=1, source_target_pairs={{0,4},{2,6},{4,0},{6,2},{8,12},{10,14},{12,8},{14,10},{1,5},{3,7},... | collective-permute-start | bytes 86024 | tf_op jit(solution)/shard_map/ppermute | solution.py:144
  28.9 1.4 %collective-permute-start.10 = (bf16[8,1792]{1,0:T(8,128)(2,1)S(1)}, bf16[8,1792]{1,0:T(8,128)(2,1)S(1)}, u32[]{:S(2)}, u32[]{:S(2)}) collective-permute-start(bf16[8,1792]{1,0:T(8,128)(2,1)S(1)} %get-tuple-element.24), channel_id=1, source_target_pairs={{0,6},{2,4},{4,2},{6,0},{8,14},{10,12},{12,10},{14,8},{1,7},{3,5},... | collective-permute-start | bytes 86024 | tf_op jit(solution)/shard_map/ppermute | solution.py:144
  30.6 2.0 %collective-permute-start.14 = (bf16[8,1792]{1,0:T(8,128)(2,1)S(1)}, bf16[8,1792]{1,0:T(8,128)(2,1)S(1)}, u32[]{:S(2)}, u32[]{:S(2)}) collective-permute-start(bf16[8,1792]{1,0:T(8,128)(2,1)S(1)} %shard_map.85), channel_id=1, source_target_pairs={{0,8},{2,10},{4,12},{6,14},{8,0},{10,2},{12,4},{14,6},{1,9},{3,11}... | collective-permute-start | bytes 86024 | tf_op jit(solution)/shard_map/ppermute | solution.py:151
  32.6 1.1 %collective-permute-done.10.refs_3_ = bf16[8,1792]{1,0:T(8,128)(2,1)S(1)} collective-permute-done((bf16[8,1792]{1,0:T(8,128)(2,1)S(1)}, bf16[8,1792]{1,0:T(8,128)(2,1)S(1)}, u32[]{:S(2)}, u32[]{:S(2)}) %collective-permute-start.10) | collective-permute-done | bytes 28704 | tf_op jit(solution)/shard_map/ppermute | solution.py:144
  33.7 1.7 %collective-permute-done.14.refs_4_ = bf16[8,1792]{1,0:T(8,128)(2,1)S(1)} collective-permute-done((bf16[8,1792]{1,0:T(8,128)(2,1)S(1)}, bf16[8,1792]{1,0:T(8,128)(2,1)S(1)}, u32[]{:S(2)}, u32[]{:S(2)}) %collective-permute-start.14) | collective-permute-done | bytes 28704 | tf_op jit(solution)/shard_map/ppermute | solution.py:151
  35.4 0.7 %copy-done.7 = f32[2,8,1]{1,2,0:T(1,128)S(1)} copy-done((f32[2,8,1]{1,2,0:T(1,128)S(1)}, f32[2,8,1]{1,2,0:T(1,128)}, u32[]{:S(2)}) %copy-start.7) | copy-done | bytes 88
  36.1 1.2 %shard_map.86 = bf16[2,8,1792]{2,1,0:T(8,128)(2,1)} custom-call(bf16[2,8,3584]{2,1,0:T(8,128)(2,1)S(1)} %copy-done.4, s32[2,1,8]{2,1,0:T(1,128)S(1)} %bitcast.10, s32[2,1,8]{2,1,0:T(1,128)S(1)} %bitcast.12, f32[2,1,8]{2,1,0:T(1,128)S(1)} %bitcast.13, f32[8,1792]{1,0:T(8,128)S(1)} %get-tuple-element.21.refs_0_, ...), custom_call_target="tpu_custom_call" | custom-call | tf_op jit(solution)/shard_map/pallas_call | solution.py:136
  (28 shorter events, 3.4 us)
Async XLA Ops:
  0.7 0.7 %copy-start.6 = (s32[2,8,1]{1,2,0:T(1,128)S(1)}, s32[2,8,1]{1,2,0:T(1,128)}, u32[]{:S(2)}) copy-start(s32[2,8,1]{1,2,0:T(1,128)} %param.12) | copy-start | bytes 196
  0.7 0.7 %copy-start.5 = (s32[2,8,1]{1,2,0:T(1,128)S(1)}, s32[2,8,1]{1,2,0:T(1,128)}, u32[]{:S(2)}) copy-start(s32[2,8,1]{1,2,0:T(1,128)} %param.10) | copy-start | bytes 196
  1.4 0.9 %copy-start.3 = (bf16[2,8,3584]{2,1,0:T(8,128)(2,1)S(1)}, bf16[2,8,3584]{2,1,0:T(8,128)(2,1)}, u32[]{:S(2)}) copy-start(bf16[2,8,3584]{2,1,0:T(8,128)(2,1)} %hidden_ref.3) | copy-start | bytes 344068
  2.7 7.6 %collective-permute-start = (bf16[8,3584]{1,0:T(8,128)(2,1)S(1)}, bf16[8,3584]{1,0:T(8,128)(2,1)S(1)}, u32[]{:S(2)}, u32[]{:S(2)}) collective-permute-start(bf16[8,3584]{1,0:T(8,128)(2,1)S(1)} %get-tuple-element.18), channel_id=1, source_target_pairs={{0,8},{2,10},{4,12},{6,14},{8,0},{10,2},{12,4},{14,6},{1,9},{3,11}... | collective-permute-start | bytes 172040 | tf_op jit(solution)/shard_map/ppermute | solution.py:151
  6.8 6.5 %collective-permute-start.5 = (bf16[8,3584]{1,0:T(8,128)(2,1)S(1)}, bf16[8,3584]{1,0:T(8,128)(2,1)S(1)}, u32[]{:S(2)}, u32[]{:S(2)}) collective-permute-start(bf16[8,3584]{1,0:T(8,128)(2,1)S(1)} %get-tuple-element.17.refs_0_), channel_id=1, source_target_pairs={{0,6},{2,4},{4,2},{6,0},{8,14},{10,12},{12,10},{14,8},{1,7},{3,5},... | collective-permute-start | bytes 172040 | tf_op jit(solution)/shard_map/ppermute | solution.py:144
  9.3 4.6 %collective-permute-start.3 = (bf16[8,3584]{1,0:T(8,128)(2,1)S(1)}, bf16[8,3584]{1,0:T(8,128)(2,1)S(1)}, u32[]{:S(2)}, u32[]{:S(2)}) collective-permute-start(bf16[8,3584]{1,0:T(8,128)(2,1)S(1)} %get-tuple-element.17.refs_0_), channel_id=1, source_target_pairs={{0,4},{2,6},{4,0},{6,2},{8,12},{10,14},{12,8},{14,10},{1,5},{3,7},... | collective-permute-start | bytes 172040 | tf_op jit(solution)/shard_map/ppermute | solution.py:144
  9.7 4.2 %collective-permute-start.1 = (bf16[8,3584]{1,0:T(8,128)(2,1)S(1)}, bf16[8,3584]{1,0:T(8,128)(2,1)S(1)}, u32[]{:S(2)}, u32[]{:S(2)}) collective-permute-start(bf16[8,3584]{1,0:T(8,128)(2,1)S(1)} %get-tuple-element.17.refs_0_), channel_id=1, source_target_pairs={{0,2},{2,0},{4,6},{6,4},{8,10},{10,8},{12,14},{14,12},{1,3},{3,1},... | collective-permute-start | bytes 172040 | tf_op jit(solution)/shard_map/ppermute | solution.py:144
  10.3 5.1 %collective-permute-start.6 = (bf16[8,3584]{1,0:T(8,128)(2,1)S(1)}, bf16[8,3584]{1,0:T(8,128)(2,1)S(1)}, u32[]{:S(2)}, u32[]{:S(2)}) collective-permute-start(bf16[8,3584]{1,0:T(8,128)(2,1)S(1)} %collective-permute-done.refs_1_), channel_id=1, source_target_pairs={{0,6},{2,4},{4,2},{6,0},{8,14},{10,12},{12,10},{14,8},{1,7},{3,5},... | collective-permute-start | bytes 172040 | tf_op jit(solution)/shard_map/ppermute | solution.py:144
  12.8 4.2 %collective-permute-start.4 = (bf16[8,3584]{1,0:T(8,128)(2,1)S(1)}, bf16[8,3584]{1,0:T(8,128)(2,1)S(1)}, u32[]{:S(2)}, u32[]{:S(2)}) collective-permute-start(bf16[8,3584]{1,0:T(8,128)(2,1)S(1)} %collective-permute-done.refs_1_), channel_id=1, source_target_pairs={{0,4},{2,6},{4,0},{6,2},{8,12},{10,14},{12,8},{14,10},{1,5},{3,7},... | collective-permute-start | bytes 172040 | tf_op jit(solution)/shard_map/ppermute | solution.py:144
  13.2 4.2 %collective-permute-start.2 = (bf16[8,3584]{1,0:T(8,128)(2,1)S(1)}, bf16[8,3584]{1,0:T(8,128)(2,1)S(1)}, u32[]{:S(2)}, u32[]{:S(2)}) collective-permute-start(bf16[8,3584]{1,0:T(8,128)(2,1)S(1)} %collective-permute-done.refs_1_), channel_id=1, source_target_pairs={{0,2},{2,0},{4,6},{6,4},{8,10},{10,8},{12,14},{14,12},{1,3},{3,1},... | collective-permute-start | bytes 172040 | tf_op jit(solution)/shard_map/ppermute | solution.py:144
  17.4 1.2 %copy-start = (bf16[3584,128]{1,0:T(8,128)(2,1)S(1)}, bf16[3584,128]{1,0:T(8,128)(2,1)}, u32[]{:S(2)}) copy-start(bf16[3584,128]{1,0:T(8,128)(2,1)} %refs_8_.1) | copy-start | bytes 2752516
  18.6 1.2 %copy-start.1 = (bf16[3584,128]{1,0:T(8,128)(2,1)S(1)}, bf16[3584,128]{1,0:T(8,128)(2,1)}, u32[]{:S(2)}) copy-start(bf16[3584,128]{1,0:T(8,128)(2,1)} %refs_9_.1) | copy-start | bytes 2752516
  19.8 1.2 %copy-start.2 = (bf16[128,3584]{1,0:T(8,128)(2,1)S(1)}, bf16[128,3584]{1,0:T(8,128)(2,1)}, u32[]{:S(2)}) copy-start(bf16[128,3584]{1,0:T(8,128)(2,1)} %refs_10_.1) | copy-start | bytes 2752516
  21.6 1.6 %collective-permute-start.7 = (bf16[4,16,1792]{2,1,0:T(8,128)(2,1)S(1)}, bf16[4,16,1792]{2,1,0:T(8,128)(2,1)S(1)}, u32[]{:S(2)}, u32[]{:S(2)}) collective-permute-start(bf16[4,16,1792]{2,1,0:T(8,128)(2,1)S(1)} %get-tuple-element.20), channel_id=1, source_target_pairs={{0,1},{1,0},{2,3},{3,2},{4,5},{5,4},{6,7},{7,6},{8,9},{9,8},{10,11... | collective-permute-start | bytes 688136 | tf_op jit(solution)/shard_map/ppermute | solution.py:175
  23.2 12.2 %copy-start.4 = (bf16[2,8,3584]{2,1,0:T(8,128)(2,1)S(1)}, bf16[2,8,3584]{2,1,0:T(8,128)(2,1)}, u32[]{:S(2)}) copy-start(bf16[2,8,3584]{2,1,0:T(8,128)(2,1)} %hidden_ref.3) | copy-start | bytes 344068
  23.2 5.7 %collective-permute-start.11 = (bf16[8,1792]{1,0:T(8,128)(2,1)S(1)}, bf16[8,1792]{1,0:T(8,128)(2,1)S(1)}, u32[]{:S(2)}, u32[]{:S(2)}) collective-permute-start(bf16[8,1792]{1,0:T(8,128)(2,1)S(1)} %get-tuple-element.26), channel_id=1, source_target_pairs={{0,2},{2,0},{4,6},{6,4},{8,10},{10,8},{12,14},{14,12},{1,3},{3,1},... | collective-permute-start | bytes 86024 | tf_op jit(solution)/shard_map/ppermute | solution.py:144
  23.9 6.4 %collective-permute-start.12 = (bf16[8,1792]{1,0:T(8,128)(2,1)S(1)}, bf16[8,1792]{1,0:T(8,128)(2,1)S(1)}, u32[]{:S(2)}, u32[]{:S(2)}) collective-permute-start(bf16[8,1792]{1,0:T(8,128)(2,1)S(1)} %get-tuple-element.27), channel_id=1, source_target_pairs={{0,4},{2,6},{4,0},{6,2},{8,12},{10,14},{12,8},{14,10},{1,5},{3,7},... | collective-permute-start | bytes 86024 | tf_op jit(solution)/shard_map/ppermute | solution.py:144
  25.4 5.2 %collective-permute-start.13 = (bf16[8,1792]{1,0:T(8,128)(2,1)S(1)}, bf16[8,1792]{1,0:T(8,128)(2,1)S(1)}, u32[]{:S(2)}, u32[]{:S(2)}) collective-permute-start(bf16[8,1792]{1,0:T(8,128)(2,1)S(1)} %get-tuple-element.28), channel_id=1, source_target_pairs={{0,6},{2,4},{4,2},{6,0},{8,14},{10,12},{12,10},{14,8},{1,7},{3,5},... | collective-permute-start | bytes 86024 | tf_op jit(solution)/shard_map/ppermute | solution.py:144
  26.8 5.9 %collective-permute-start.8 = (bf16[8,1792]{1,0:T(8,128)(2,1)S(1)}, bf16[8,1792]{1,0:T(8,128)(2,1)S(1)}, u32[]{:S(2)}, u32[]{:S(2)}) collective-permute-start(bf16[8,1792]{1,0:T(8,128)(2,1)S(1)} %get-tuple-element.22), channel_id=1, source_target_pairs={{0,2},{2,0},{4,6},{6,4},{8,10},{10,8},{12,14},{14,12},{1,3},{3,1},... | collective-permute-start | bytes 86024 | tf_op jit(solution)/shard_map/ppermute | solution.py:144
  27.4 5.2 %collective-permute-start.9 = (bf16[8,1792]{1,0:T(8,128)(2,1)S(1)}, bf16[8,1792]{1,0:T(8,128)(2,1)S(1)}, u32[]{:S(2)}, u32[]{:S(2)}) collective-permute-start(bf16[8,1792]{1,0:T(8,128)(2,1)S(1)} %get-tuple-element.23), channel_id=1, source_target_pairs={{0,4},{2,6},{4,0},{6,2},{8,12},{10,14},{12,8},{14,10},{1,5},{3,7},... | collective-permute-start | bytes 86024 | tf_op jit(solution)/shard_map/ppermute | solution.py:144
  28.9 4.8 %collective-permute-start.10 = (bf16[8,1792]{1,0:T(8,128)(2,1)S(1)}, bf16[8,1792]{1,0:T(8,128)(2,1)S(1)}, u32[]{:S(2)}, u32[]{:S(2)}) collective-permute-start(bf16[8,1792]{1,0:T(8,128)(2,1)S(1)} %get-tuple-element.24), channel_id=1, source_target_pairs={{0,6},{2,4},{4,2},{6,0},{8,14},{10,12},{12,10},{14,8},{1,7},{3,5},... | collective-permute-start | bytes 86024 | tf_op jit(solution)/shard_map/ppermute | solution.py:144
  30.6 4.8 %collective-permute-start.14 = (bf16[8,1792]{1,0:T(8,128)(2,1)S(1)}, bf16[8,1792]{1,0:T(8,128)(2,1)S(1)}, u32[]{:S(2)}, u32[]{:S(2)}) collective-permute-start(bf16[8,1792]{1,0:T(8,128)(2,1)S(1)} %shard_map.85), channel_id=1, source_target_pairs={{0,8},{2,10},{4,12},{6,14},{8,0},{10,2},{12,4},{14,6},{1,9},{3,11}... | collective-permute-start | bytes 86024 | tf_op jit(solution)/shard_map/ppermute | solution.py:151
  35.4 0.7 %copy-start.7 = (f32[2,8,1]{1,2,0:T(1,128)S(1)}, f32[2,8,1]{1,2,0:T(1,128)}, u32[]{:S(2)}) copy-start(f32[2,8,1]{1,2,0:T(1,128)} %param.11) | copy-start | bytes 196

commit v2 on v0

v2 whole, which is shorter than its diff:
```python
import functools

import jax
import jax.numpy as jnp
from jax import lax
from jax.experimental import pallas as pl
from jax.experimental.pallas import tpu as pltpu
from jax.sharding import PartitionSpec as P

FF = 1024
SLICE = 128
BF16 = jnp.bfloat16
F32 = jnp.float32


def hits(ids, placed, sizes, node, micro_batch, first, count):
    nodes, capacity, per_node = sizes
    slot = lax.broadcasted_iota(jnp.int32, (count * per_node, ids.shape[1]), 0) + first * per_node
    offset = ids - node
    offset = jnp.where(offset < 0, offset + nodes, offset)
    place = jnp.where(placed >= 0, offset * per_node + micro_batch * capacity + placed, -1)
    return [slot == place[k : k + 1, :] for k in range(ids.shape[0])]


def picks_kernel(sizes, node_size, ids_ref, placed_ref, picks_ref):
    node = lax.axis_index("ep") // node_size
    for m in range(ids_ref.shape[0]):
        flags = hits(ids_ref[m], placed_ref[m], sizes, node, m, 0, sizes[0])
        flags = functools.reduce(jnp.logical_or, flags)
        picks_ref[m] = jnp.where(flags, 1.0, 0.0)


def dispatch_kernel(hidden_ref, gain_ref, picks_ref, own_ref, rest_ref):
    gain = gain_ref[...].astype(F32).reshape(1, -1)
    slots = 0.0
    for m in range(hidden_ref.shape[0]):
        values = hidden_ref[m].astype(F32)
        scale = lax.rsqrt(jnp.mean(values * values, axis=-1, keepdims=True) + 1e-06)
        normed = (values * scale * gain).astype(BF16)
        slots = slots + jnp.dot(picks_ref[m].astype(BF16), normed, preferred_element_type=F32)
    per_node = own_ref.shape[0]
    own_ref[...] = slots[:per_node].astype(BF16)
    rest_ref[...] = slots[per_node:].astype(BF16)


def table_kernel(sizes, node_size, ids_ref, placed_ref, shares_ref, table_ref):
    node = lax.axis_index("ep") // node_size
    for m in range(ids_ref.shape[0]):
        flags = hits(ids_ref[m], placed_ref[m], sizes, node, m, 0, sizes[0])
        table = sum(
            jnp.where(flag, shares_ref[m][k : k + 1, :], 0.0) for k, flag in enumerate(flags)
        )
        table_ref[m] = table.T


def join_kernel(own_ref, inbox_ref, mine_ref):
    mine_ref[...] = jnp.concatenate(
        [own_ref[...].astype(F32), inbox_ref[...].astype(F32)], 0
    ).astype(BF16)


def expert_kernel(
    mine_ref,
    first_ref,
    second_ref,
    far_ref,
    gate_ref,
    up_ref,
    down_ref,
    keep_ref,
    send_ref,
    rows_ref,
):
    core = lax.axis_index("tp")
    half = keep_ref.shape[2]
    rows_ref[0] = mine_ref[...]
    rows_ref[1 + core] = first_ref[...]
    rows_ref[2 - core] = second_ref[...]
    rows_ref[3] = far_ref[...]
    rows = rows_ref[...].reshape(-1, rows_ref.shape[2])
    gate_val = jnp.dot(rows, gate_ref[...], preferred_element_type=F32)
    up_val = jnp.dot(rows, up_ref[...], preferred_element_type=F32)
    active = (gate_val / (1.0 + jnp.exp(-gate_val)) * up_val).astype(BF16)

    def down(which):
        columns = pl.ds(pl.multiple_of(which * half, 128), half)
        return jnp.dot(active, down_ref[:, columns], preferred_element_type=F32)

    send_ref[...] = down(1 - core).astype(BF16).reshape(send_ref.shape)
    keep_ref[...] = down(core).reshape(keep_ref.shape)


def add_cores_kernel(keep_ref, got_ref, far_ref, second_ref, first_ref, mine_ref):
    core = lax.axis_index("tp")

    def total(k):
        return keep_ref[k] + got_ref[k].astype(F32)

    far_ref[...] = total(3).astype(BF16)
    second_ref[...] = total(2 - core).astype(BF16)
    first_ref[...] = total(1 + core)
    mine_ref[...] = total(0)


def pass_on_kernel(first_ref, got_ref, out_ref):
    out_ref[...] = (first_ref[...] + got_ref[...].astype(F32)).astype(BF16)


def members_kernel(mine_ref, first_ref, second_ref, own_ref, outbox_ref):
    total = mine_ref[...] + first_ref[...].astype(F32) + second_ref[...].astype(F32)
    per_node = own_ref.shape[0]
    own_ref[...] = total[:per_node]
    outbox_ref[...] = total[per_node:].astype(BF16)


def weighted(base, weights, block, sizes, micro_batch, first, count):
    nodes, capacity, per_node = sizes
    for n in range(count):
        for c in range(capacity):
            slot = n * per_node + micro_batch * capacity + c
            column = first * per_node + slot
            base = base + weights[:, column : column + 1] * block[slot : slot + 1, :]
    return base


def own_kernel(sizes, hidden_ref, weights_ref, own_ref, out_ref):
    own = own_ref[...]
    half = out_ref.shape[2]
    columns = pl.ds(pl.multiple_of(lax.axis_index("tp") * half, 128), half)
    for m in range(hidden_ref.shape[0]):
        base = hidden_ref[m, :, columns].astype(F32)
        out_ref[m] = weighted(base, weights_ref[m], own, sizes, m, 0, 1)


def rest_kernel(sizes, base_ref, weights_ref, rest_ref, out_ref):
    rest = rest_ref[...].astype(F32)
    for m in range(base_ref.shape[0]):
        out_ref[m] = weighted(base_ref[m], weights_ref[m], rest, sizes, m, 1, sizes[0] - 1).astype(
            BF16
        )


def per_device(hidden, norm_gain, expert_ids, shares, slot_index, w_gate, w_up, w_down):
    micro_count, row_count, model_width = hidden.shape
    top_count = expert_ids.shape[2]
    ep_count = lax.axis_size("ep")
    share_count = lax.axis_size("tp")
    node_size = FF // SLICE // share_count
    nodes = ep_count // node_size
    capacity = row_count * top_count // nodes
    half = model_width // share_count
    per_node = micro_count * capacity
    all_rows = nodes * per_node
    rest_rows = all_rows - per_node
    sizes = (nodes, capacity, per_node)
    ids, placed, weights = (jnp.swapaxes(a, 1, 2) for a in (expert_ids, slot_index, shares))
    small = all_rows <= 32
    params = pltpu.CompilerParams(vmem_limit_bytes=(16 if small else 56) * 1024 * 1024)

    def call(kernel, outs, *args, scratch=(), cost=0):
        return pl.pallas_call(
            kernel,
            out_shape=[jax.ShapeDtypeStruct(shape, kind) for shape, kind in outs],
            scratch_shapes=scratch,
            compiler_params=params,
            cost_estimate=pl.CostEstimate(flops=cost, bytes_accessed=cost // 500, transcendentals=0),
        )(*args)

    def to_first(array):
        return to_partner(array, lambda core: 1 + core)

    def to_second(array):
        return to_partner(array, lambda core: 2 - core)

    def to_partner(array, flip):
        pairs = []
        for j in range(ep_count):
            for core in range(share_count):
                other = j // node_size * node_size + (j % node_size ^ flip(core))
                pairs.append((j * share_count + core, other * share_count + core))
        return lax.ppermute(array, ("ep", "tp"), pairs)

    def to_nodes(array, sign):
        blocks = []
        for n in range(1, nodes):
            block = array if nodes == 2 else array[(n - 1) * per_node : n * per_node]
            pairs = [(j, (j + sign * n * node_size) % ep_count) for j in range(ep_count)]
            blocks.append(lax.ppermute(block, "ep", pairs))
        return blocks[0] if nodes == 2 else jnp.concatenate(blocks, 0)

    (picks,) = call(
        functools.partial(picks_kernel, sizes, node_size),
        [((micro_count, all_rows, row_count), F32)],
        ids,
        placed,
        cost=3 * 10**9,
    )
    own, rest = call(
        dispatch_kernel,
        [((per_node, model_width), BF16), ((rest_rows, model_width), BF16)],
        hidden,
        norm_gain,
        picks,
        cost=20 * 10**9,
    )
    (table,) = call(
        functools.partial(table_kernel, sizes, node_size),
        [((micro_count, row_count, all_rows), F32)],
        ids,
        placed,
        weights,
    )
    inbox = to_nodes(rest, 1)
    (mine,) = call(join_kernel, [((all_rows, model_width), BF16)], own, inbox)
    first = to_first(mine)
    second = to_second(mine)
    far = to_second(first)
    blocks = (node_size, all_rows, half)
    keep, send = call(
        expert_kernel,
        [(blocks, F32), (blocks, BF16)],
        mine,
        first,
        second,
        far,
        w_gate,
        w_up,
        w_down,
        scratch=[pltpu.VMEM((node_size, all_rows, model_width), BF16)],
        cost=10**6,
    )
    got = lax.ppermute(send, "tp", [(i, (i + 1) % share_count) for i in range(share_count)])
    block = (all_rows, half)
    far_sum, second_sum, first_sum, mine_sum = call(
        add_cores_kernel, [(block, BF16), (block, BF16), (block, F32), (block, F32)], keep, got
    )
    far_got = to_second(far_sum)
    second_got = to_second(second_sum)
    (first_sum,) = call(pass_on_kernel, [(block, BF16)], first_sum, far_got)
    first_got = to_first(first_sum)
    own_sum, outbox = call(
        members_kernel,
        [((per_node, half), F32), ((rest_rows, half), BF16)],
        mine_sum,
        first_got,
        second_got,
    )
    returned = to_nodes(outbox, -1)
    rows = (micro_count, row_count, half)
    (base,) = call(functools.partial(own_kernel, sizes), [(rows, F32)], hidden, table, own_sum)
    (mixed,) = call(functools.partial(rest_kernel, sizes), [(rows, BF16)], base, table, returned)
    return mixed


def solution(mesh):
    in_specs = (
        P(None, ("groups", "ep"), None),
        P(),
        P(None, ("groups", "ep"), None),
        P(None, ("groups", "ep"), None),
        P(None, ("groups", "ep"), None),
        P(None, ("ep", "tp")),
        P(None, ("ep", "tp")),
        P(("ep", "tp"), None),
    )
    out_specs = P(None, ("groups", "ep"), "tp")
    return jax.shard_map(
        per_device, mesh=mesh, in_specs=in_specs, out_specs=out_specs, check_vma=False
    )
```

time: 81.2 us -> 35.4 us (0.44)
  local copies, waits for them, and re-layouts: 17.1 us -> 1.59 us
  between operations: 13.8 us -> 0.07 us
  waiting for transfers between devices: 24.1 us -> 16.5 us
  other arithmetic: 5.13 us -> 0 us
  matrix products: 2.8 us -> 0 us
  starting transfers between devices: 17.5 us -> 15 us
  Pallas kernels: 0 us -> 2.02 us
    all_to_all x4 -> x0, waiting for transfers between devices: 17.7 us -> none  [the longest x2 9.44 us: expert_block(): lax.all_to_all(partial_value, 'ep', split_axis=0, concat_axis=0, tiled=True)]
    all_to_all x4 -> x0, starting transfers between devices: 17.5 us -> none  [the longest x2 10.7 us: route_rows(): lax.all_to_all(buffer, 'ep', split_axis=0, concat_axis=0, tiled=True)]
    ppermute x0 -> x9, waiting for transfers between devices: none -> 16.5 us  [the longest x6 10.6 us: to_partner(): return lax.ppermute(array, ('ep', 'tp'), pairs)]
    ppermute x0 -> x9, starting transfers between devices: none -> 15 us  [the longest x6 7.86 us: to_partner(): return lax.ppermute(array, ('ep', 'tp'), pairs)]
    gather x10 -> x0, local copies, waits for them, and re-layouts: 6.55 us -> none  [the longest x8 5.18 us: combine(): picked = flat_rows[place].astype(jnp.float32)]
    reduce_scatter x1 -> x0, waiting for transfers between devices: 6.41 us -> none  [per_device(): lax.psum_scatter(routed.astype(jnp.bfloat16), 'tp', scatter_dimension=2,...]
    scatter x8 -> x0, local copies, waits for them, and re-layouts: 4.78 us -> none  [fill_buffer(): row_table = row_table.at[place.reshape(-1)].set(row_ids.reshape(-1))]
    reshape x9 -> x0, local copies, waits for them, and re-layouts: 3.24 us -> none  [the longest x2 1.51 us: expert_block(): partial_value = partial_value.reshape(ep_count, -1, model_width)]
  transfers between devices with their start and end apart: 5 -> 9, of which waited for: 5 -> 8; matrix products, arithmetic and copies ran while one was open for 15% -> 0% of each run, Pallas kernels for 0% -> 1%
where the time goes in v2:
time: 35.4 us; the launch traced here: 35.2 us
  waiting for transfers between devices  16.5 us (47%)
  starting transfers between devices  15 us (42%)
  Pallas kernels  2.02 us (6%)
  local copies, waits for them, and re-layouts  1.59 us (4%)
    ppermute x6, waiting for transfers between devices, to_partner(): return lax.ppermute(array, ('ep', 'tp'), pairs)  10.6 us
    ppermute x6, starting transfers between devices, to_partner(): return lax.ppermute(array, ('ep', 'tp'), pairs)  7.86 us
    ppermute x2, starting transfers between devices, to_nodes(): blocks.append(lax.ppermute(block, 'ep', pairs))  7.11 us
    ppermute x2, waiting for transfers between devices, to_nodes(): blocks.append(lax.ppermute(block, 'ep', pairs))  4.43 us
    pallas_call x10, Pallas kernels, call(): pl.pallas_call(kernel, out_shape=[jax.ShapeDtypeStruct(shape, kind) for s...  2.02 us
    unnamed x16, local copies, waits for them, and re-layouts  1.59 us
    ppermute x1, waiting for transfers between devices, per_device(): lax.ppermute(send, 'tp', [(i, (i + 1) % share_count) for i in range(share...  1.48 us
  transfers between devices with their start and end apart: 9, of which 8 were waited for; matrix products, arithmetic and copies ran while one was open for 0% of the time, Pallas kernels for 1%

profile of v2, /device:TPU:0, one launch (start us, length us, event | category | flops | bytes accessed | tf_op | source)
XLA Modules:
  0.0 35.2 jit_solution(11085422319406408810)
XLA Ops:
  0.0 0.7 %copy-done.5 = s32[2,8,1]{1,2,0:T(1,128)S(1)} copy-done((s32[2,8,1]{1,2,0:T(1,128)S(1)}, s32[2,8,1]{1,2,0:T(1,128)}, u32[]{:S(2)}) %copy-start.5) | copy-done | bytes 88
  0.7 0.9 %copy-done.3 = bf16[2,8,3584]{2,1,0:T(8,128)(2,1)S(1)} copy-done((bf16[2,8,3584]{2,1,0:T(8,128)(2,1)S(1)}, bf16[2,8,3584]{2,1,0:T(8,128)(2,1)}, u32[]{:S(2)}) %copy-start.3) | copy-done | bytes 114712
  1.6 0.3 shard_map.84
  1.9 4.1 %collective-permute-start = (bf16[8,3584]{1,0:T(8,128)(2,1)S(1)}, bf16[8,3584]{1,0:T(8,128)(2,1)S(1)}, u32[]{:S(2)}, u32[]{:S(2)}) collective-permute-start(bf16[8,3584]{1,0:T(8,128)(2,1)S(1)} %get-tuple-element.16), channel_id=1, source_target_pairs={{0,8},{2,10},{4,12},{6,14},{8,0},{10,2},{12,4},{14,6},{1,9},{3,11}... | collective-permute-start | bytes 172040 | tf_op jit(solution)/shard_map/ppermute | solution.py:188
  6.0 2.8 %collective-permute-done.inbox_ref = bf16[8,3584]{1,0:T(8,128)(2,1)S(1)} collective-permute-done((bf16[8,3584]{1,0:T(8,128)(2,1)S(1)}, bf16[8,3584]{1,0:T(8,128)(2,1)S(1)}, u32[]{:S(2)}, u32[]{:S(2)}) %collective-permute-start) | collective-permute-done | bytes 57376 | tf_op jit(solution)/shard_map/ppermute | solution.py:188
  8.8 1.8 %collective-permute-start.1 = (bf16[16,3584]{1,0:T(8,128)(2,1)S(1)}, bf16[16,3584]{1,0:T(8,128)(2,1)S(1)}, u32[]{:S(2)}, u32[]{:S(2)}) collective-permute-start(bf16[16,3584]{1,0:T(8,128)(2,1)S(1)} %shard_map.85.mine_ref), channel_id=1, source_target_pairs={{0,2},{1,5},{2,0},{3,7},{4,6},{5,1},{6,4},{7,3},{8,10},{9,13},{10,... | collective-permute-start | bytes 344072 | tf_op jit(solution)/shard_map/ppermute | solution.py:181
  10.6 1.2 %collective-permute-start.2 = (bf16[16,3584]{1,0:T(8,128)(2,1)S(1)}, bf16[16,3584]{1,0:T(8,128)(2,1)S(1)}, u32[]{:S(2)}, u32[]{:S(2)}) collective-permute-start(bf16[16,3584]{1,0:T(8,128)(2,1)S(1)} %shard_map.85.mine_ref), channel_id=1, source_target_pairs={{0,4},{1,3},{2,6},{3,1},{4,0},{5,7},{6,2},{7,5},{8,12},{9,11},{10,... | collective-permute-start | bytes 344072 | tf_op jit(solution)/shard_map/ppermute | solution.py:181
  11.7 2.2 %collective-permute-done.1.first_ref = bf16[16,3584]{1,0:T(8,128)(2,1)S(1)} collective-permute-done((bf16[16,3584]{1,0:T(8,128)(2,1)S(1)}, bf16[16,3584]{1,0:T(8,128)(2,1)S(1)}, u32[]{:S(2)}, u32[]{:S(2)}) %collective-permute-start.1) | collective-permute-done | bytes 114720 | tf_op jit(solution)/shard_map/ppermute | solution.py:181
  14.0 1.0 %collective-permute-start.3 = (bf16[16,3584]{1,0:T(8,128)(2,1)S(1)}, bf16[16,3584]{1,0:T(8,128)(2,1)S(1)}, u32[]{:S(2)}, u32[]{:S(2)}) collective-permute-start(bf16[16,3584]{1,0:T(8,128)(2,1)S(1)} %collective-permute-done.1.first_ref), channel_id=1, source_target_pairs={{0,4},{1,3},{2,6},{3,1},{4,0},{5,7},{6,2},{7,5},{8,12},{9,11},{10,... | collective-permute-start | bytes 344072 | tf_op jit(solution)/shard_map/ppermute | solution.py:181
  15.0 0.4 %collective-permute-done.2.second_ref = bf16[16,3584]{1,0:T(8,128)(2,1)S(1)} collective-permute-done((bf16[16,3584]{1,0:T(8,128)(2,1)S(1)}, bf16[16,3584]{1,0:T(8,128)(2,1)S(1)}, u32[]{:S(2)}, u32[]{:S(2)}) %collective-permute-start.2) | collective-permute-done | bytes 114720 | tf_op jit(solution)/shard_map/ppermute | solution.py:181
  15.4 3.4 %collective-permute-done.3.far_ref = bf16[16,3584]{1,0:T(8,128)(2,1)S(1)} collective-permute-done((bf16[16,3584]{1,0:T(8,128)(2,1)S(1)}, bf16[16,3584]{1,0:T(8,128)(2,1)S(1)}, u32[]{:S(2)}, u32[]{:S(2)}) %collective-permute-start.3) | collective-permute-done | bytes 114720 | tf_op jit(solution)/shard_map/ppermute | solution.py:181
  18.8 0.7 %shard_map.86 = (f32[4,16,1792]{2,1,0:T(8,128)S(1)}, bf16[4,16,1792]{2,1,0:T(8,128)(2,1)S(1)}) custom-call(bf16[16,3584]{1,0:T(8,128)(2,1)S(1)} %shard_map.85.mine_ref, bf16[16,3584]{1,0:T(8,128)(2,1)S(1)} %collective-permute-done.1.first_ref, bf16[16,3584]{1,0:T(8,128)(2,1)S(1)} %collective-permute-done.2.second_ref, ...), custom_call_target="tpu_custom_call" | custom-call | flops 1000000 | bytes 2000 | tf_op jit(solution)/shard_map/pallas_call | solution.py:161
  19.5 0.1 collective-permute-start.4
  19.5 1.5 %collective-permute-done.4.got_ref = bf16[4,16,1792]{2,1,0:T(8,128)(2,1)S(1)} collective-permute-done((bf16[4,16,1792]{2,1,0:T(8,128)(2,1)S(1)}, bf16[4,16,1792]{2,1,0:T(8,128)(2,1)S(1)}, u32[]{:S(2)}, u32[]{:S(2)}) %collective-permute-start.4) | collective-permute-done | bytes 229408 | tf_op jit(solution)/shard_map/ppermute | solution.py:232
  21.1 1.0 %collective-permute-start.5 = (bf16[16,1792]{1,0:T(8,128)(2,1)S(1)}, bf16[16,1792]{1,0:T(8,128)(2,1)S(1)}, u32[]{:S(2)}, u32[]{:S(2)}) collective-permute-start(bf16[16,1792]{1,0:T(8,128)(2,1)S(1)} %get-tuple-element.21), channel_id=1, source_target_pairs={{0,4},{1,3},{2,6},{3,1},{4,0},{5,7},{6,2},{7,5},{8,12},{9,11},{10,... | collective-permute-start | bytes 172040 | tf_op jit(solution)/shard_map/ppermute | solution.py:181
  22.1 1.1 %collective-permute-start.7 = (bf16[16,1792]{1,0:T(8,128)(2,1)S(1)}, bf16[16,1792]{1,0:T(8,128)(2,1)S(1)}, u32[]{:S(2)}, u32[]{:S(2)}) collective-permute-start(bf16[16,1792]{1,0:T(8,128)(2,1)S(1)} %get-tuple-element.22), channel_id=1, source_target_pairs={{0,4},{1,3},{2,6},{3,1},{4,0},{5,7},{6,2},{7,5},{8,12},{9,11},{10,... | collective-permute-start | bytes 172040 | tf_op jit(solution)/shard_map/ppermute | solution.py:181
  23.2 2.2 %collective-permute-done.5.got_ref = bf16[16,1792]{1,0:T(8,128)(2,1)S(1)} collective-permute-done((bf16[16,1792]{1,0:T(8,128)(2,1)S(1)}, bf16[16,1792]{1,0:T(8,128)(2,1)S(1)}, u32[]{:S(2)}, u32[]{:S(2)}) %collective-permute-start.5) | collective-permute-done | bytes 57376 | tf_op jit(solution)/shard_map/ppermute | solution.py:181
  25.3 1.8 %collective-permute-start.6 = (bf16[16,1792]{1,0:T(8,128)(2,1)S(1)}, bf16[16,1792]{1,0:T(8,128)(2,1)S(1)}, u32[]{:S(2)}, u32[]{:S(2)}) collective-permute-start(bf16[16,1792]{1,0:T(8,128)(2,1)S(1)} %shard_map.88), channel_id=1, source_target_pairs={{0,2},{1,5},{2,0},{3,7},{4,6},{5,1},{6,4},{7,3},{8,10},{9,13},{10,... | collective-permute-start | bytes 172040 | tf_op jit(solution)/shard_map/ppermute | solution.py:181
  27.2 2.4 %collective-permute-done.6.first_ref = bf16[16,1792]{1,0:T(8,128)(2,1)S(1)} collective-permute-done((bf16[16,1792]{1,0:T(8,128)(2,1)S(1)}, bf16[16,1792]{1,0:T(8,128)(2,1)S(1)}, u32[]{:S(2)}, u32[]{:S(2)}) %collective-permute-start.6) | collective-permute-done | bytes 57376 | tf_op jit(solution)/shard_map/ppermute | solution.py:181
  29.6 3.0 %collective-permute-start.8 = (bf16[8,1792]{1,0:T(8,128)(2,1)S(1)}, bf16[8,1792]{1,0:T(8,128)(2,1)S(1)}, u32[]{:S(2)}, u32[]{:S(2)}) collective-permute-start(bf16[8,1792]{1,0:T(8,128)(2,1)S(1)} %get-tuple-element.24), channel_id=1, source_target_pairs={{0,8},{2,10},{4,12},{6,14},{8,0},{10,2},{12,4},{14,6},{1,9},{3,11}... | collective-permute-start | bytes 86024 | tf_op jit(solution)/shard_map/ppermute | solution.py:188
  32.6 0.1 shard_map.82.weights_ref
  32.7 0.1 shard_map.90.base_ref
  32.8 1.7 %collective-permute-done.8.rest_ref = bf16[8,1792]{1,0:T(8,128)(2,1)S(1)} collective-permute-done((bf16[8,1792]{1,0:T(8,128)(2,1)S(1)}, bf16[8,1792]{1,0:T(8,128)(2,1)S(1)}, u32[]{:S(2)}, u32[]{:S(2)}) %collective-permute-start.8) | collective-permute-done | bytes 28704 | tf_op jit(solution)/shard_map/ppermute | solution.py:188
  34.5 0.7 %shard_map.91 = bf16[2,8,1792]{2,1,0:T(8,128)(2,1)} custom-call(f32[2,8,1792]{2,1,0:T(8,128)S(1)} %shard_map.90.base_ref, f32[2,8,16]{2,1,0:T(8,128)S(1)} %shard_map.82.weights_ref, bf16[8,1792]{1,0:T(8,128)(2,1)S(1)} %collective-permute-done.8.rest_ref), custom_call_target="tpu_custom_call" | custom-call | tf_op jit(solution)/shard_map/pallas_call | solution.py:161
  (20 shorter events, 0.1 us)
Async XLA Ops:
  0.0 0.7 %copy-start.5 = (s32[2,8,1]{1,2,0:T(1,128)S(1)}, s32[2,8,1]{1,2,0:T(1,128)}, u32[]{:S(2)}) copy-start(s32[2,8,1]{1,2,0:T(1,128)} %param.12) | copy-start | bytes 196
  0.0 0.7 %copy-start.4 = (s32[2,8,1]{1,2,0:T(1,128)S(1)}, s32[2,8,1]{1,2,0:T(1,128)}, u32[]{:S(2)}) copy-start(s32[2,8,1]{1,2,0:T(1,128)} %param.10) | copy-start | bytes 196
  0.7 0.9 %copy-start.3 = (bf16[2,8,3584]{2,1,0:T(8,128)(2,1)S(1)}, bf16[2,8,3584]{2,1,0:T(8,128)(2,1)}, u32[]{:S(2)}) copy-start(bf16[2,8,3584]{2,1,0:T(8,128)(2,1)} %hidden_ref.3) | copy-start | bytes 344068
  0.7 0.9 %copy-start.7 = (bf16[3584]{0:T(1024)(128)(2,1)S(1)}, bf16[3584]{0:T(1024)(128)(2,1)}, u32[]{:S(2)}) copy-start(bf16[3584]{0:T(1024)(128)(2,1)} %gain_ref.1) | copy-start | bytes 21508
  1.6 17.2 %copy-start = (bf16[3584,128]{1,0:T(8,128)(2,1)S(1)}, bf16[3584,128]{1,0:T(8,128)(2,1)}, u32[]{:S(2)}) copy-start(bf16[3584,128]{1,0:T(8,128)(2,1)} %gate_ref.1) | copy-start | bytes 2752516
  1.6 17.2 %copy-start.1 = (bf16[3584,128]{1,0:T(8,128)(2,1)S(1)}, bf16[3584,128]{1,0:T(8,128)(2,1)}, u32[]{:S(2)}) copy-start(bf16[3584,128]{1,0:T(8,128)(2,1)} %up_ref.1) | copy-start | bytes 2752516
  1.6 17.2 %copy-start.2 = (bf16[128,3584]{1,0:T(8,128)(2,1)S(1)}, bf16[128,3584]{1,0:T(8,128)(2,1)}, u32[]{:S(2)}) copy-start(bf16[128,3584]{1,0:T(8,128)(2,1)} %down_ref.1) | copy-start | bytes 2752516
  1.9 6.9 %collective-permute-start = (bf16[8,3584]{1,0:T(8,128)(2,1)S(1)}, bf16[8,3584]{1,0:T(8,128)(2,1)S(1)}, u32[]{:S(2)}, u32[]{:S(2)}) collective-permute-start(bf16[8,3584]{1,0:T(8,128)(2,1)S(1)} %get-tuple-element.16), channel_id=1, source_target_pairs={{0,8},{2,10},{4,12},{6,14},{8,0},{10,2},{12,4},{14,6},{1,9},{3,11}... | collective-permute-start | bytes 172040 | tf_op jit(solution)/shard_map/ppermute | solution.py:188
  8.8 5.2 %collective-permute-start.1 = (bf16[16,3584]{1,0:T(8,128)(2,1)S(1)}, bf16[16,3584]{1,0:T(8,128)(2,1)S(1)}, u32[]{:S(2)}, u32[]{:S(2)}) collective-permute-start(bf16[16,3584]{1,0:T(8,128)(2,1)S(1)} %shard_map.85.mine_ref), channel_id=1, source_target_pairs={{0,2},{1,5},{2,0},{3,7},{4,6},{5,1},{6,4},{7,3},{8,10},{9,13},{10,... | collective-permute-start | bytes 344072 | tf_op jit(solution)/shard_map/ppermute | solution.py:181
  10.6 4.8 %collective-permute-start.2 = (bf16[16,3584]{1,0:T(8,128)(2,1)S(1)}, bf16[16,3584]{1,0:T(8,128)(2,1)S(1)}, u32[]{:S(2)}, u32[]{:S(2)}) collective-permute-start(bf16[16,3584]{1,0:T(8,128)(2,1)S(1)} %shard_map.85.mine_ref), channel_id=1, source_target_pairs={{0,4},{1,3},{2,6},{3,1},{4,0},{5,7},{6,2},{7,5},{8,12},{9,11},{10,... | collective-permute-start | bytes 344072 | tf_op jit(solution)/shard_map/ppermute | solution.py:181
  14.0 4.8 %collective-permute-start.3 = (bf16[16,3584]{1,0:T(8,128)(2,1)S(1)}, bf16[16,3584]{1,0:T(8,128)(2,1)S(1)}, u32[]{:S(2)}, u32[]{:S(2)}) collective-permute-start(bf16[16,3584]{1,0:T(8,128)(2,1)S(1)} %collective-permute-done.1.first_ref), channel_id=1, source_target_pairs={{0,4},{1,3},{2,6},{3,1},{4,0},{5,7},{6,2},{7,5},{8,12},{9,11},{10,... | collective-permute-start | bytes 344072 | tf_op jit(solution)/shard_map/ppermute | solution.py:181
  19.5 1.6 %collective-permute-start.4 = (bf16[4,16,1792]{2,1,0:T(8,128)(2,1)S(1)}, bf16[4,16,1792]{2,1,0:T(8,128)(2,1)S(1)}, u32[]{:S(2)}, u32[]{:S(2)}) collective-permute-start(bf16[4,16,1792]{2,1,0:T(8,128)(2,1)S(1)} %get-tuple-element.18), channel_id=1, source_target_pairs={{0,1},{1,0},{2,3},{3,2},{4,5},{5,4},{6,7},{7,6},{8,9},{9,8},{10,11... | collective-permute-start | bytes 688136 | tf_op jit(solution)/shard_map/ppermute | solution.py:232
  21.1 4.2 %collective-permute-start.5 = (bf16[16,1792]{1,0:T(8,128)(2,1)S(1)}, bf16[16,1792]{1,0:T(8,128)(2,1)S(1)}, u32[]{:S(2)}, u32[]{:S(2)}) collective-permute-start(bf16[16,1792]{1,0:T(8,128)(2,1)S(1)} %get-tuple-element.21), channel_id=1, source_target_pairs={{0,4},{1,3},{2,6},{3,1},{4,0},{5,7},{6,2},{7,5},{8,12},{9,11},{10,... | collective-permute-start | bytes 172040 | tf_op jit(solution)/shard_map/ppermute | solution.py:181
  22.1 5.1 %collective-permute-start.7 = (bf16[16,1792]{1,0:T(8,128)(2,1)S(1)}, bf16[16,1792]{1,0:T(8,128)(2,1)S(1)}, u32[]{:S(2)}, u32[]{:S(2)}) collective-permute-start(bf16[16,1792]{1,0:T(8,128)(2,1)S(1)} %get-tuple-element.22), channel_id=1, source_target_pairs={{0,4},{1,3},{2,6},{3,1},{4,0},{5,7},{6,2},{7,5},{8,12},{9,11},{10,... | collective-permute-start | bytes 172040 | tf_op jit(solution)/shard_map/ppermute | solution.py:181
  25.3 4.2 %collective-permute-start.6 = (bf16[16,1792]{1,0:T(8,128)(2,1)S(1)}, bf16[16,1792]{1,0:T(8,128)(2,1)S(1)}, u32[]{:S(2)}, u32[]{:S(2)}) collective-permute-start(bf16[16,1792]{1,0:T(8,128)(2,1)S(1)} %shard_map.88), channel_id=1, source_target_pairs={{0,2},{1,5},{2,0},{3,7},{4,6},{5,1},{6,4},{7,3},{8,10},{9,13},{10,... | collective-permute-start | bytes 172040 | tf_op jit(solution)/shard_map/ppermute | solution.py:181
  29.6 3.0 %copy-start.6 = (f32[2,8,1]{1,2,0:T(1,128)S(1)}, f32[2,8,1]{1,2,0:T(1,128)}, u32[]{:S(2)}) copy-start(f32[2,8,1]{1,2,0:T(1,128)} %param.11) | copy-start | bytes 196
  29.6 4.9 %collective-permute-start.8 = (bf16[8,1792]{1,0:T(8,128)(2,1)S(1)}, bf16[8,1792]{1,0:T(8,128)(2,1)S(1)}, u32[]{:S(2)}, u32[]{:S(2)}) collective-permute-start(bf16[8,1792]{1,0:T(8,128)(2,1)S(1)} %get-tuple-element.24), channel_id=1, source_target_pairs={{0,8},{2,10},{4,12},{6,14},{8,0},{10,2},{12,4},{14,6},{1,9},{3,11}... | collective-permute-start | bytes 86024 | tf_op jit(solution)/shard_map/ppermute | solution.py:188

commit v3 on v2

v3 whole, which is shorter than its diff:
```python
import functools

import jax
import jax.numpy as jnp
from jax import lax
from jax.experimental import pallas as pl
from jax.experimental.pallas import tpu as pltpu
from jax.sharding import PartitionSpec as P

FF = 1024
SLICE = 128
BF16 = jnp.bfloat16
F32 = jnp.float32


def hits(ids, placed, slot, sizes, node, micro_batch):
    nodes, capacity, per_node = sizes
    offset = ids - node
    offset = jnp.where(offset < 0, offset + nodes, offset)
    place = jnp.where(placed >= 0, offset * per_node + micro_batch * capacity + placed, -1)
    return [slot == place[k : k + 1, :] for k in range(ids.shape[0])]


def slots_kernel(slot_ref):
    slot_ref[...] = lax.broadcasted_iota(jnp.int32, slot_ref.shape, 0)


def dispatch_kernel(
    sizes, node_size, slot_ref, hidden_ref, gain_ref, ids_ref, placed_ref, own_ref, rest_ref
):
    node = lax.axis_index("ep") // node_size
    gain = gain_ref[...].astype(F32).reshape(1, -1)
    slots = 0.0
    for m in range(hidden_ref.shape[0]):
        flags = hits(ids_ref[m], placed_ref[m], slot_ref[...], sizes, node, m)
        picks = jnp.where(functools.reduce(jnp.logical_or, flags), 1.0, 0.0).astype(BF16)
        values = hidden_ref[m].astype(F32)
        scale = lax.rsqrt(jnp.mean(values * values, axis=-1, keepdims=True) + 1e-06)
        normed = (values * scale * gain).astype(BF16)
        slots = slots + jnp.dot(picks, normed, preferred_element_type=F32)
    per_node = own_ref.shape[0]
    own_ref[...] = slots[:per_node].astype(BF16)
    rest_ref[...] = slots[per_node:].astype(BF16)


def table_kernel(sizes, node_size, slot_ref, ids_ref, placed_ref, shares_ref, table_ref):
    node = lax.axis_index("ep") // node_size
    for m in range(ids_ref.shape[0]):
        flags = hits(ids_ref[m], placed_ref[m], slot_ref[...], sizes, node, m)
        table = sum(
            jnp.where(flag, shares_ref[m][k : k + 1, :], 0.0) for k, flag in enumerate(flags)
        )
        table_ref[m] = table.T


def expert_kernel(*refs):
    pieces, (gate_ref, up_ref, down_ref, keep_ref, send_ref) = refs[:-5], refs[-5:]
    core = lax.axis_index("tp")
    half = keep_ref.shape[2]
    rows = jnp.concatenate([ref[...].astype(F32) for ref in pieces], 0).astype(BF16)
    gate_val = jnp.dot(rows, gate_ref[...], preferred_element_type=F32)
    up_val = jnp.dot(rows, up_ref[...], preferred_element_type=F32)
    active = (gate_val / (1.0 + jnp.exp(-gate_val)) * up_val).astype(BF16)

    def down(which):
        columns = pl.ds(pl.multiple_of(which * half, 128), half)
        return jnp.dot(active, down_ref[:, columns], preferred_element_type=F32)

    send_ref[...] = down(1 - core).astype(BF16).reshape(send_ref.shape)
    keep_ref[...] = down(core).reshape(keep_ref.shape)


def add_cores_kernel(keep_ref, got_ref, *out_refs):
    for k in range(keep_ref.shape[0]):
        total = keep_ref[k] + got_ref[k].astype(F32)
        own_ref, rest_ref = out_refs[2 * k : 2 * k + 2]
        per_node = own_ref.shape[0]
        own_ref[...] = total[:per_node].astype(own_ref.dtype)
        rest_ref[...] = total[per_node:].astype(rest_ref.dtype)


def add_members_kernel(*refs):
    total = refs[0][...]
    for ref in refs[1:-1]:
        total = total + ref[...].astype(F32)
    refs[-1][...] = total.astype(BF16)


def weighted(base, weights, block, sizes, micro_batch, first, count):
    nodes, capacity, per_node = sizes
    for n in range(count):
        for c in range(capacity):
            slot = n * per_node + micro_batch * capacity + c
            column = first * per_node + slot
            base = base + weights[:, column : column + 1] * block[slot : slot + 1, :]
    return base


def own_kernel(sizes, hidden_ref, weights_ref, *refs):
    own_refs, out_ref = refs[:-1], refs[-1]
    own = own_refs[0][...]
    for ref in own_refs[1:]:
        own = own + ref[...].astype(F32)
    half = out_ref.shape[2]
    columns = pl.ds(pl.multiple_of(lax.axis_index("tp") * half, 128), half)
    for m in range(hidden_ref.shape[0]):
        base = hidden_ref[m, :, columns].astype(F32)
        out_ref[m] = weighted(base, weights_ref[m], own, sizes, m, 0, 1)


def rest_kernel(sizes, base_ref, weights_ref, rest_ref, out_ref):
    rest = rest_ref[...].astype(F32)
    for m in range(base_ref.shape[0]):
        out_ref[m] = weighted(base_ref[m], weights_ref[m], rest, sizes, m, 1, sizes[0] - 1).astype(
            BF16
        )


def per_device(hidden, norm_gain, expert_ids, shares, slot_index, w_gate, w_up, w_down):
    micro_count, row_count, model_width = hidden.shape
    top_count = expert_ids.shape[2]
    ep_count = lax.axis_size("ep")
    share_count = lax.axis_size("tp")
    node_size = FF // SLICE // share_count
    nodes = ep_count // node_size
    capacity = row_count * top_count // nodes
    half = model_width // share_count
    per_node = micro_count * capacity
    all_rows = nodes * per_node
    rest_rows = all_rows - per_node
    sizes = (nodes, capacity, per_node)
    ids, placed, weights = (jnp.swapaxes(a, 1, 2) for a in (expert_ids, slot_index, shares))
    small = all_rows <= 32
    params = pltpu.CompilerParams(vmem_limit_bytes=(16 if small else 56) * 1024 * 1024)

    def call(kernel, outs, *args, scratch=(), cost=0):
        return pl.pallas_call(
            kernel,
            out_shape=[jax.ShapeDtypeStruct(shape, kind) for shape, kind in outs],
            scratch_shapes=scratch,
            compiler_params=params,
            cost_estimate=pl.CostEstimate(flops=cost, bytes_accessed=cost // 500, transcendentals=0),
        )(*args)

    def to_member(array, k):
        pairs = [(j, j // node_size * node_size + (j % node_size ^ k)) for j in range(ep_count)]
        return lax.ppermute(array, "ep", pairs)

    def to_nodes(array, sign):
        blocks = []
        for n in range(1, nodes):
            block = array if nodes == 2 else array[(n - 1) * per_node : n * per_node]
            pairs = [(j, (j + sign * n * node_size) % ep_count) for j in range(ep_count)]
            blocks.append(lax.ppermute(block, "ep", pairs))
        return blocks[0] if nodes == 2 else jnp.concatenate(blocks, 0)

    (slot,) = call(slots_kernel, [((all_rows, row_count), jnp.int32)], cost=5 * 10**9)
    own, rest = call(
        functools.partial(dispatch_kernel, sizes, node_size),
        [((per_node, model_width), BF16), ((rest_rows, model_width), BF16)],
        slot,
        hidden,
        norm_gain,
        ids,
        placed,
        cost=20 * 10**9,
    )
    (table,) = call(
        functools.partial(table_kernel, sizes, node_size),
        [((micro_count, row_count, all_rows), F32)],
        slot,
        ids,
        placed,
        weights,
    )
    members = range(1, node_size)
    inbox = to_nodes(rest, 1)
    owns = [own] + [to_member(own, k) for k in members]
    rests = [inbox] + [to_member(inbox, k) for k in members]
    blocks = (node_size, all_rows, half)
    keep, send = call(
        expert_kernel,
        [(blocks, F32), (blocks, BF16)],
        *[piece for pair in zip(owns, rests) for piece in pair],
        w_gate,
        w_up,
        w_down,
        cost=10**6,
    )
    got = lax.ppermute(send, "tp", [(i, (i + 1) % share_count) for i in range(share_count)])
    sums = call(
        add_cores_kernel,
        [
            ((count, half), kind)
            for kind in [F32] + [BF16] * (node_size - 1)
            for count in (per_node, rest_rows)
        ],
        keep,
        got,
    )
    away = [sums[1]] + [to_member(sums[2 * k + 1], k) for k in members]
    home = [sums[0]] + [to_member(sums[2 * k], k) for k in members]
    (outbox,) = call(add_members_kernel, [((rest_rows, half), BF16)], *away)
    returned = to_nodes(outbox, -1)
    rows = (micro_count, row_count, half)
    (base,) = call(functools.partial(own_kernel, sizes), [(rows, F32)], hidden, table, *home)
    (mixed,) = call(functools.partial(rest_kernel, sizes), [(rows, BF16)], base, table, returned)
    return mixed


def solution(mesh):
    in_specs = (
        P(None, ("groups", "ep"), None),
        P(),
        P(None, ("groups", "ep"), None),
        P(None, ("groups", "ep"), None),
        P(None, ("groups", "ep"), None),
        P(None, ("ep", "tp")),
        P(None, ("ep", "tp")),
        P(("ep", "tp"), None),
    )
    out_specs = P(None, ("groups", "ep"), "tp")
    return jax.shard_map(
        per_device, mesh=mesh, in_specs=in_specs, out_specs=out_specs, check_vma=False
    )
```

time: 35.4 us -> 31.3 us (0.88)
  waiting for transfers between devices: 16.5 us -> 7.93 us
  starting transfers between devices: 15 us -> 20.3 us
  local copies, waits for them, and re-layouts: 1.59 us -> 0.91 us
    ppermute x6 -> x12, starting transfers between devices: 7.86 us -> 14.1 us  [to_member(): return lax.ppermute(array, 'ep', pairs)]
    ppermute x6 -> x12, waiting for transfers between devices: 10.6 us -> 4.89 us  [to_member(): return lax.ppermute(array, 'ep', pairs)]
    ppermute x2, waiting for transfers between devices: 4.43 us -> 1.56 us  [to_nodes(): blocks.append(lax.ppermute(block, 'ep', pairs))]
    ppermute x2, starting transfers between devices: 7.11 us -> 6.14 us  [to_nodes(): blocks.append(lax.ppermute(block, 'ep', pairs))]
    unnamed x16, local copies, waits for them, and re-layouts: 1.59 us -> 0.91 us
    pallas_call x10 -> x8, Pallas kernels: 2.02 us -> 1.97 us  [call(): pl.pallas_call(kernel, out_shape=[jax.ShapeDtypeStruct(shape, kind) for s...]
  transfers between devices with their start and end apart: 9 -> 15, of which waited for: 8 -> 8; matrix products, arithmetic and copies ran while one was open for 0% -> 0% of each run, Pallas kernels for 1% -> 1%
where the time goes in v3:
time: 31.3 us; the launch traced here: 31.2 us
  starting transfers between devices  20.3 us (65%)
  waiting for transfers between devices  7.93 us (25%)
  Pallas kernels  1.97 us (6%)
  local copies, waits for them, and re-layouts  0.91 us (3%)
    ppermute x12, starting transfers between devices, to_member(): return lax.ppermute(array, 'ep', pairs)  14.1 us
    ppermute x2, starting transfers between devices, to_nodes(): blocks.append(lax.ppermute(block, 'ep', pairs))  6.14 us
    ppermute x12, waiting for transfers between devices, to_member(): return lax.ppermute(array, 'ep', pairs)  4.89 us
    pallas_call x8, Pallas kernels, call(): pl.pallas_call(kernel, out_shape=[jax.ShapeDtypeStruct(shape, kind) for s...  1.97 us
    ppermute x2, waiting for transfers between devices, to_nodes(): blocks.append(lax.ppermute(block, 'ep', pairs))  1.56 us
    ppermute x1, waiting for transfers between devices, per_device(): lax.ppermute(send, 'tp', [(i, (i + 1) % share_count) for i in range(share...  1.48 us
    unnamed x16, local copies, waits for them, and re-layouts  0.91 us
  transfers between devices with their start and end apart: 15, of which 8 were waited for; matrix products, arithmetic and copies ran while one was open for 0% of the time, Pallas kernels for 1%

profile of v3, /device:TPU:0, one launch (start us, length us, event | category | flops | bytes accessed | tf_op | source)
XLA Modules:
  0.0 31.2 jit_solution(7273658013413330573)
XLA Ops:
  0.0 0.9 %copy-done.3 = bf16[2,8,3584]{2,1,0:T(8,128)(2,1)S(1)} copy-done((bf16[2,8,3584]{2,1,0:T(8,128)(2,1)S(1)}, bf16[2,8,3584]{2,1,0:T(8,128)(2,1)}, u32[]{:S(2)}) %copy-start.3) | copy-done | bytes 114712
  0.9 0.3 shard_map.84
  1.3 4.1 %collective-permute-start = (bf16[8,3584]{1,0:T(8,128)(2,1)S(1)}, bf16[8,3584]{1,0:T(8,128)(2,1)S(1)}, u32[]{:S(2)}, u32[]{:S(2)}) collective-permute-start(bf16[8,3584]{1,0:T(8,128)(2,1)S(1)} %get-tuple-element.18), channel_id=1, source_target_pairs={{0,8},{2,10},{4,12},{6,14},{8,0},{10,2},{12,4},{14,6},{1,9},{3,11}... | collective-permute-start | bytes 172040 | tf_op jit(solution)/shard_map/ppermute | solution.py:154
  5.4 2.5 %collective-permute-start.5 = (bf16[8,3584]{1,0:T(8,128)(2,1)S(1)}, bf16[8,3584]{1,0:T(8,128)(2,1)S(1)}, u32[]{:S(2)}, u32[]{:S(2)}) collective-permute-start(bf16[8,3584]{1,0:T(8,128)(2,1)S(1)} %get-tuple-element.17.refs_0_), channel_id=1, source_target_pairs={{0,6},{2,4},{4,2},{6,0},{8,14},{10,12},{12,10},{14,8},{1,7},{3,5},... | collective-permute-start | bytes 172040 | tf_op jit(solution)/shard_map/ppermute | solution.py:147
  7.9 0.4 %collective-permute-start.3 = (bf16[8,3584]{1,0:T(8,128)(2,1)S(1)}, bf16[8,3584]{1,0:T(8,128)(2,1)S(1)}, u32[]{:S(2)}, u32[]{:S(2)}) collective-permute-start(bf16[8,3584]{1,0:T(8,128)(2,1)S(1)} %get-tuple-element.17.refs_0_), channel_id=1, source_target_pairs={{0,4},{2,6},{4,0},{6,2},{8,12},{10,14},{12,8},{14,10},{1,5},{3,7},... | collective-permute-start | bytes 172040 | tf_op jit(solution)/shard_map/ppermute | solution.py:147
  8.3 0.5 %collective-permute-start.1 = (bf16[8,3584]{1,0:T(8,128)(2,1)S(1)}, bf16[8,3584]{1,0:T(8,128)(2,1)S(1)}, u32[]{:S(2)}, u32[]{:S(2)}) collective-permute-start(bf16[8,3584]{1,0:T(8,128)(2,1)S(1)} %get-tuple-element.17.refs_0_), channel_id=1, source_target_pairs={{0,2},{2,0},{4,6},{6,4},{8,10},{10,8},{12,14},{14,12},{1,3},{3,1},... | collective-permute-start | bytes 172040 | tf_op jit(solution)/shard_map/ppermute | solution.py:147
  8.8 2.5 %collective-permute-start.6 = (bf16[8,3584]{1,0:T(8,128)(2,1)S(1)}, bf16[8,3584]{1,0:T(8,128)(2,1)S(1)}, u32[]{:S(2)}, u32[]{:S(2)}) collective-permute-start(bf16[8,3584]{1,0:T(8,128)(2,1)S(1)} %collective-permute-done.refs_1_), channel_id=1, source_target_pairs={{0,6},{2,4},{4,2},{6,0},{8,14},{10,12},{12,10},{14,8},{1,7},{3,5},... | collective-permute-start | bytes 172040 | tf_op jit(solution)/shard_map/ppermute | solution.py:147
  11.4 0.4 %collective-permute-start.4 = (bf16[8,3584]{1,0:T(8,128)(2,1)S(1)}, bf16[8,3584]{1,0:T(8,128)(2,1)S(1)}, u32[]{:S(2)}, u32[]{:S(2)}) collective-permute-start(bf16[8,3584]{1,0:T(8,128)(2,1)S(1)} %collective-permute-done.refs_1_), channel_id=1, source_target_pairs={{0,4},{2,6},{4,0},{6,2},{8,12},{10,14},{12,8},{14,10},{1,5},{3,7},... | collective-permute-start | bytes 172040 | tf_op jit(solution)/shard_map/ppermute | solution.py:147
  11.8 0.6 %collective-permute-start.2 = (bf16[8,3584]{1,0:T(8,128)(2,1)S(1)}, bf16[8,3584]{1,0:T(8,128)(2,1)S(1)}, u32[]{:S(2)}, u32[]{:S(2)}) collective-permute-start(bf16[8,3584]{1,0:T(8,128)(2,1)S(1)} %collective-permute-done.refs_1_), channel_id=1, source_target_pairs={{0,2},{2,0},{4,6},{6,4},{8,10},{10,8},{12,14},{14,12},{1,3},{3,1},... | collective-permute-start | bytes 172040 | tf_op jit(solution)/shard_map/ppermute | solution.py:147
  12.5 1.4 %collective-permute-done.6.refs_7_ = bf16[8,3584]{1,0:T(8,128)(2,1)S(1)} collective-permute-done((bf16[8,3584]{1,0:T(8,128)(2,1)S(1)}, bf16[8,3584]{1,0:T(8,128)(2,1)S(1)}, u32[]{:S(2)}, u32[]{:S(2)}) %collective-permute-start.6) | collective-permute-done | bytes 57376 | tf_op jit(solution)/shard_map/ppermute | solution.py:147
  13.9 1.6 %collective-permute-done.4.refs_5_ = bf16[8,3584]{1,0:T(8,128)(2,1)S(1)} collective-permute-done((bf16[8,3584]{1,0:T(8,128)(2,1)S(1)}, bf16[8,3584]{1,0:T(8,128)(2,1)S(1)}, u32[]{:S(2)}, u32[]{:S(2)}) %collective-permute-start.4) | collective-permute-done | bytes 57376 | tf_op jit(solution)/shard_map/ppermute | solution.py:147
  15.5 0.5 %collective-permute-done.2.refs_3_ = bf16[8,3584]{1,0:T(8,128)(2,1)S(1)} collective-permute-done((bf16[8,3584]{1,0:T(8,128)(2,1)S(1)}, bf16[8,3584]{1,0:T(8,128)(2,1)S(1)}, u32[]{:S(2)}, u32[]{:S(2)}) %collective-permute-start.2) | collective-permute-done | bytes 57376 | tf_op jit(solution)/shard_map/ppermute | solution.py:147
  16.0 0.7 %shard_map.85 = (f32[4,16,1792]{2,1,0:T(8,128)S(1)}, bf16[4,16,1792]{2,1,0:T(8,128)(2,1)S(1)}) custom-call(bf16[8,3584]{1,0:T(8,128)(2,1)S(1)} %get-tuple-element.17.refs_0_, bf16[8,3584]{1,0:T(8,128)(2,1)S(1)} %collective-permute-done.refs_1_, bf16[8,3584]{1,0:T(8,128)(2,1)S(1)} %collective-permute-done.1.refs_2_, ...), custom_call_target="tpu_custom_call" | custom-call | flops 1000000 | bytes 2000 | tf_op jit(solution)/shard_map/pallas_call | solution.py:137
  16.7 1.5 %collective-permute-done.7.got_ref = bf16[4,16,1792]{2,1,0:T(8,128)(2,1)S(1)} collective-permute-done((bf16[4,16,1792]{2,1,0:T(8,128)(2,1)S(1)}, bf16[4,16,1792]{2,1,0:T(8,128)(2,1)S(1)}, u32[]{:S(2)}, u32[]{:S(2)}) %collective-permute-start.7) | collective-permute-done | bytes 229408 | tf_op jit(solution)/shard_map/ppermute | solution.py:190
  18.3 0.7 %collective-permute-start.11 = (bf16[8,1792]{1,0:T(8,128)(2,1)S(1)}, bf16[8,1792]{1,0:T(8,128)(2,1)S(1)}, u32[]{:S(2)}, u32[]{:S(2)}) collective-permute-start(bf16[8,1792]{1,0:T(8,128)(2,1)S(1)} %get-tuple-element.26), channel_id=1, source_target_pairs={{0,2},{2,0},{4,6},{6,4},{8,10},{10,8},{12,14},{14,12},{1,3},{3,1},... | collective-permute-start | bytes 86024 | tf_op jit(solution)/shard_map/ppermute | solution.py:147
  18.9 1.5 %collective-permute-start.12 = (bf16[8,1792]{1,0:T(8,128)(2,1)S(1)}, bf16[8,1792]{1,0:T(8,128)(2,1)S(1)}, u32[]{:S(2)}, u32[]{:S(2)}) collective-permute-start(bf16[8,1792]{1,0:T(8,128)(2,1)S(1)} %get-tuple-element.27), channel_id=1, source_target_pairs={{0,4},{2,6},{4,0},{6,2},{8,12},{10,14},{12,8},{14,10},{1,5},{3,7},... | collective-permute-start | bytes 86024 | tf_op jit(solution)/shard_map/ppermute | solution.py:147
  20.4 1.4 %collective-permute-start.13 = (bf16[8,1792]{1,0:T(8,128)(2,1)S(1)}, bf16[8,1792]{1,0:T(8,128)(2,1)S(1)}, u32[]{:S(2)}, u32[]{:S(2)}) collective-permute-start(bf16[8,1792]{1,0:T(8,128)(2,1)S(1)} %get-tuple-element.28), channel_id=1, source_target_pairs={{0,6},{2,4},{4,2},{6,0},{8,14},{10,12},{12,10},{14,8},{1,7},{3,5},... | collective-permute-start | bytes 86024 | tf_op jit(solution)/shard_map/ppermute | solution.py:147
  21.8 0.6 %collective-permute-start.8 = (bf16[8,1792]{1,0:T(8,128)(2,1)S(1)}, bf16[8,1792]{1,0:T(8,128)(2,1)S(1)}, u32[]{:S(2)}, u32[]{:S(2)}) collective-permute-start(bf16[8,1792]{1,0:T(8,128)(2,1)S(1)} %get-tuple-element.22), channel_id=1, source_target_pairs={{0,2},{2,0},{4,6},{6,4},{8,10},{10,8},{12,14},{14,12},{1,3},{3,1},... | collective-permute-start | bytes 86024 | tf_op jit(solution)/shard_map/ppermute | solution.py:147
  22.4 1.5 %collective-permute-start.9 = (bf16[8,1792]{1,0:T(8,128)(2,1)S(1)}, bf16[8,1792]{1,0:T(8,128)(2,1)S(1)}, u32[]{:S(2)}, u32[]{:S(2)}) collective-permute-start(bf16[8,1792]{1,0:T(8,128)(2,1)S(1)} %get-tuple-element.23), channel_id=1, source_target_pairs={{0,4},{2,6},{4,0},{6,2},{8,12},{10,14},{12,8},{14,10},{1,5},{3,7},... | collective-permute-start | bytes 86024 | tf_op jit(solution)/shard_map/ppermute | solution.py:147
  23.9 1.4 %collective-permute-start.10 = (bf16[8,1792]{1,0:T(8,128)(2,1)S(1)}, bf16[8,1792]{1,0:T(8,128)(2,1)S(1)}, u32[]{:S(2)}, u32[]{:S(2)}) collective-permute-start(bf16[8,1792]{1,0:T(8,128)(2,1)S(1)} %get-tuple-element.24), channel_id=1, source_target_pairs={{0,6},{2,4},{4,2},{6,0},{8,14},{10,12},{12,10},{14,8},{1,7},{3,5},... | collective-permute-start | bytes 86024 | tf_op jit(solution)/shard_map/ppermute | solution.py:147
  25.6 2.0 %collective-permute-start.14 = (bf16[8,1792]{1,0:T(8,128)(2,1)S(1)}, bf16[8,1792]{1,0:T(8,128)(2,1)S(1)}, u32[]{:S(2)}, u32[]{:S(2)}) collective-permute-start(bf16[8,1792]{1,0:T(8,128)(2,1)S(1)} %shard_map.88), channel_id=1, source_target_pairs={{0,8},{2,10},{4,12},{6,14},{8,0},{10,2},{12,4},{14,6},{1,9},{3,11}... | collective-permute-start | bytes 86024 | tf_op jit(solution)/shard_map/ppermute | solution.py:154
  27.8 1.0 %collective-permute-done.10.refs_3_ = bf16[8,1792]{1,0:T(8,128)(2,1)S(1)} collective-permute-done((bf16[8,1792]{1,0:T(8,128)(2,1)S(1)}, bf16[8,1792]{1,0:T(8,128)(2,1)S(1)}, u32[]{:S(2)}, u32[]{:S(2)}) %collective-permute-start.10) | collective-permute-done | bytes 28704 | tf_op jit(solution)/shard_map/ppermute | solution.py:147
  28.9 1.6 %collective-permute-done.14.rest_ref = bf16[8,1792]{1,0:T(8,128)(2,1)S(1)} collective-permute-done((bf16[8,1792]{1,0:T(8,128)(2,1)S(1)}, bf16[8,1792]{1,0:T(8,128)(2,1)S(1)}, u32[]{:S(2)}, u32[]{:S(2)}) %collective-permute-start.14) | collective-permute-done | bytes 28704 | tf_op jit(solution)/shard_map/ppermute | solution.py:154
  30.5 0.7 %shard_map.89 = bf16[2,8,1792]{2,1,0:T(8,128)(2,1)} custom-call(f32[2,8,1792]{2,1,0:T(8,128)S(1)} %shard_map.87.base_ref, f32[2,8,16]{2,1,0:T(8,128)S(1)} %shard_map.83.weights_ref, bf16[8,1792]{1,0:T(8,128)(2,1)S(1)} %collective-permute-done.14.rest_ref), custom_call_target="tpu_custom_call" | custom-call | tf_op jit(solution)/shard_map/pallas_call | solution.py:137
  (30 shorter events, 0.8 us)
Async XLA Ops:
  0.0 0.9 %copy-start.3 = (bf16[2,8,3584]{2,1,0:T(8,128)(2,1)S(1)}, bf16[2,8,3584]{2,1,0:T(8,128)(2,1)}, u32[]{:S(2)}) copy-start(bf16[2,8,3584]{2,1,0:T(8,128)(2,1)} %hidden_ref.3) | copy-start | bytes 344068
  0.0 0.9 %copy-start.7 = (bf16[3584]{0:T(1024)(128)(2,1)S(1)}, bf16[3584]{0:T(1024)(128)(2,1)}, u32[]{:S(2)}) copy-start(bf16[3584]{0:T(1024)(128)(2,1)} %gain_ref.1) | copy-start | bytes 21508
  0.0 0.9 %copy-start.5 = (s32[2,8,1]{1,2,0:T(1,128)S(1)}, s32[2,8,1]{1,2,0:T(1,128)}, u32[]{:S(2)}) copy-start(s32[2,8,1]{1,2,0:T(1,128)} %param.12) | copy-start | bytes 196
  0.0 0.9 %copy-start.4 = (s32[2,8,1]{1,2,0:T(1,128)S(1)}, s32[2,8,1]{1,2,0:T(1,128)}, u32[]{:S(2)}) copy-start(s32[2,8,1]{1,2,0:T(1,128)} %param.10) | copy-start | bytes 196
  0.9 15.1 %copy-start = (bf16[3584,128]{1,0:T(8,128)(2,1)S(1)}, bf16[3584,128]{1,0:T(8,128)(2,1)}, u32[]{:S(2)}) copy-start(bf16[3584,128]{1,0:T(8,128)(2,1)} %refs_8_.1) | copy-start | bytes 2752516
  0.9 15.1 %copy-start.1 = (bf16[3584,128]{1,0:T(8,128)(2,1)S(1)}, bf16[3584,128]{1,0:T(8,128)(2,1)}, u32[]{:S(2)}) copy-start(bf16[3584,128]{1,0:T(8,128)(2,1)} %refs_9_.1) | copy-start | bytes 2752516
  0.9 15.1 %copy-start.2 = (bf16[128,3584]{1,0:T(8,128)(2,1)S(1)}, bf16[128,3584]{1,0:T(8,128)(2,1)}, u32[]{:S(2)}) copy-start(bf16[128,3584]{1,0:T(8,128)(2,1)} %refs_10_.1) | copy-start | bytes 2752516
  1.3 7.6 %collective-permute-start = (bf16[8,3584]{1,0:T(8,128)(2,1)S(1)}, bf16[8,3584]{1,0:T(8,128)(2,1)S(1)}, u32[]{:S(2)}, u32[]{:S(2)}) collective-permute-start(bf16[8,3584]{1,0:T(8,128)(2,1)S(1)} %get-tuple-element.18), channel_id=1, source_target_pairs={{0,8},{2,10},{4,12},{6,14},{8,0},{10,2},{12,4},{14,6},{1,9},{3,11}... | collective-permute-start | bytes 172040 | tf_op jit(solution)/shard_map/ppermute | solution.py:154
  5.4 6.5 %collective-permute-start.5 = (bf16[8,3584]{1,0:T(8,128)(2,1)S(1)}, bf16[8,3584]{1,0:T(8,128)(2,1)S(1)}, u32[]{:S(2)}, u32[]{:S(2)}) collective-permute-start(bf16[8,3584]{1,0:T(8,128)(2,1)S(1)} %get-tuple-element.17.refs_0_), channel_id=1, source_target_pairs={{0,6},{2,4},{4,2},{6,0},{8,14},{10,12},{12,10},{14,8},{1,7},{3,5},... | collective-permute-start | bytes 172040 | tf_op jit(solution)/shard_map/ppermute | solution.py:147
  7.9 4.6 %collective-permute-start.3 = (bf16[8,3584]{1,0:T(8,128)(2,1)S(1)}, bf16[8,3584]{1,0:T(8,128)(2,1)S(1)}, u32[]{:S(2)}, u32[]{:S(2)}) collective-permute-start(bf16[8,3584]{1,0:T(8,128)(2,1)S(1)} %get-tuple-element.17.refs_0_), channel_id=1, source_target_pairs={{0,4},{2,6},{4,0},{6,2},{8,12},{10,14},{12,8},{14,10},{1,5},{3,7},... | collective-permute-start | bytes 172040 | tf_op jit(solution)/shard_map/ppermute | solution.py:147
  8.3 4.2 %collective-permute-start.1 = (bf16[8,3584]{1,0:T(8,128)(2,1)S(1)}, bf16[8,3584]{1,0:T(8,128)(2,1)S(1)}, u32[]{:S(2)}, u32[]{:S(2)}) collective-permute-start(bf16[8,3584]{1,0:T(8,128)(2,1)S(1)} %get-tuple-element.17.refs_0_), channel_id=1, source_target_pairs={{0,2},{2,0},{4,6},{6,4},{8,10},{10,8},{12,14},{14,12},{1,3},{3,1},... | collective-permute-start | bytes 172040 | tf_op jit(solution)/shard_map/ppermute | solution.py:147
  8.8 5.1 %collective-permute-start.6 = (bf16[8,3584]{1,0:T(8,128)(2,1)S(1)}, bf16[8,3584]{1,0:T(8,128)(2,1)S(1)}, u32[]{:S(2)}, u32[]{:S(2)}) collective-permute-start(bf16[8,3584]{1,0:T(8,128)(2,1)S(1)} %collective-permute-done.refs_1_), channel_id=1, source_target_pairs={{0,6},{2,4},{4,2},{6,0},{8,14},{10,12},{12,10},{14,8},{1,7},{3,5},... | collective-permute-start | bytes 172040 | tf_op jit(solution)/shard_map/ppermute | solution.py:147
  11.4 4.2 %collective-permute-start.4 = (bf16[8,3584]{1,0:T(8,128)(2,1)S(1)}, bf16[8,3584]{1,0:T(8,128)(2,1)S(1)}, u32[]{:S(2)}, u32[]{:S(2)}) collective-permute-start(bf16[8,3584]{1,0:T(8,128)(2,1)S(1)} %collective-permute-done.refs_1_), channel_id=1, source_target_pairs={{0,4},{2,6},{4,0},{6,2},{8,12},{10,14},{12,8},{14,10},{1,5},{3,7},... | collective-permute-start | bytes 172040 | tf_op jit(solution)/shard_map/ppermute | solution.py:147
  11.8 4.2 %collective-permute-start.2 = (bf16[8,3584]{1,0:T(8,128)(2,1)S(1)}, bf16[8,3584]{1,0:T(8,128)(2,1)S(1)}, u32[]{:S(2)}, u32[]{:S(2)}) collective-permute-start(bf16[8,3584]{1,0:T(8,128)(2,1)S(1)} %collective-permute-done.refs_1_), channel_id=1, source_target_pairs={{0,2},{2,0},{4,6},{6,4},{8,10},{10,8},{12,14},{14,12},{1,3},{3,1},... | collective-permute-start | bytes 172040 | tf_op jit(solution)/shard_map/ppermute | solution.py:147
  16.7 1.6 %collective-permute-start.7 = (bf16[4,16,1792]{2,1,0:T(8,128)(2,1)S(1)}, bf16[4,16,1792]{2,1,0:T(8,128)(2,1)S(1)}, u32[]{:S(2)}, u32[]{:S(2)}) collective-permute-start(bf16[4,16,1792]{2,1,0:T(8,128)(2,1)S(1)} %get-tuple-element.20), channel_id=1, source_target_pairs={{0,1},{1,0},{2,3},{3,2},{4,5},{5,4},{6,7},{7,6},{8,9},{9,8},{10,11... | collective-permute-start | bytes 688136 | tf_op jit(solution)/shard_map/ppermute | solution.py:190
  18.3 5.7 %collective-permute-start.11 = (bf16[8,1792]{1,0:T(8,128)(2,1)S(1)}, bf16[8,1792]{1,0:T(8,128)(2,1)S(1)}, u32[]{:S(2)}, u32[]{:S(2)}) collective-permute-start(bf16[8,1792]{1,0:T(8,128)(2,1)S(1)} %get-tuple-element.26), channel_id=1, source_target_pairs={{0,2},{2,0},{4,6},{6,4},{8,10},{10,8},{12,14},{14,12},{1,3},{3,1},... | collective-permute-start | bytes 86024 | tf_op jit(solution)/shard_map/ppermute | solution.py:147
  18.9 6.4 %collective-permute-start.12 = (bf16[8,1792]{1,0:T(8,128)(2,1)S(1)}, bf16[8,1792]{1,0:T(8,128)(2,1)S(1)}, u32[]{:S(2)}, u32[]{:S(2)}) collective-permute-start(bf16[8,1792]{1,0:T(8,128)(2,1)S(1)} %get-tuple-element.27), channel_id=1, source_target_pairs={{0,4},{2,6},{4,0},{6,2},{8,12},{10,14},{12,8},{14,10},{1,5},{3,7},... | collective-permute-start | bytes 86024 | tf_op jit(solution)/shard_map/ppermute | solution.py:147
  20.4 5.2 %collective-permute-start.13 = (bf16[8,1792]{1,0:T(8,128)(2,1)S(1)}, bf16[8,1792]{1,0:T(8,128)(2,1)S(1)}, u32[]{:S(2)}, u32[]{:S(2)}) collective-permute-start(bf16[8,1792]{1,0:T(8,128)(2,1)S(1)} %get-tuple-element.28), channel_id=1, source_target_pairs={{0,6},{2,4},{4,2},{6,0},{8,14},{10,12},{12,10},{14,8},{1,7},{3,5},... | collective-permute-start | bytes 86024 | tf_op jit(solution)/shard_map/ppermute | solution.py:147
  21.8 5.9 %collective-permute-start.8 = (bf16[8,1792]{1,0:T(8,128)(2,1)S(1)}, bf16[8,1792]{1,0:T(8,128)(2,1)S(1)}, u32[]{:S(2)}, u32[]{:S(2)}) collective-permute-start(bf16[8,1792]{1,0:T(8,128)(2,1)S(1)} %get-tuple-element.22), channel_id=1, source_target_pairs={{0,2},{2,0},{4,6},{6,4},{8,10},{10,8},{12,14},{14,12},{1,3},{3,1},... | collective-permute-start | bytes 86024 | tf_op jit(solution)/shard_map/ppermute | solution.py:147
  22.4 5.3 %collective-permute-start.9 = (bf16[8,1792]{1,0:T(8,128)(2,1)S(1)}, bf16[8,1792]{1,0:T(8,128)(2,1)S(1)}, u32[]{:S(2)}, u32[]{:S(2)}) collective-permute-start(bf16[8,1792]{1,0:T(8,128)(2,1)S(1)} %get-tuple-element.23), channel_id=1, source_target_pairs={{0,4},{2,6},{4,0},{6,2},{8,12},{10,14},{12,8},{14,10},{1,5},{3,7},... | collective-permute-start | bytes 86024 | tf_op jit(solution)/shard_map/ppermute | solution.py:147
  23.9 4.9 %collective-permute-start.10 = (bf16[8,1792]{1,0:T(8,128)(2,1)S(1)}, bf16[8,1792]{1,0:T(8,128)(2,1)S(1)}, u32[]{:S(2)}, u32[]{:S(2)}) collective-permute-start(bf16[8,1792]{1,0:T(8,128)(2,1)S(1)} %get-tuple-element.24), channel_id=1, source_target_pairs={{0,6},{2,4},{4,2},{6,0},{8,14},{10,12},{12,10},{14,8},{1,7},{3,5},... | collective-permute-start | bytes 86024 | tf_op jit(solution)/shard_map/ppermute | solution.py:147
  25.6 2.1 %copy-start.6 = (f32[2,8,1]{1,2,0:T(1,128)S(1)}, f32[2,8,1]{1,2,0:T(1,128)}, u32[]{:S(2)}) copy-start(f32[2,8,1]{1,2,0:T(1,128)} %param.11) | copy-start | bytes 196
  25.6 4.8 %collective-permute-start.14 = (bf16[8,1792]{1,0:T(8,128)(2,1)S(1)}, bf16[8,1792]{1,0:T(8,128)(2,1)S(1)}, u32[]{:S(2)}, u32[]{:S(2)}) collective-permute-start(bf16[8,1792]{1,0:T(8,128)(2,1)S(1)} %shard_map.88), channel_id=1, source_target_pairs={{0,8},{2,10},{4,12},{6,14},{8,0},{10,2},{12,4},{14,6},{1,9},{3,11}... | collective-permute-start | bytes 86024 | tf_op jit(solution)/shard_map/ppermute | solution.py:154

commit v4 on v3

--- a/solution.py
+++ b/solution.py
@@ -116,6 +116,80 @@
         )
 
 
+def own_or_rest(own, rest):
+    return jnp.where(lax.axis_index("tp") == 0, own, rest)
+
+
+def choose_kernel(own_ref, rest_ref, out_ref):
+    out_ref[...] = own_or_rest(own_ref[...].astype(F32), rest_ref[...].astype(F32)).astype(BF16)
+
+
+def pack_kernel(*refs):
+    refs[-1][...] = jnp.concatenate([ref[...].astype(F32) for ref in refs[:-1]], 0).astype(BF16)
+
+
+def shared_expert_kernel(
+    mine_ref, other_ref, gate_ref, up_ref, down_ref, keep_ref, send_ref
+):
+    count = mine_ref.shape[0]
+    rows = jnp.concatenate([mine_ref[...].astype(F32), other_ref[...].astype(F32)], 0).astype(BF16)
+    gate_val = jnp.dot(rows, gate_ref[...], preferred_element_type=F32)
+    up_val = jnp.dot(rows, up_ref[...], preferred_element_type=F32)
+    active = (gate_val / (1.0 + jnp.exp(-gate_val)) * up_val).astype(BF16)
+    partial_value = jnp.dot(active, down_ref[...], preferred_element_type=F32)
+    keep_ref[...] = partial_value[:count]
+    send_ref[...] = partial_value[count:].astype(BF16)
+
+
+def split_members_kernel(keep_ref, got_ref, *out_refs):
+    total = keep_ref[...] + got_ref[...].astype(F32)
+    count = out_refs[0].shape[0]
+    for k, ref in enumerate(out_refs):
+        ref[...] = total[k * count : (k + 1) * count].astype(ref.dtype)
+
+
+def gather_members_kernel(*refs):
+    total = refs[0][...]
+    for ref in refs[1:-2]:
+        total = total + ref[...].astype(F32)
+    refs[-2][...] = total
+    refs[-1][...] = total.astype(BF16)
+
+
+def halves_kernel(own_ref, rest_ref, keep_ref, send_ref):
+    core = lax.axis_index("tp")
+    half = keep_ref.shape[1]
+
+    def columns(which):
+        block = pl.ds(pl.multiple_of(which * half, 128), half)
+        return own_or_rest(own_ref[:, block], rest_ref[:, block].astype(F32))
+
+    keep_ref[...] = columns(core)
+    send_ref[...] = columns(1 - core).astype(BF16)
+
+
+def kind_weights(table_ref, micro_batch, other, count):
+    table = table_ref[micro_batch]
+    own, rest = table[:, :count], table[:, count:]
+    return own_or_rest(rest, own) if other else own_or_rest(own, rest)
+
+
+def mine_kernel(sizes, hidden_ref, table_ref, mine_ref, out_ref):
+    mine = mine_ref[...]
+    count, half = mine.shape
+    columns = pl.ds(pl.multiple_of(lax.axis_index("tp") * half, 128), half)
+    for m in range(hidden_ref.shape[0]):
+        base = hidden_ref[m, :, columns].astype(F32)
+        out_ref[m] = weighted(base, kind_weights(table_ref, m, False, count), mine, sizes, m, 0, 1)
+
+
+def other_kernel(sizes, base_ref, table_ref, other_ref, out_ref):
+    other = other_ref[...].astype(F32)
+    for m in range(base_ref.shape[0]):
+        weights = kind_weights(table_ref, m, True, other.shape[0])
+        out_ref[m] = weighted(base_ref[m], weights, other, sizes, m, 0, 1).astype(BF16)
+
+
 def per_device(hidden, norm_gain, expert_ids, shares, slot_index, w_gate, w_up, w_down):
     micro_count, row_count, model_width = hidden.shape
     top_count = expert_ids.shape[2]
@@ -174,6 +248,47 @@
         weights,
     )
     members = range(1, node_size)
+    rows = (micro_count, row_count, half)
+    swap = [(i, (i + 1) % share_count) for i in range(share_count)]
+    if nodes == 2 and share_count == 2:
+        full = (per_node, model_width)
+
+        def to_other_node(array):
+            pairs = [(2 * j + 1, 2 * ((j + node_size) % ep_count) + 1) for j in range(ep_count)]
+            return lax.ppermute(array, ("ep", "tp"), pairs)
+
+        inbox = to_other_node(rest)
+        (mine,) = call(choose_kernel, [(full, BF16)], own, inbox)
+        pieces = [mine] + [to_member(mine, k) for k in members]
+        packed_shape = (node_size * per_node, model_width)
+        (packed,) = call(pack_kernel, [(packed_shape, BF16)], *pieces)
+        other = lax.ppermute(packed, "tp", swap)
+        keep, send = call(
+            shared_expert_kernel,
+            [(packed_shape, F32), (packed_shape, BF16)],
+            packed,
+            other,
+            w_gate,
+            w_up,
+            w_down,
+        )
+        got = lax.ppermute(send, "tp", swap)
+        sums = call(
+            split_members_kernel,
+            [(full, F32)] + [(full, BF16)] * (node_size - 1),
+            keep,
+            got,
+        )
+        arrived = [to_member(sums[k], k) for k in members]
+        total, outbox = call(gather_members_kernel, [(full, F32), (full, BF16)], sums[0], *arrived)
+        returned = to_other_node(outbox)
+        narrow = (per_node, half)
+        keep, send = call(halves_kernel, [(narrow, F32), (narrow, BF16)], total, returned)
+        other = lax.ppermute(send, "tp", swap)
+        (base,) = call(functools.partial(mine_kernel, sizes), [(rows, F32)], hidden, table, keep)
+        (mixed,) = call(functools.partial(other_kernel, sizes), [(rows, BF16)], base, table, other)
+        return mixed
+
     inbox = to_nodes(rest, 1)
     owns = [own] + [to_member(own, k) for k in members]
     rests = [inbox] + [to_member(inbox, k) for k in members]
@@ -187,7 +302,7 @@
         w_down,
         cost=10**6,
     )
-    got = lax.ppermute(send, "tp", [(i, (i + 1) % share_count) for i in range(share_count)])
+    got = lax.ppermute(send, "tp", swap)
     sums = call(
         add_cores_kernel,
         [
@@ -202,7 +317,6 @@
     home = [sums[0]] + [to_member(sums[2 * k], k) for k in members]
     (outbox,) = call(add_members_kernel, [((rest_rows, half), BF16)], *away)
     returned = to_nodes(outbox, -1)
-    rows = (micro_count, row_count, half)
     (base,) = call(functools.partial(own_kernel, sizes), [(rows, F32)], hidden, table, *home)
     (mixed,) = call(functools.partial(rest_kernel, sizes), [(rows, BF16)], base, table, returned)
     return mixed

time: 31.3 us -> 32.1 us (1.026)
  waiting for transfers between devices: 7.93 us -> 10.8 us
  starting transfers between devices: 20.3 us -> 17.9 us
    ppermute x12 -> x6, starting transfers between devices: 14.1 us -> 8.23 us  [to_member(): return lax.ppermute(array, 'ep', pairs)]
    ppermute x3 -> x5, starting transfers between devices: 6.21 us -> 9.7 us  [the longest x1 3.96 us: per_device(): other = lax.ppermute(packed, 'tp', swap)]
    ppermute x12 -> x6, waiting for transfers between devices: 4.89 us -> 7.93 us  [to_member(): return lax.ppermute(array, 'ep', pairs)]
    ppermute x3 -> x5, waiting for transfers between devices: 3.04 us -> 2.83 us  [the longest x1 1.12 us: per_device(): got = lax.ppermute(send, 'tp', swap)]
    pallas_call x8 -> x11, Pallas kernels: 1.97 us -> 2.18 us  [call(): pl.pallas_call(kernel, out_shape=[jax.ShapeDtypeStruct(shape, kind) for s...]
  transfers between devices with their start and end apart: 15 -> 11, of which waited for: 8 -> 9; matrix products, arithmetic and copies ran while one was open for 0% -> 0% of each run, Pallas kernels for 1% -> 1%
where the time goes in v4:
time: 32.1 us; the launch traced here: 31.9 us
  starting transfers between devices  17.9 us (56%)
  waiting for transfers between devices  10.8 us (34%)
  Pallas kernels  2.18 us (7%)
  local copies, waits for them, and re-layouts  0.91 us (3%)
    ppermute x6, starting transfers between devices, to_member(): return lax.ppermute(array, 'ep', pairs)  8.23 us
    ppermute x6, waiting for transfers between devices, to_member(): return lax.ppermute(array, 'ep', pairs)  7.93 us
    ppermute x1, starting transfers between devices, per_device(): other = lax.ppermute(packed, 'tp', swap)  3.96 us
    ppermute x1, starting transfers between devices, per_device(): other = lax.ppermute(send, 'tp', swap)  3.84 us
    pallas_call x11, Pallas kernels, call(): pl.pallas_call(kernel, out_shape=[jax.ShapeDtypeStruct(shape, kind) for s...  2.18 us
    ppermute x2, starting transfers between devices, to_other_node(): return lax.ppermute(array, ('ep', 'tp'), pairs)  1.46 us
    ppermute x1, waiting for transfers between devices, per_device(): got = lax.ppermute(send, 'tp', swap)  1.12 us
    ppermute x1, waiting for transfers between devices, per_device(): other = lax.ppermute(packed, 'tp', swap)  1.12 us
  transfers between devices with their start and end apart: 11, of which 9 were waited for; matrix products, arithmetic and copies ran while one was open for 0% of the time, Pallas kernels for 1%

profile of v4, /device:TPU:0, one launch (start us, length us, event | category | flops | bytes accessed | tf_op | source)
XLA Modules:
  0.0 31.9 jit_solution(12620780941411925298)
XLA Ops:
  0.0 0.9 %copy-done.3 = bf16[2,8,3584]{2,1,0:T(8,128)(2,1)S(1)} copy-done((bf16[2,8,3584]{2,1,0:T(8,128)(2,1)S(1)}, bf16[2,8,3584]{2,1,0:T(8,128)(2,1)}, u32[]{:S(2)}) %copy-start.3) | copy-done | bytes 114712
  0.9 0.3 shard_map.84
  1.3 0.8 %collective-permute-start = (bf16[8,3584]{1,0:T(8,128)(2,1)S(1)}, bf16[8,3584]{1,0:T(8,128)(2,1)S(1)}, u32[]{:S(2)}, u32[]{:S(2)}) collective-permute-start(bf16[8,3584]{1,0:T(8,128)(2,1)S(1)} %get-tuple-element.18), channel_id=1, source_target_pairs={{1,9},{3,11},{5,13},{7,15},{9,1},{11,3},{13,5},{15,7},{17,25},{19,... | collective-permute-start | bytes 172040 | tf_op jit(solution)/shard_map/ppermute | solution.py:258
  2.1 4.0 %collective-permute-start.3 = (bf16[8,3584]{1,0:T(8,128)(2,1)S(1)}, bf16[8,3584]{1,0:T(8,128)(2,1)S(1)}, u32[]{:S(2)}, u32[]{:S(2)}) collective-permute-start(bf16[8,3584]{1,0:T(8,128)(2,1)S(1)} %shard_map.85.refs_0_), channel_id=1, source_target_pairs={{0,6},{2,4},{4,2},{6,0},{8,14},{10,12},{12,10},{14,8},{1,7},{3,5},... | collective-permute-start | bytes 172040 | tf_op jit(solution)/shard_map/ppermute | solution.py:221
  6.1 0.4 %collective-permute-start.2 = (bf16[8,3584]{1,0:T(8,128)(2,1)S(1)}, bf16[8,3584]{1,0:T(8,128)(2,1)S(1)}, u32[]{:S(2)}, u32[]{:S(2)}) collective-permute-start(bf16[8,3584]{1,0:T(8,128)(2,1)S(1)} %shard_map.85.refs_0_), channel_id=1, source_target_pairs={{0,4},{2,6},{4,0},{6,2},{8,12},{10,14},{12,8},{14,10},{1,5},{3,7},... | collective-permute-start | bytes 172040 | tf_op jit(solution)/shard_map/ppermute | solution.py:221
  6.6 0.2 collective-permute-start.1
  6.8 1.6 %collective-permute-done.3.refs_3_ = bf16[8,3584]{1,0:T(8,128)(2,1)S(1)} collective-permute-done((bf16[8,3584]{1,0:T(8,128)(2,1)S(1)}, bf16[8,3584]{1,0:T(8,128)(2,1)S(1)}, u32[]{:S(2)}, u32[]{:S(2)}) %collective-permute-start.3) | collective-permute-done | bytes 57376 | tf_op jit(solution)/shard_map/ppermute | solution.py:221
  8.4 1.9 %collective-permute-done.2.refs_2_ = bf16[8,3584]{1,0:T(8,128)(2,1)S(1)} collective-permute-done((bf16[8,3584]{1,0:T(8,128)(2,1)S(1)}, bf16[8,3584]{1,0:T(8,128)(2,1)S(1)}, u32[]{:S(2)}, u32[]{:S(2)}) %collective-permute-start.2) | collective-permute-done | bytes 57376 | tf_op jit(solution)/shard_map/ppermute | solution.py:221
  10.3 0.4 %collective-permute-done.1.refs_1_ = bf16[8,3584]{1,0:T(8,128)(2,1)S(1)} collective-permute-done((bf16[8,3584]{1,0:T(8,128)(2,1)S(1)}, bf16[8,3584]{1,0:T(8,128)(2,1)S(1)}, u32[]{:S(2)}, u32[]{:S(2)}) %collective-permute-start.1) | collective-permute-done | bytes 57376 | tf_op jit(solution)/shard_map/ppermute | solution.py:221
  10.8 4.0 %collective-permute-start.4 = (bf16[32,3584]{1,0:T(8,128)(2,1)S(1)}, bf16[32,3584]{1,0:T(8,128)(2,1)S(1)}, u32[]{:S(2)}, u32[]{:S(2)}) collective-permute-start(bf16[32,3584]{1,0:T(8,128)(2,1)S(1)} %shard_map.86.mine_ref), channel_id=1, source_target_pairs={{0,1},{1,0},{2,3},{3,2},{4,5},{5,4},{6,7},{7,6},{8,9},{9,8},{10,11... | collective-permute-start | bytes 688136 | tf_op jit(solution)/shard_map/ppermute | solution.py:265
  14.7 1.1 %collective-permute-done.4.other_ref = bf16[32,3584]{1,0:T(8,128)(2,1)S(1)} collective-permute-done((bf16[32,3584]{1,0:T(8,128)(2,1)S(1)}, bf16[32,3584]{1,0:T(8,128)(2,1)S(1)}, u32[]{:S(2)}, u32[]{:S(2)}) %collective-permute-start.4) | collective-permute-done | bytes 229408 | tf_op jit(solution)/shard_map/ppermute | solution.py:265
  15.8 0.7 %shard_map.87 = (f32[32,3584]{1,0:T(8,128)S(1)}, bf16[32,3584]{1,0:T(8,128)(2,1)S(1)}) custom-call(bf16[32,3584]{1,0:T(8,128)(2,1)S(1)} %shard_map.86.mine_ref, bf16[32,3584]{1,0:T(8,128)(2,1)S(1)} %collective-permute-done.4.other_ref, bf16[3584,128]{1,0:T(8,128)(2,1)S(1)} %copy-done, bf16[3584,128]{1,0:T(8,128)(2,1)S(1)} %copy-done.1, ...), custom_call_target="tpu_custom_call" | custom-call | tf_op jit(solution)/shard_map/pallas_call | solution.py:211
  16.5 0.4 %collective-permute-start.5 = (bf16[32,3584]{1,0:T(8,128)(2,1)S(1)}, bf16[32,3584]{1,0:T(8,128)(2,1)S(1)}, u32[]{:S(2)}, u32[]{:S(2)}) collective-permute-start(bf16[32,3584]{1,0:T(8,128)(2,1)S(1)} %get-tuple-element.20), channel_id=1, source_target_pairs={{0,1},{1,0},{2,3},{3,2},{4,5},{5,4},{6,7},{7,6},{8,9},{9,8},{10,11... | collective-permute-start | bytes 688136 | tf_op jit(solution)/shard_map/ppermute | solution.py:275
  17.0 1.1 %collective-permute-done.5.got_ref = bf16[32,3584]{1,0:T(8,128)(2,1)S(1)} collective-permute-done((bf16[32,3584]{1,0:T(8,128)(2,1)S(1)}, bf16[32,3584]{1,0:T(8,128)(2,1)S(1)}, u32[]{:S(2)}, u32[]{:S(2)}) %collective-permute-start.5) | collective-permute-done | bytes 229408 | tf_op jit(solution)/shard_map/ppermute | solution.py:275
  18.1 0.7 %collective-permute-start.6 = (bf16[8,3584]{1,0:T(8,128)(2,1)S(1)}, bf16[8,3584]{1,0:T(8,128)(2,1)S(1)}, u32[]{:S(2)}, u32[]{:S(2)}) collective-permute-start(bf16[8,3584]{1,0:T(8,128)(2,1)S(1)} %get-tuple-element.22), channel_id=1, source_target_pairs={{0,2},{2,0},{4,6},{6,4},{8,10},{10,8},{12,14},{14,12},{1,3},{3,1},... | collective-permute-start | bytes 172040 | tf_op jit(solution)/shard_map/ppermute | solution.py:221
  18.8 1.7 %collective-permute-start.7 = (bf16[8,3584]{1,0:T(8,128)(2,1)S(1)}, bf16[8,3584]{1,0:T(8,128)(2,1)S(1)}, u32[]{:S(2)}, u32[]{:S(2)}) collective-permute-start(bf16[8,3584]{1,0:T(8,128)(2,1)S(1)} %get-tuple-element.23), channel_id=1, source_target_pairs={{0,4},{2,6},{4,0},{6,2},{8,12},{10,14},{12,8},{14,10},{1,5},{3,7},... | collective-permute-start | bytes 172040 | tf_op jit(solution)/shard_map/ppermute | solution.py:221
  20.6 1.1 %collective-permute-start.8 = (bf16[8,3584]{1,0:T(8,128)(2,1)S(1)}, bf16[8,3584]{1,0:T(8,128)(2,1)S(1)}, u32[]{:S(2)}, u32[]{:S(2)}) collective-permute-start(bf16[8,3584]{1,0:T(8,128)(2,1)S(1)} %get-tuple-element.24), channel_id=1, source_target_pairs={{0,6},{2,4},{4,2},{6,0},{8,14},{10,12},{12,10},{14,8},{1,7},{3,5},... | collective-permute-start | bytes 172040 | tf_op jit(solution)/shard_map/ppermute | solution.py:221
  21.7 0.7 %collective-permute-done.6.refs_1_ = bf16[8,3584]{1,0:T(8,128)(2,1)S(1)} collective-permute-done((bf16[8,3584]{1,0:T(8,128)(2,1)S(1)}, bf16[8,3584]{1,0:T(8,128)(2,1)S(1)}, u32[]{:S(2)}, u32[]{:S(2)}) %collective-permute-start.6) | collective-permute-done | bytes 57376 | tf_op jit(solution)/shard_map/ppermute | solution.py:221
  22.4 0.6 %collective-permute-done.7.refs_2_ = bf16[8,3584]{1,0:T(8,128)(2,1)S(1)} collective-permute-done((bf16[8,3584]{1,0:T(8,128)(2,1)S(1)}, bf16[8,3584]{1,0:T(8,128)(2,1)S(1)}, u32[]{:S(2)}, u32[]{:S(2)}) %collective-permute-start.7) | collective-permute-done | bytes 57376 | tf_op jit(solution)/shard_map/ppermute | solution.py:221
  23.0 2.6 %collective-permute-done.8.refs_3_ = bf16[8,3584]{1,0:T(8,128)(2,1)S(1)} collective-permute-done((bf16[8,3584]{1,0:T(8,128)(2,1)S(1)}, bf16[8,3584]{1,0:T(8,128)(2,1)S(1)}, u32[]{:S(2)}, u32[]{:S(2)}) %collective-permute-start.8) | collective-permute-done | bytes 57376 | tf_op jit(solution)/shard_map/ppermute | solution.py:221
  25.7 0.7 %collective-permute-start.9 = (bf16[8,3584]{1,0:T(8,128)(2,1)S(1)}, bf16[8,3584]{1,0:T(8,128)(2,1)S(1)}, u32[]{:S(2)}, u32[]{:S(2)}) collective-permute-start(bf16[8,3584]{1,0:T(8,128)(2,1)S(1)} %get-tuple-element.26), channel_id=1, source_target_pairs={{1,9},{3,11},{5,13},{7,15},{9,1},{11,3},{13,5},{15,7},{17,25},{19,... | collective-permute-start | bytes 172040 | tf_op jit(solution)/shard_map/ppermute | solution.py:258
  26.4 3.8 %collective-permute-start.10 = (bf16[8,1792]{1,0:T(8,128)(2,1)S(1)}, bf16[8,1792]{1,0:T(8,128)(2,1)S(1)}, u32[]{:S(2)}, u32[]{:S(2)}) collective-permute-start(bf16[8,1792]{1,0:T(8,128)(2,1)S(1)} %get-tuple-element.28), channel_id=1, source_target_pairs={{0,1},{1,0},{2,3},{3,2},{4,5},{5,4},{6,7},{7,6},{8,9},{9,8},{10,11... | collective-permute-start | bytes 86024 | tf_op jit(solution)/shard_map/ppermute | solution.py:287
  30.5 0.6 %collective-permute-done.10.other_ref = bf16[8,1792]{1,0:T(8,128)(2,1)S(1)} collective-permute-done((bf16[8,1792]{1,0:T(8,128)(2,1)S(1)}, bf16[8,1792]{1,0:T(8,128)(2,1)S(1)}, u32[]{:S(2)}, u32[]{:S(2)}) %collective-permute-start.10) | collective-permute-done | bytes 28704 | tf_op jit(solution)/shard_map/ppermute | solution.py:287
  31.1 0.8 %shard_map.92 = bf16[2,8,1792]{2,1,0:T(8,128)(2,1)} custom-call(f32[2,8,1792]{2,1,0:T(8,128)S(1)} %shard_map.91.base_ref, f32[2,8,16]{2,1,0:T(8,128)S(1)} %shard_map.83.table_ref, bf16[8,1792]{1,0:T(8,128)(2,1)S(1)} %collective-permute-done.10.other_ref), custom_call_target="tpu_custom_call" | custom-call | tf_op jit(solution)/shard_map/pallas_call | solution.py:211
  (25 shorter events, 0.4 us)
Async XLA Ops:
  0.0 0.9 %copy-start.3 = (bf16[2,8,3584]{2,1,0:T(8,128)(2,1)S(1)}, bf16[2,8,3584]{2,1,0:T(8,128)(2,1)}, u32[]{:S(2)}) copy-start(bf16[2,8,3584]{2,1,0:T(8,128)(2,1)} %hidden_ref.3) | copy-start | bytes 344068
  0.0 0.9 %copy-start.7 = (bf16[3584]{0:T(1024)(128)(2,1)S(1)}, bf16[3584]{0:T(1024)(128)(2,1)}, u32[]{:S(2)}) copy-start(bf16[3584]{0:T(1024)(128)(2,1)} %gain_ref.1) | copy-start | bytes 21508
  0.0 0.9 %copy-start.5 = (s32[2,8,1]{1,2,0:T(1,128)S(1)}, s32[2,8,1]{1,2,0:T(1,128)}, u32[]{:S(2)}) copy-start(s32[2,8,1]{1,2,0:T(1,128)} %param.12) | copy-start | bytes 196
  0.0 0.9 %copy-start.4 = (s32[2,8,1]{1,2,0:T(1,128)S(1)}, s32[2,8,1]{1,2,0:T(1,128)}, u32[]{:S(2)}) copy-start(s32[2,8,1]{1,2,0:T(1,128)} %param.10) | copy-start | bytes 196
  0.9 14.9 %copy-start = (bf16[3584,128]{1,0:T(8,128)(2,1)S(1)}, bf16[3584,128]{1,0:T(8,128)(2,1)}, u32[]{:S(2)}) copy-start(bf16[3584,128]{1,0:T(8,128)(2,1)} %gate_ref.1) | copy-start | bytes 2752516
  0.9 14.9 %copy-start.1 = (bf16[3584,128]{1,0:T(8,128)(2,1)S(1)}, bf16[3584,128]{1,0:T(8,128)(2,1)}, u32[]{:S(2)}) copy-start(bf16[3584,128]{1,0:T(8,128)(2,1)} %up_ref.1) | copy-start | bytes 2752516
  0.9 14.9 %copy-start.2 = (bf16[128,3584]{1,0:T(8,128)(2,1)S(1)}, bf16[128,3584]{1,0:T(8,128)(2,1)}, u32[]{:S(2)}) copy-start(bf16[128,3584]{1,0:T(8,128)(2,1)} %down_ref.1) | copy-start | bytes 2752516
  1.3 0.8 %collective-permute-start = (bf16[8,3584]{1,0:T(8,128)(2,1)S(1)}, bf16[8,3584]{1,0:T(8,128)(2,1)S(1)}, u32[]{:S(2)}, u32[]{:S(2)}) collective-permute-start(bf16[8,3584]{1,0:T(8,128)(2,1)S(1)} %get-tuple-element.18), channel_id=1, source_target_pairs={{1,9},{3,11},{5,13},{7,15},{9,1},{11,3},{13,5},{15,7},{17,25},{19,... | collective-permute-start | bytes 172040 | tf_op jit(solution)/shard_map/ppermute | solution.py:258
  2.1 6.3 %collective-permute-start.3 = (bf16[8,3584]{1,0:T(8,128)(2,1)S(1)}, bf16[8,3584]{1,0:T(8,128)(2,1)S(1)}, u32[]{:S(2)}, u32[]{:S(2)}) collective-permute-start(bf16[8,3584]{1,0:T(8,128)(2,1)S(1)} %shard_map.85.refs_0_), channel_id=1, source_target_pairs={{0,6},{2,4},{4,2},{6,0},{8,14},{10,12},{12,10},{14,8},{1,7},{3,5},... | collective-permute-start | bytes 172040 | tf_op jit(solution)/shard_map/ppermute | solution.py:221
  6.1 4.2 %collective-permute-start.2 = (bf16[8,3584]{1,0:T(8,128)(2,1)S(1)}, bf16[8,3584]{1,0:T(8,128)(2,1)S(1)}, u32[]{:S(2)}, u32[]{:S(2)}) collective-permute-start(bf16[8,3584]{1,0:T(8,128)(2,1)S(1)} %shard_map.85.refs_0_), channel_id=1, source_target_pairs={{0,4},{2,6},{4,0},{6,2},{8,12},{10,14},{12,8},{14,10},{1,5},{3,7},... | collective-permute-start | bytes 172040 | tf_op jit(solution)/shard_map/ppermute | solution.py:221
  6.6 4.2 %collective-permute-start.1 = (bf16[8,3584]{1,0:T(8,128)(2,1)S(1)}, bf16[8,3584]{1,0:T(8,128)(2,1)S(1)}, u32[]{:S(2)}, u32[]{:S(2)}) collective-permute-start(bf16[8,3584]{1,0:T(8,128)(2,1)S(1)} %shard_map.85.refs_0_), channel_id=1, source_target_pairs={{0,2},{2,0},{4,6},{6,4},{8,10},{10,8},{12,14},{14,12},{1,3},{3,1},... | collective-permute-start | bytes 172040 | tf_op jit(solution)/shard_map/ppermute | solution.py:221
  10.8 5.1 %collective-permute-start.4 = (bf16[32,3584]{1,0:T(8,128)(2,1)S(1)}, bf16[32,3584]{1,0:T(8,128)(2,1)S(1)}, u32[]{:S(2)}, u32[]{:S(2)}) collective-permute-start(bf16[32,3584]{1,0:T(8,128)(2,1)S(1)} %shard_map.86.mine_ref), channel_id=1, source_target_pairs={{0,1},{1,0},{2,3},{3,2},{4,5},{5,4},{6,7},{7,6},{8,9},{9,8},{10,11... | collective-permute-start | bytes 688136 | tf_op jit(solution)/shard_map/ppermute | solution.py:265
  16.5 1.6 %collective-permute-start.5 = (bf16[32,3584]{1,0:T(8,128)(2,1)S(1)}, bf16[32,3584]{1,0:T(8,128)(2,1)S(1)}, u32[]{:S(2)}, u32[]{:S(2)}) collective-permute-start(bf16[32,3584]{1,0:T(8,128)(2,1)S(1)} %get-tuple-element.20), channel_id=1, source_target_pairs={{0,1},{1,0},{2,3},{3,2},{4,5},{5,4},{6,7},{7,6},{8,9},{9,8},{10,11... | collective-permute-start | bytes 688136 | tf_op jit(solution)/shard_map/ppermute | solution.py:275
  18.1 4.3 %collective-permute-start.6 = (bf16[8,3584]{1,0:T(8,128)(2,1)S(1)}, bf16[8,3584]{1,0:T(8,128)(2,1)S(1)}, u32[]{:S(2)}, u32[]{:S(2)}) collective-permute-start(bf16[8,3584]{1,0:T(8,128)(2,1)S(1)} %get-tuple-element.22), channel_id=1, source_target_pairs={{0,2},{2,0},{4,6},{6,4},{8,10},{10,8},{12,14},{14,12},{1,3},{3,1},... | collective-permute-start | bytes 172040 | tf_op jit(solution)/shard_map/ppermute | solution.py:221
  18.8 4.2 %collective-permute-start.7 = (bf16[8,3584]{1,0:T(8,128)(2,1)S(1)}, bf16[8,3584]{1,0:T(8,128)(2,1)S(1)}, u32[]{:S(2)}, u32[]{:S(2)}) collective-permute-start(bf16[8,3584]{1,0:T(8,128)(2,1)S(1)} %get-tuple-element.23), channel_id=1, source_target_pairs={{0,4},{2,6},{4,0},{6,2},{8,12},{10,14},{12,8},{14,10},{1,5},{3,7},... | collective-permute-start | bytes 172040 | tf_op jit(solution)/shard_map/ppermute | solution.py:221
  20.6 5.1 %collective-permute-start.8 = (bf16[8,3584]{1,0:T(8,128)(2,1)S(1)}, bf16[8,3584]{1,0:T(8,128)(2,1)S(1)}, u32[]{:S(2)}, u32[]{:S(2)}) collective-permute-start(bf16[8,3584]{1,0:T(8,128)(2,1)S(1)} %get-tuple-element.24), channel_id=1, source_target_pairs={{0,6},{2,4},{4,2},{6,0},{8,14},{10,12},{12,10},{14,8},{1,7},{3,5},... | collective-permute-start | bytes 172040 | tf_op jit(solution)/shard_map/ppermute | solution.py:221
  25.7 0.7 %collective-permute-start.9 = (bf16[8,3584]{1,0:T(8,128)(2,1)S(1)}, bf16[8,3584]{1,0:T(8,128)(2,1)S(1)}, u32[]{:S(2)}, u32[]{:S(2)}) collective-permute-start(bf16[8,3584]{1,0:T(8,128)(2,1)S(1)} %get-tuple-element.26), channel_id=1, source_target_pairs={{1,9},{3,11},{5,13},{7,15},{9,1},{11,3},{13,5},{15,7},{17,25},{19,... | collective-permute-start | bytes 172040 | tf_op jit(solution)/shard_map/ppermute | solution.py:258
  26.4 3.9 %copy-start.6 = (f32[2,8,1]{1,2,0:T(1,128)S(1)}, f32[2,8,1]{1,2,0:T(1,128)}, u32[]{:S(2)}) copy-start(f32[2,8,1]{1,2,0:T(1,128)} %param.11) | copy-start | bytes 196
  26.4 4.7 %collective-permute-start.10 = (bf16[8,1792]{1,0:T(8,128)(2,1)S(1)}, bf16[8,1792]{1,0:T(8,128)(2,1)S(1)}, u32[]{:S(2)}, u32[]{:S(2)}) collective-permute-start(bf16[8,1792]{1,0:T(8,128)(2,1)S(1)} %get-tuple-element.28), channel_id=1, source_target_pairs={{0,1},{1,0},{2,3},{3,2},{4,5},{5,4},{6,7},{7,6},{8,9},{9,8},{10,11... | collective-permute-start | bytes 86024 | tf_op jit(solution)/shard_map/ppermute | solution.py:287

commit v5 on v3

--- a/solution.py
+++ b/solution.py
@@ -53,36 +53,52 @@
         table_ref[m] = table.T
 
 
-def expert_kernel(*refs):
-    pieces, (gate_ref, up_ref, down_ref, keep_ref, send_ref) = refs[:-5], refs[-5:]
-    core = lax.axis_index("tp")
-    half = keep_ref.shape[2]
+def join_kernel(own_ref, rest_ref, out_ref):
+    out_ref[...] = jnp.concatenate([own_ref[...].astype(F32), rest_ref[...].astype(F32)], 0).astype(
+        BF16
+    )
+
+
+def hidden_units(pieces, gate_ref, up_ref):
     rows = jnp.concatenate([ref[...].astype(F32) for ref in pieces], 0).astype(BF16)
     gate_val = jnp.dot(rows, gate_ref[...], preferred_element_type=F32)
     up_val = jnp.dot(rows, up_ref[...], preferred_element_type=F32)
-    active = (gate_val / (1.0 + jnp.exp(-gate_val)) * up_val).astype(BF16)
+    return gate_val / (1.0 + jnp.exp(-gate_val)) * up_val
+
+
+def early_kernel(*refs):
+    refs[-1][...] = hidden_units(refs[:-3], *refs[-3:-1])
+
+
+def expert_kernel(*refs):
+    pieces, (gate_ref, up_ref, early_ref, down_ref, keep_ref, send_ref) = refs[:-6], refs[-6:]
+    core = lax.axis_index("tp")
+    half = keep_ref.shape[1]
+    late = hidden_units(pieces, gate_ref, up_ref)
+    active = jnp.concatenate([early_ref[...], late], 0).astype(BF16)
 
     def down(which):
         columns = pl.ds(pl.multiple_of(which * half, 128), half)
         return jnp.dot(active, down_ref[:, columns], preferred_element_type=F32)
 
-    send_ref[...] = down(1 - core).astype(BF16).reshape(send_ref.shape)
-    keep_ref[...] = down(core).reshape(keep_ref.shape)
+    send_ref[...] = down(1 - core).astype(BF16)
+    keep_ref[...] = down(core)
 
 
 def add_cores_kernel(keep_ref, got_ref, *out_refs):
-    for k in range(keep_ref.shape[0]):
-        total = keep_ref[k] + got_ref[k].astype(F32)
-        own_ref, rest_ref = out_refs[2 * k : 2 * k + 2]
-        per_node = own_ref.shape[0]
-        own_ref[...] = total[:per_node].astype(own_ref.dtype)
-        rest_ref[...] = total[per_node:].astype(rest_ref.dtype)
+    total = keep_ref[...] + got_ref[...].astype(F32)
+    start = 0
+    for ref in out_refs:
+        ref[...] = total[start : start + ref.shape[0]].astype(ref.dtype)
+        start += ref.shape[0]
 
 
 def add_members_kernel(*refs):
+    count = refs[-1].shape[0]
     total = refs[0][...]
     for ref in refs[1:-1]:
-        total = total + ref[...].astype(F32)
+        block = ref[...].astype(F32)
+        total = total + block[block.shape[0] - count :]
     refs[-1][...] = total.astype(BF16)
 
 
@@ -100,7 +116,7 @@
     own_refs, out_ref = refs[:-1], refs[-1]
     own = own_refs[0][...]
     for ref in own_refs[1:]:
-        own = own + ref[...].astype(F32)
+        own = own + ref[...].astype(F32)[: own.shape[0]]
     half = out_ref.shape[2]
     columns = pl.ds(pl.multiple_of(lax.axis_index("tp") * half, 128), half)
     for m in range(hidden_ref.shape[0]):
@@ -173,34 +189,53 @@
         placed,
         weights,
     )
-    members = range(1, node_size)
     inbox = to_nodes(rest, 1)
-    owns = [own] + [to_member(own, k) for k in members]
-    rests = [inbox] + [to_member(inbox, k) for k in members]
-    blocks = (node_size, all_rows, half)
+    own_one, own_two = to_member(own, 1), to_member(own, 2)
+    (joined,) = call(join_kernel, [((all_rows, model_width), BF16)], own, inbox)
+    far = to_member(joined, 3)
+    rest_two, rest_one = to_member(inbox, 2), to_member(inbox, 1)
+    (early,) = call(
+        early_kernel,
+        [((3 * per_node, w_gate.shape[1]), F32)],
+        own,
+        own_one,
+        own_two,
+        w_gate,
+        w_up,
+        cost=4 * 10**9,
+    )
+    block = (node_size * all_rows, half)
     keep, send = call(
         expert_kernel,
-        [(blocks, F32), (blocks, BF16)],
-        *[piece for pair in zip(owns, rests) for piece in pair],
+        [(block, F32), (block, BF16)],
+        inbox,
+        rest_one,
+        rest_two,
+        far,
         w_gate,
         w_up,
+        early,
         w_down,
         cost=10**6,
     )
     got = lax.ppermute(send, "tp", [(i, (i + 1) % share_count) for i in range(share_count)])
-    sums = call(
+    narrow, wide = (per_node, half), (rest_rows, half)
+    own, own_one, own_two, rest, rest_one, rest_two, own_far, rest_far = call(
         add_cores_kernel,
-        [
-            ((count, half), kind)
-            for kind in [F32] + [BF16] * (node_size - 1)
-            for count in (per_node, rest_rows)
-        ],
+        [(narrow, F32)]
+        + [(narrow, BF16)] * 2
+        + [(wide, F32)]
+        + [(wide, BF16)] * 2
+        + [(narrow, BF16), (wide, BF16)],
         keep,
         got,
     )
-    away = [sums[1]] + [to_member(sums[2 * k + 1], k) for k in members]
-    home = [sums[0]] + [to_member(sums[2 * k], k) for k in members]
-    (outbox,) = call(add_members_kernel, [((rest_rows, half), BF16)], *away)
+    rest_far, rest_two = to_member(rest_far, 3), to_member(rest_two, 2)
+    (near,) = call(join_kernel, [((all_rows, half), BF16)], own_one, rest_one)
+    near = to_member(near, 1)
+    own_far, own_two = to_member(own_far, 3), to_member(own_two, 2)
+    home = [own, near, own_far, own_two]
+    (outbox,) = call(add_members_kernel, [(wide, BF16)], rest, rest_far, rest_two, near)
     returned = to_nodes(outbox, -1)
     rows = (micro_count, row_count, half)
     (base,) = call(functools.partial(own_kernel, sizes), [(rows, F32)], hidden, table, *home)

time: 31.3 us -> 30.5 us (0.974)
  starting transfers between devices: 20.3 us -> 19.6 us
  waiting for transfers between devices: 7.93 us -> 7.33 us
  Pallas kernels: 1.97 us -> 2.37 us
    ppermute x12 -> x10, starting transfers between devices: 14.1 us -> 12.3 us  [to_member(): return lax.ppermute(array, 'ep', pairs)]
    ppermute x2, starting transfers between devices: 6.14 us -> 7.25 us  [to_nodes(): blocks.append(lax.ppermute(block, 'ep', pairs))]
    ppermute x12 -> x10, waiting for transfers between devices: 4.89 us -> 4.2 us  [to_member(): return lax.ppermute(array, 'ep', pairs)]
    pallas_call x8 -> x11, Pallas kernels: 1.97 us -> 2.37 us  [call(): pl.pallas_call(kernel, out_shape=[jax.ShapeDtypeStruct(shape, kind) for s...]
  transfers between devices with their start and end apart: 15 -> 13, of which waited for: 8 -> 6; matrix products, arithmetic and copies ran while one was open for 0% -> 0% of each run, Pallas kernels for 1% -> 2%
where the time goes in v5:
time: 30.5 us; the launch traced here: 30.3 us
  starting transfers between devices  19.6 us (64%)
  waiting for transfers between devices  7.33 us (24%)
  Pallas kernels  2.37 us (8%)
  local copies, waits for them, and re-layouts  0.91 us (3%)
    ppermute x10, starting transfers between devices, to_member(): return lax.ppermute(array, 'ep', pairs)  12.3 us
    ppermute x2, starting transfers between devices, to_nodes(): blocks.append(lax.ppermute(block, 'ep', pairs))  7.25 us
    ppermute x10, waiting for transfers between devices, to_member(): return lax.ppermute(array, 'ep', pairs)  4.2 us
    pallas_call x11, Pallas kernels, call(): pl.pallas_call(kernel, out_shape=[jax.ShapeDtypeStruct(shape, kind) for s...  2.37 us
    ppermute x2, waiting for transfers between devices, to_nodes(): blocks.append(lax.ppermute(block, 'ep', pairs))  1.65 us
    ppermute x1, waiting for transfers between devices, per_device(): lax.ppermute(send, 'tp', [(i, (i + 1) % share_count) for i in range(share...  1.48 us
    unnamed x16, local copies, waits for them, and re-layouts  0.91 us
  transfers between devices with their start and end apart: 13, of which 6 were waited for; matrix products, arithmetic and copies ran while one was open for 0% of the time, Pallas kernels for 2%

profile of v5, /device:TPU:0, one launch (start us, length us, event | category | flops | bytes accessed | tf_op | source)
XLA Modules:
  0.0 30.3 jit_solution(15499199414421619016)
XLA Ops:
  0.0 0.9 %copy-done.3 = bf16[2,8,3584]{2,1,0:T(8,128)(2,1)S(1)} copy-done((bf16[2,8,3584]{2,1,0:T(8,128)(2,1)S(1)}, bf16[2,8,3584]{2,1,0:T(8,128)(2,1)}, u32[]{:S(2)}) %copy-start.3) | copy-done | bytes 114712
  0.9 0.3 %shard_map.84 = (bf16[8,3584]{1,0:T(8,128)(2,1)S(1)}, bf16[8,3584]{1,0:T(8,128)(2,1)S(1)}) custom-call(s32[16,8]{1,0:T(8,128)S(1)} %shard_map.82.slot_ref, bf16[2,8,3584]{2,1,0:T(8,128)(2,1)S(1)} %copy-done.3, bf16[3584]{0:T(1024)(128)(2,1)S(1)} %copy-done.7, s32[2,1,8]{2,1,0:T(1,128)S(1)} %bitcast.9, s32[2,1,8]{2,1,0:T(1,128)S(1)} %bitcast.11), custom_call_target="tpu_custom_call" | custom-call | flops 20000000000 | bytes 40000000 | tf_op jit(solution)/shard_map/pallas_call | solution.py:153
  1.2 4.1 %collective-permute-start = (bf16[8,3584]{1,0:T(8,128)(2,1)S(1)}, bf16[8,3584]{1,0:T(8,128)(2,1)S(1)}, u32[]{:S(2)}, u32[]{:S(2)}) collective-permute-start(bf16[8,3584]{1,0:T(8,128)(2,1)S(1)} %get-tuple-element.17), channel_id=1, source_target_pairs={{0,8},{2,10},{4,12},{6,14},{8,0},{10,2},{12,4},{14,6},{1,9},{3,11}... | collective-permute-start | bytes 172040 | tf_op jit(solution)/shard_map/ppermute | solution.py:170
  5.3 1.6 %collective-permute-start.5 = (bf16[8,3584]{1,0:T(8,128)(2,1)S(1)}, bf16[8,3584]{1,0:T(8,128)(2,1)S(1)}, u32[]{:S(2)}, u32[]{:S(2)}) collective-permute-start(bf16[8,3584]{1,0:T(8,128)(2,1)S(1)} %get-tuple-element.18.own_ref.refs_0_), channel_id=1, source_target_pairs={{0,4},{2,6},{4,0},{6,2},{8,12},{10,14},{12,8},{14,10},{1,5},{3,7},... | collective-permute-start | bytes 172040 | tf_op jit(solution)/shard_map/ppermute | solution.py:163
  6.9 1.5 %collective-permute-start.4 = (bf16[8,3584]{1,0:T(8,128)(2,1)S(1)}, bf16[8,3584]{1,0:T(8,128)(2,1)S(1)}, u32[]{:S(2)}, u32[]{:S(2)}) collective-permute-start(bf16[8,3584]{1,0:T(8,128)(2,1)S(1)} %get-tuple-element.18.own_ref.refs_0_), channel_id=1, source_target_pairs={{0,2},{2,0},{4,6},{6,4},{8,10},{10,8},{12,14},{14,12},{1,3},{3,1},... | collective-permute-start | bytes 172040 | tf_op jit(solution)/shard_map/ppermute | solution.py:163
  8.4 2.1 %collective-permute-start.3 = (bf16[16,3584]{1,0:T(8,128)(2,1)S(1)}, bf16[16,3584]{1,0:T(8,128)(2,1)S(1)}, u32[]{:S(2)}, u32[]{:S(2)}) collective-permute-start(bf16[16,3584]{1,0:T(8,128)(2,1)S(1)} %shard_map.85), channel_id=1, source_target_pairs={{0,6},{2,4},{4,2},{6,0},{8,14},{10,12},{12,10},{14,8},{1,7},{3,5},... | collective-permute-start | bytes 344072 | tf_op jit(solution)/shard_map/ppermute | solution.py:163
  10.5 1.0 %collective-permute-start.2 = (bf16[8,3584]{1,0:T(8,128)(2,1)S(1)}, bf16[8,3584]{1,0:T(8,128)(2,1)S(1)}, u32[]{:S(2)}, u32[]{:S(2)}) collective-permute-start(bf16[8,3584]{1,0:T(8,128)(2,1)S(1)} %collective-permute-done.rest_ref.refs_0_), channel_id=1, source_target_pairs={{0,4},{2,6},{4,0},{6,2},{8,12},{10,14},{12,8},{14,10},{1,5},{3,7},... | collective-permute-start | bytes 172040 | tf_op jit(solution)/shard_map/ppermute | solution.py:163
  11.5 0.5 %collective-permute-start.1 = (bf16[8,3584]{1,0:T(8,128)(2,1)S(1)}, bf16[8,3584]{1,0:T(8,128)(2,1)S(1)}, u32[]{:S(2)}, u32[]{:S(2)}) collective-permute-start(bf16[8,3584]{1,0:T(8,128)(2,1)S(1)} %collective-permute-done.rest_ref.refs_0_), channel_id=1, source_target_pairs={{0,2},{2,0},{4,6},{6,4},{8,10},{10,8},{12,14},{14,12},{1,3},{3,1},... | collective-permute-start | bytes 172040 | tf_op jit(solution)/shard_map/ppermute | solution.py:163
  12.0 0.3 %collective-permute-done.4.refs_1_ = bf16[8,3584]{1,0:T(8,128)(2,1)S(1)} collective-permute-done((bf16[8,3584]{1,0:T(8,128)(2,1)S(1)}, bf16[8,3584]{1,0:T(8,128)(2,1)S(1)}, u32[]{:S(2)}, u32[]{:S(2)}) %collective-permute-start.4) | collective-permute-done | bytes 57376 | tf_op jit(solution)/shard_map/ppermute | solution.py:163
  12.3 0.4 %shard_map.86.refs_6_ = f32[24,128]{1,0:T(8,128)S(1)} custom-call(bf16[8,3584]{1,0:T(8,128)(2,1)S(1)} %get-tuple-element.18.own_ref.refs_0_, bf16[8,3584]{1,0:T(8,128)(2,1)S(1)} %collective-permute-done.4.refs_1_, bf16[8,3584]{1,0:T(8,128)(2,1)S(1)} %collective-permute-done.5.refs_2_, bf16[3584,128]{1,0:T(8,128)(2,1)S(1)} %copy-done, ...), custom_call_target="tpu_custom_call" | custom-call | flops 4000000000 | bytes 8000000 | tf_op jit(solution)/shard_map/pallas_call | solution.py:153
  12.7 2.1 %collective-permute-done.2.refs_2_ = bf16[8,3584]{1,0:T(8,128)(2,1)S(1)} collective-permute-done((bf16[8,3584]{1,0:T(8,128)(2,1)S(1)}, bf16[8,3584]{1,0:T(8,128)(2,1)S(1)}, u32[]{:S(2)}, u32[]{:S(2)}) %collective-permute-start.2) | collective-permute-done | bytes 57376 | tf_op jit(solution)/shard_map/ppermute | solution.py:163
  14.9 0.8 %collective-permute-done.1.refs_1_ = bf16[8,3584]{1,0:T(8,128)(2,1)S(1)} collective-permute-done((bf16[8,3584]{1,0:T(8,128)(2,1)S(1)}, bf16[8,3584]{1,0:T(8,128)(2,1)S(1)}, u32[]{:S(2)}, u32[]{:S(2)}) %collective-permute-start.1) | collective-permute-done | bytes 57376 | tf_op jit(solution)/shard_map/ppermute | solution.py:163
  15.7 0.7 %shard_map.87 = (f32[64,1792]{1,0:T(8,128)S(1)}, bf16[64,1792]{1,0:T(8,128)(2,1)S(1)}) custom-call(bf16[8,3584]{1,0:T(8,128)(2,1)S(1)} %collective-permute-done.rest_ref.refs_0_, bf16[8,3584]{1,0:T(8,128)(2,1)S(1)} %collective-permute-done.1.refs_1_, bf16[8,3584]{1,0:T(8,128)(2,1)S(1)} %collective-permute-done.2.refs_2_, ...), custom_call_target="tpu_custom_call" | custom-call | flops 1000000 | bytes 2000 | tf_op jit(solution)/shard_map/pallas_call | solution.py:153
  16.4 1.5 %collective-permute-done.6.got_ref = bf16[64,1792]{1,0:T(8,128)(2,1)S(1)} collective-permute-done((bf16[64,1792]{1,0:T(8,128)(2,1)S(1)}, bf16[64,1792]{1,0:T(8,128)(2,1)S(1)}, u32[]{:S(2)}, u32[]{:S(2)}) %collective-permute-start.6) | collective-permute-done | bytes 229408 | tf_op jit(solution)/shard_map/ppermute | solution.py:221
  17.9 0.7 %collective-permute-start.7 = (bf16[16,1792]{1,0:T(8,128)(2,1)S(1)}, bf16[16,1792]{1,0:T(8,128)(2,1)S(1)}, u32[]{:S(2)}, u32[]{:S(2)}) collective-permute-start(bf16[16,1792]{1,0:T(8,128)(2,1)S(1)} %shard_map.89), channel_id=1, source_target_pairs={{0,2},{2,0},{4,6},{6,4},{8,10},{10,8},{12,14},{14,12},{1,3},{3,1},... | collective-permute-start | bytes 172040 | tf_op jit(solution)/shard_map/ppermute | solution.py:163
  18.7 1.9 %collective-permute-start.10 = (bf16[8,1792]{1,0:T(8,128)(2,1)S(1)}, bf16[8,1792]{1,0:T(8,128)(2,1)S(1)}, u32[]{:S(2)}, u32[]{:S(2)}) collective-permute-start(bf16[8,1792]{1,0:T(8,128)(2,1)S(1)} %get-tuple-element.27), channel_id=1, source_target_pairs={{0,6},{2,4},{4,2},{6,0},{8,14},{10,12},{12,10},{14,8},{1,7},{3,5},... | collective-permute-start | bytes 86024 | tf_op jit(solution)/shard_map/ppermute | solution.py:163
  20.5 1.0 %collective-permute-start.11 = (bf16[8,1792]{1,0:T(8,128)(2,1)S(1)}, bf16[8,1792]{1,0:T(8,128)(2,1)S(1)}, u32[]{:S(2)}, u32[]{:S(2)}) collective-permute-start(bf16[8,1792]{1,0:T(8,128)(2,1)S(1)} %get-tuple-element.28), channel_id=1, source_target_pairs={{0,4},{2,6},{4,0},{6,2},{8,12},{10,14},{12,8},{14,10},{1,5},{3,7},... | collective-permute-start | bytes 86024 | tf_op jit(solution)/shard_map/ppermute | solution.py:163
  21.5 1.2 %collective-permute-start.8 = (bf16[8,1792]{1,0:T(8,128)(2,1)S(1)}, bf16[8,1792]{1,0:T(8,128)(2,1)S(1)}, u32[]{:S(2)}, u32[]{:S(2)}) collective-permute-start(bf16[8,1792]{1,0:T(8,128)(2,1)S(1)} %get-tuple-element.24), channel_id=1, source_target_pairs={{0,6},{2,4},{4,2},{6,0},{8,14},{10,12},{12,10},{14,8},{1,7},{3,5},... | collective-permute-start | bytes 86024 | tf_op jit(solution)/shard_map/ppermute | solution.py:163
  22.7 0.9 %collective-permute-start.9 = (bf16[8,1792]{1,0:T(8,128)(2,1)S(1)}, bf16[8,1792]{1,0:T(8,128)(2,1)S(1)}, u32[]{:S(2)}, u32[]{:S(2)}) collective-permute-start(bf16[8,1792]{1,0:T(8,128)(2,1)S(1)} %get-tuple-element.25), channel_id=1, source_target_pairs={{0,4},{2,6},{4,0},{6,2},{8,12},{10,14},{12,8},{14,10},{1,5},{3,7},... | collective-permute-start | bytes 86024 | tf_op jit(solution)/shard_map/ppermute | solution.py:163
  23.6 0.9 %collective-permute-done.11.refs_2_ = bf16[8,1792]{1,0:T(8,128)(2,1)S(1)} collective-permute-done((bf16[8,1792]{1,0:T(8,128)(2,1)S(1)}, bf16[8,1792]{1,0:T(8,128)(2,1)S(1)}, u32[]{:S(2)}, u32[]{:S(2)}) %collective-permute-start.11) | collective-permute-done | bytes 28704 | tf_op jit(solution)/shard_map/ppermute | solution.py:163
  24.6 3.1 %collective-permute-start.12 = (bf16[8,1792]{1,0:T(8,128)(2,1)S(1)}, bf16[8,1792]{1,0:T(8,128)(2,1)S(1)}, u32[]{:S(2)}, u32[]{:S(2)}) collective-permute-start(bf16[8,1792]{1,0:T(8,128)(2,1)S(1)} %shard_map.91), channel_id=1, source_target_pairs={{0,8},{2,10},{4,12},{6,14},{8,0},{10,2},{12,4},{14,6},{1,9},{3,11}... | collective-permute-start | bytes 86024 | tf_op jit(solution)/shard_map/ppermute | solution.py:170
  27.8 0.1 shard_map.90.base_ref
  28.0 1.6 %collective-permute-done.12.rest_ref = bf16[8,1792]{1,0:T(8,128)(2,1)S(1)} collective-permute-done((bf16[8,1792]{1,0:T(8,128)(2,1)S(1)}, bf16[8,1792]{1,0:T(8,128)(2,1)S(1)}, u32[]{:S(2)}, u32[]{:S(2)}) %collective-permute-start.12) | collective-permute-done | bytes 28704 | tf_op jit(solution)/shard_map/ppermute | solution.py:170
  29.6 0.7 %shard_map.92 = bf16[2,8,1792]{2,1,0:T(8,128)(2,1)} custom-call(f32[2,8,1792]{2,1,0:T(8,128)S(1)} %shard_map.90.base_ref, f32[2,8,16]{2,1,0:T(8,128)S(1)} %shard_map.83.weights_ref, bf16[8,1792]{1,0:T(8,128)(2,1)S(1)} %collective-permute-done.12.rest_ref), custom_call_target="tpu_custom_call" | custom-call | tf_op jit(solution)/shard_map/pallas_call | solution.py:153
  (29 shorter events, 0.3 us)
Async XLA Ops:
  0.0 0.9 %copy-start.3 = (bf16[2,8,3584]{2,1,0:T(8,128)(2,1)S(1)}, bf16[2,8,3584]{2,1,0:T(8,128)(2,1)}, u32[]{:S(2)}) copy-start(bf16[2,8,3584]{2,1,0:T(8,128)(2,1)} %hidden_ref.3) | copy-start | bytes 344068
  0.0 0.9 %copy-start.7 = (bf16[3584]{0:T(1024)(128)(2,1)S(1)}, bf16[3584]{0:T(1024)(128)(2,1)}, u32[]{:S(2)}) copy-start(bf16[3584]{0:T(1024)(128)(2,1)} %gain_ref.1) | copy-start | bytes 21508
  0.0 0.9 %copy-start.5 = (s32[2,8,1]{1,2,0:T(1,128)S(1)}, s32[2,8,1]{1,2,0:T(1,128)}, u32[]{:S(2)}) copy-start(s32[2,8,1]{1,2,0:T(1,128)} %param.12) | copy-start | bytes 196
  0.0 0.9 %copy-start.4 = (s32[2,8,1]{1,2,0:T(1,128)S(1)}, s32[2,8,1]{1,2,0:T(1,128)}, u32[]{:S(2)}) copy-start(s32[2,8,1]{1,2,0:T(1,128)} %param.10) | copy-start | bytes 196
  0.9 11.4 %copy-start = (bf16[3584,128]{1,0:T(8,128)(2,1)S(1)}, bf16[3584,128]{1,0:T(8,128)(2,1)}, u32[]{:S(2)}) copy-start(bf16[3584,128]{1,0:T(8,128)(2,1)} %refs_4_.3) | copy-start | bytes 2752516
  0.9 11.4 %copy-start.1 = (bf16[3584,128]{1,0:T(8,128)(2,1)S(1)}, bf16[3584,128]{1,0:T(8,128)(2,1)}, u32[]{:S(2)}) copy-start(bf16[3584,128]{1,0:T(8,128)(2,1)} %refs_5_.1) | copy-start | bytes 2752516
  1.2 7.2 %collective-permute-start = (bf16[8,3584]{1,0:T(8,128)(2,1)S(1)}, bf16[8,3584]{1,0:T(8,128)(2,1)S(1)}, u32[]{:S(2)}, u32[]{:S(2)}) collective-permute-start(bf16[8,3584]{1,0:T(8,128)(2,1)S(1)} %get-tuple-element.17), channel_id=1, source_target_pairs={{0,8},{2,10},{4,12},{6,14},{8,0},{10,2},{12,4},{14,6},{1,9},{3,11}... | collective-permute-start | bytes 172040 | tf_op jit(solution)/shard_map/ppermute | solution.py:170
  5.3 6.7 %collective-permute-start.5 = (bf16[8,3584]{1,0:T(8,128)(2,1)S(1)}, bf16[8,3584]{1,0:T(8,128)(2,1)S(1)}, u32[]{:S(2)}, u32[]{:S(2)}) collective-permute-start(bf16[8,3584]{1,0:T(8,128)(2,1)S(1)} %get-tuple-element.18.own_ref.refs_0_), channel_id=1, source_target_pairs={{0,4},{2,6},{4,0},{6,2},{8,12},{10,14},{12,8},{14,10},{1,5},{3,7},... | collective-permute-start | bytes 172040 | tf_op jit(solution)/shard_map/ppermute | solution.py:163
  6.9 5.4 %collective-permute-start.4 = (bf16[8,3584]{1,0:T(8,128)(2,1)S(1)}, bf16[8,3584]{1,0:T(8,128)(2,1)S(1)}, u32[]{:S(2)}, u32[]{:S(2)}) collective-permute-start(bf16[8,3584]{1,0:T(8,128)(2,1)S(1)} %get-tuple-element.18.own_ref.refs_0_), channel_id=1, source_target_pairs={{0,2},{2,0},{4,6},{6,4},{8,10},{10,8},{12,14},{14,12},{1,3},{3,1},... | collective-permute-start | bytes 172040 | tf_op jit(solution)/shard_map/ppermute | solution.py:163
  8.4 7.2 %copy-start.2 = (bf16[128,3584]{1,0:T(8,128)(2,1)S(1)}, bf16[128,3584]{1,0:T(8,128)(2,1)}, u32[]{:S(2)}) copy-start(bf16[128,3584]{1,0:T(8,128)(2,1)} %refs_7_.1) | copy-start | bytes 2752516
  8.4 7.2 %collective-permute-start.3 = (bf16[16,3584]{1,0:T(8,128)(2,1)S(1)}, bf16[16,3584]{1,0:T(8,128)(2,1)S(1)}, u32[]{:S(2)}, u32[]{:S(2)}) collective-permute-start(bf16[16,3584]{1,0:T(8,128)(2,1)S(1)} %shard_map.85), channel_id=1, source_target_pairs={{0,6},{2,4},{4,2},{6,0},{8,14},{10,12},{12,10},{14,8},{1,7},{3,5},... | collective-permute-start | bytes 344072 | tf_op jit(solution)/shard_map/ppermute | solution.py:163
  10.5 4.3 %collective-permute-start.2 = (bf16[8,3584]{1,0:T(8,128)(2,1)S(1)}, bf16[8,3584]{1,0:T(8,128)(2,1)S(1)}, u32[]{:S(2)}, u32[]{:S(2)}) collective-permute-start(bf16[8,3584]{1,0:T(8,128)(2,1)S(1)} %collective-permute-done.rest_ref.refs_0_), channel_id=1, source_target_pairs={{0,4},{2,6},{4,0},{6,2},{8,12},{10,14},{12,8},{14,10},{1,5},{3,7},... | collective-permute-start | bytes 172040 | tf_op jit(solution)/shard_map/ppermute | solution.py:163
  11.5 4.2 %collective-permute-start.1 = (bf16[8,3584]{1,0:T(8,128)(2,1)S(1)}, bf16[8,3584]{1,0:T(8,128)(2,1)S(1)}, u32[]{:S(2)}, u32[]{:S(2)}) collective-permute-start(bf16[8,3584]{1,0:T(8,128)(2,1)S(1)} %collective-permute-done.rest_ref.refs_0_), channel_id=1, source_target_pairs={{0,2},{2,0},{4,6},{6,4},{8,10},{10,8},{12,14},{14,12},{1,3},{3,1},... | collective-permute-start | bytes 172040 | tf_op jit(solution)/shard_map/ppermute | solution.py:163
  16.3 1.6 %collective-permute-start.6 = (bf16[64,1792]{1,0:T(8,128)(2,1)S(1)}, bf16[64,1792]{1,0:T(8,128)(2,1)S(1)}, u32[]{:S(2)}, u32[]{:S(2)}) collective-permute-start(bf16[64,1792]{1,0:T(8,128)(2,1)S(1)} %get-tuple-element.20), channel_id=1, source_target_pairs={{0,1},{1,0},{2,3},{3,2},{4,5},{5,4},{6,7},{7,6},{8,9},{9,8},{10,11... | collective-permute-start | bytes 688136 | tf_op jit(solution)/shard_map/ppermute | solution.py:221
  17.9 6.6 %collective-permute-start.7 = (bf16[16,1792]{1,0:T(8,128)(2,1)S(1)}, bf16[16,1792]{1,0:T(8,128)(2,1)S(1)}, u32[]{:S(2)}, u32[]{:S(2)}) collective-permute-start(bf16[16,1792]{1,0:T(8,128)(2,1)S(1)} %shard_map.89), channel_id=1, source_target_pairs={{0,2},{2,0},{4,6},{6,4},{8,10},{10,8},{12,14},{14,12},{1,3},{3,1},... | collective-permute-start | bytes 172040 | tf_op jit(solution)/shard_map/ppermute | solution.py:163
  18.7 5.0 %collective-permute-start.10 = (bf16[8,1792]{1,0:T(8,128)(2,1)S(1)}, bf16[8,1792]{1,0:T(8,128)(2,1)S(1)}, u32[]{:S(2)}, u32[]{:S(2)}) collective-permute-start(bf16[8,1792]{1,0:T(8,128)(2,1)S(1)} %get-tuple-element.27), channel_id=1, source_target_pairs={{0,6},{2,4},{4,2},{6,0},{8,14},{10,12},{12,10},{14,8},{1,7},{3,5},... | collective-permute-start | bytes 86024 | tf_op jit(solution)/shard_map/ppermute | solution.py:163
  20.5 4.0 %collective-permute-start.11 = (bf16[8,1792]{1,0:T(8,128)(2,1)S(1)}, bf16[8,1792]{1,0:T(8,128)(2,1)S(1)}, u32[]{:S(2)}, u32[]{:S(2)}) collective-permute-start(bf16[8,1792]{1,0:T(8,128)(2,1)S(1)} %get-tuple-element.28), channel_id=1, source_target_pairs={{0,4},{2,6},{4,0},{6,2},{8,12},{10,14},{12,8},{14,10},{1,5},{3,7},... | collective-permute-start | bytes 86024 | tf_op jit(solution)/shard_map/ppermute | solution.py:163
  21.5 6.3 %collective-permute-start.8 = (bf16[8,1792]{1,0:T(8,128)(2,1)S(1)}, bf16[8,1792]{1,0:T(8,128)(2,1)S(1)}, u32[]{:S(2)}, u32[]{:S(2)}) collective-permute-start(bf16[8,1792]{1,0:T(8,128)(2,1)S(1)} %get-tuple-element.24), channel_id=1, source_target_pairs={{0,6},{2,4},{4,2},{6,0},{8,14},{10,12},{12,10},{14,8},{1,7},{3,5},... | collective-permute-start | bytes 86024 | tf_op jit(solution)/shard_map/ppermute | solution.py:163
  22.7 5.1 %collective-permute-start.9 = (bf16[8,1792]{1,0:T(8,128)(2,1)S(1)}, bf16[8,1792]{1,0:T(8,128)(2,1)S(1)}, u32[]{:S(2)}, u32[]{:S(2)}) collective-permute-start(bf16[8,1792]{1,0:T(8,128)(2,1)S(1)} %get-tuple-element.25), channel_id=1, source_target_pairs={{0,4},{2,6},{4,0},{6,2},{8,12},{10,14},{12,8},{14,10},{1,5},{3,7},... | collective-permute-start | bytes 86024 | tf_op jit(solution)/shard_map/ppermute | solution.py:163
  24.6 3.2 %copy-start.6 = (f32[2,8,1]{1,2,0:T(1,128)S(1)}, f32[2,8,1]{1,2,0:T(1,128)}, u32[]{:S(2)}) copy-start(f32[2,8,1]{1,2,0:T(1,128)} %param.11) | copy-start | bytes 196
  24.6 5.0 %collective-permute-start.12 = (bf16[8,1792]{1,0:T(8,128)(2,1)S(1)}, bf16[8,1792]{1,0:T(8,128)(2,1)S(1)}, u32[]{:S(2)}, u32[]{:S(2)}) collective-permute-start(bf16[8,1792]{1,0:T(8,128)(2,1)S(1)} %shard_map.91), channel_id=1, source_target_pairs={{0,8},{2,10},{4,12},{6,14},{8,0},{10,2},{12,4},{14,6},{1,9},{3,11}... | collective-permute-start | bytes 86024 | tf_op jit(solution)/shard_map/ppermute | solution.py:170

commit v6 on v5

--- a/solution.py
+++ b/solution.py
@@ -70,12 +70,9 @@
     refs[-1][...] = hidden_units(refs[:-3], *refs[-3:-1])
 
 
-def expert_kernel(*refs):
-    pieces, (gate_ref, up_ref, early_ref, down_ref, keep_ref, send_ref) = refs[:-6], refs[-6:]
+def down_halves(active, down_ref, keep_ref, send_ref):
     core = lax.axis_index("tp")
     half = keep_ref.shape[1]
-    late = hidden_units(pieces, gate_ref, up_ref)
-    active = jnp.concatenate([early_ref[...], late], 0).astype(BF16)
 
     def down(which):
         columns = pl.ds(pl.multiple_of(which * half, 128), half)
@@ -83,6 +80,93 @@
 
     send_ref[...] = down(1 - core).astype(BF16)
     keep_ref[...] = down(core)
+
+
+def expert_kernel(*refs):
+    pieces, (gate_ref, up_ref, early_ref, down_ref, keep_ref, send_ref) = refs[:-6], refs[-6:]
+    late = hidden_units(pieces, gate_ref, up_ref)
+    active = jnp.concatenate([early_ref[...], late], 0).astype(BF16)
+    down_halves(active, down_ref, keep_ref, send_ref)
+
+
+def pack_kernel(hop_ref, pass_ref, side_ref, unread_ref, out_ref):
+    out_ref[...] = jnp.concatenate(
+        [ref[...].astype(F32) for ref in (hop_ref, pass_ref, side_ref)], 0
+    ).astype(BF16)
+
+
+def shared_expert_kernel(
+    count,
+    hop_ref,
+    pass_ref,
+    other_ref,
+    gate_ref,
+    up_ref,
+    early_ref,
+    down_ref,
+    keep_ref,
+    keep_own_ref,
+    send_ref,
+    own_ref,
+):
+    core = lax.axis_index("tp")
+    half = keep_own_ref.shape[1]
+    late = hidden_units((hop_ref, pass_ref, other_ref), gate_ref, up_ref)
+    early = early_ref[...]
+    active = jnp.concatenate([late[: 2 * count], early[2 * count :], late[2 * count :]], 0)
+    active = jnp.concatenate([active, early[: 2 * count]], 0).astype(BF16)
+    product = jnp.dot(active, down_ref[...], preferred_element_type=F32)
+    keep_ref[...] = product[: 3 * count]
+    own_ref[...] = product[6 * count :]
+    keep_own_ref[...] = own_ref[:, pl.ds(pl.multiple_of(core * half, 128), half)]
+    own = own_ref[:, pl.ds(pl.multiple_of((1 - core) * half, 128), half)]
+    send = product[3 * count : 6 * count]
+    send_ref[...] = jnp.concatenate([send[:, :half], send[:, half:], own], 0).astype(BF16)
+
+
+def shared_sums_kernel(
+    keep_ref, keep_own_ref, got_ref, hop_ref, pass_ref, side_ref, own_ref, two_ref
+):
+    count, half = own_ref.shape
+    got = got_ref[...].astype(F32)
+    total = keep_ref[...] + jnp.concatenate([got[: 3 * count], got[3 * count : 6 * count]], 1)
+    hop_ref[...] = total[:count]
+    pass_ref[...] = total[count : 2 * count].astype(BF16)
+    side_ref[...] = total[2 * count :].astype(BF16)
+    own = keep_own_ref[...] + got[6 * count :]
+    own_ref[...] = own[:count]
+    two_ref[...] = own[count:]
+
+
+def halves_kernel(own_ref, two_ref, side_ref, back_ref, own_out, back_out, send_ref):
+    core = lax.axis_index("tp")
+    half = back_out.shape[1]
+    mine = pl.ds(pl.multiple_of(core * half, 128), half)
+    other = pl.ds(pl.multiple_of((1 - core) * half, 128), half)
+    own_out[...] = own_ref[...] + two_ref[...] + side_ref[:, mine].astype(F32)
+    back_out[...] = back_ref[:, mine]
+    send_ref[...] = jnp.concatenate(
+        [side_ref[:, other].astype(F32), back_ref[:, other].astype(F32)], 0
+    ).astype(BF16)
+
+
+def base_kernel(sizes, hidden_ref, table_ref, own_ref, back_ref, out_ref):
+    own = own_ref[...]
+    back = back_ref[...].astype(F32)
+    half = out_ref.shape[2]
+    columns = pl.ds(pl.multiple_of(lax.axis_index("tp") * half, 128), half)
+    for m in range(hidden_ref.shape[0]):
+        base = hidden_ref[m, :, columns].astype(F32)
+        base = weighted(base, table_ref[m], own, sizes, m, 0, 1)
+        out_ref[m] = weighted(base, table_ref[m], back, sizes, m, 1, 1)
+
+
+def last_kernel(sizes, base_ref, table_ref, got_ref, out_ref):
+    got = got_ref[...].astype(F32)
+    count = got.shape[0] // 2
+    for m in range(base_ref.shape[0]):
+        base = weighted(base_ref[m], table_ref[m], got[:count], sizes, m, 0, 1)
+        out_ref[m] = weighted(base, table_ref[m], got[count:], sizes, m, 1, 1).astype(BF16)
 
 
 def add_cores_kernel(keep_ref, got_ref, *out_refs):
@@ -189,22 +273,86 @@
         placed,
         weights,
     )
+    block = (node_size * all_rows, half)
+    hidden_block = ((3 * per_node, w_gate.shape[1]), F32)
+
+    def early_rows(*pieces):
+        (early,) = call(early_kernel, [hidden_block], *pieces, w_gate, w_up, cost=4 * 10**9)
+        return early
+
+    if nodes == 2 and node_size == 4 and share_count == 2:
+
+        def by_core(array, flip_zero, flip_one):
+            pairs = []
+            for j in range(ep_count):
+                pairs += [(2 * j, 2 * (j ^ flip_zero)), (2 * j + 1, 2 * (j ^ flip_one) + 1)]
+            return lax.ppermute(array, ("ep", "tp"), pairs)
+
+        swap = [(0, 1), (1, 0)]
+        full, narrow = (per_node, model_width), (per_node, half)
+        hop = by_core(rest, node_size, node_size ^ 2)
+        own_two, own_side = to_member(own, 2), by_core(own, 1, 3)
+        passed = to_member(hop, 1)
+        early = early_rows(own, own_two, own_side)
+        (packed,) = call(pack_kernel, [((3 * per_node, model_width), BF16)], hop, passed, own_side, own_two)
+        other = lax.ppermute(packed, "tp", swap)
+        keep, keep_own, send = call(
+            functools.partial(shared_expert_kernel, per_node),
+            [
+                ((3 * per_node, model_width), F32),
+                ((2 * per_node, half), F32),
+                ((8 * per_node, half), BF16),
+            ],
+            hop,
+            passed,
+            other,
+            w_gate,
+            w_up,
+            early,
+            w_down,
+            scratch=[pltpu.VMEM((2 * per_node, model_width), F32)],
+            cost=10**6,
+        )
+        got = lax.ppermute(send, "tp", swap)
+        hop, passed, side, own, two = call(
+            shared_sums_kernel,
+            [(full, F32), (full, BF16), (full, BF16), (narrow, F32), (narrow, F32)],
+            keep,
+            keep_own,
+            got,
+        )
+        passed = to_member(passed, 1)
+        side, two = by_core(side, 1, 3), to_member(two, 2)
+        (outbox,) = call(add_members_kernel, [(full, BF16)], hop, passed)
+        back = by_core(outbox, node_size, node_size ^ 2)
+        own, back, send = call(
+            halves_kernel,
+            [(narrow, F32), (narrow, BF16), ((2 * per_node, half), BF16)],
+            own,
+            two,
+            side,
+            back,
+        )
+        got = lax.ppermute(send, "tp", swap)
+        rows = (micro_count, row_count, half)
+        (base,) = call(
+            functools.partial(base_kernel, sizes),
+            [(rows, F32)],
+            hidden,
+            table,
+            own,
+            back,
+        )
+        (mixed,) = call(functools.partial(last_kernel, sizes), [(rows, BF16)], base, table, got)
+        return mixed
+
+    names = ("own", "own_one", "own_two", "rest", "rest_one", "rest_two", "own_far", "rest_far")
     inbox = to_nodes(rest, 1)
     own_one, own_two = to_member(own, 1), to_member(own, 2)
     (joined,) = call(join_kernel, [((all_rows, model_width), BF16)], own, inbox)
     far = to_member(joined, 3)
     rest_two, rest_one = to_member(inbox, 2), to_member(inbox, 1)
-    (early,) = call(
-        early_kernel,
-        [((3 * per_node, w_gate.shape[1]), F32)],
-        own,
-        own_one,
-        own_two,
-        w_gate,
-        w_up,
-        cost=4 * 10**9,
-    )
-    block = (node_size * all_rows, half)
+    early = early_rows(own, own_one, own_two)
     keep, send = call(
         expert_kernel,
         [(block, F32), (block, BF16)],
@@ -220,15 +368,14 @@
     )
     got = lax.ppermute(send, "tp", [(i, (i + 1) % share_count) for i in range(share_count)])
     narrow, wide = (per_node, half), (rest_rows, half)
-    own, own_one, own_two, rest, rest_one, rest_two, own_far, rest_far = call(
-        add_cores_kernel,
-        [(narrow, F32)]
-        + [(narrow, BF16)] * 2
-        + [(wide, F32)]
-        + [(wide, BF16)] * 2
-        + [(narrow, BF16), (wide, BF16)],
-        keep,
-        got,
+    shapes = [
+        (narrow if name.startswith("own") else wide, F32 if name in ("own", "rest") else BF16)
+        for name in names
+    ]
+    sums = dict(zip(names, call(add_cores_kernel, shapes, keep, got)))
+    own, own_one, own_two, own_far = (sums[n] for n in ("own", "own_one", "own_two", "own_far"))
+    rest, rest_one, rest_two, rest_far = (
+        sums[n] for n in ("rest", "rest_one", "rest_two", "rest_far")
     )
     rest_far, rest_two = to_member(rest_far, 3), to_member(rest_two, 2)
     (near,) = call(join_kernel, [((all_rows, half), BF16)], own_one, rest_one)

time: 30.5 us -> 28.3 us (0.928)
  starting transfers between devices: 19.6 us -> 14.3 us
  waiting for transfers between devices: 7.33 us -> 9.74 us
  local copies, waits for them, and re-layouts: 0.91 us -> 1.5 us
    ppermute x10 -> x4, starting transfers between devices: 12.3 us -> 5.59 us  [to_member(): return lax.ppermute(array, 'ep', pairs)]
    ppermute x3 -> x7, waiting for transfers between devices: 3.12 us -> 7.48 us  [the longest x4 4.75 us: by_core(): return lax.ppermute(array, ('ep', 'tp'), pairs)]
    ppermute x10 -> x4, waiting for transfers between devices: 4.2 us -> 2.27 us  [to_member(): return lax.ppermute(array, 'ep', pairs)]
    ppermute x3 -> x7, starting transfers between devices: 7.32 us -> 8.76 us  [the longest x4 8.4 us: by_core(): return lax.ppermute(array, ('ep', 'tp'), pairs)]
    unnamed x16, local copies, waits for them, and re-layouts: 0.91 us -> 1.5 us
  transfers between devices with their start and end apart: 13 -> 11, of which waited for: 6 -> 9; matrix products, arithmetic and copies ran while one was open for 0% -> 0% of each run, Pallas kernels for 2% -> 2%
where the time goes in v6:
time: 28.3 us; the launch traced here: 28.2 us
  starting transfers between devices  14.3 us (51%)
  waiting for transfers between devices  9.74 us (34%)
  Pallas kernels  2.47 us (9%)
  local copies, waits for them, and re-layouts  1.5 us (5%)
    ppermute x4, starting transfers between devices, by_core(): return lax.ppermute(array, ('ep', 'tp'), pairs)  8.4 us
    ppermute x4, starting transfers between devices, to_member(): return lax.ppermute(array, 'ep', pairs)  5.59 us
    ppermute x4, waiting for transfers between devices, by_core(): return lax.ppermute(array, ('ep', 'tp'), pairs)  4.75 us
    pallas_call x11, Pallas kernels, call(): pl.pallas_call(kernel, out_shape=[jax.ShapeDtypeStruct(shape, kind) for s...  2.47 us
    ppermute x4, waiting for transfers between devices, to_member(): return lax.ppermute(array, 'ep', pairs)  2.27 us
    ppermute x2, waiting for transfers between devices, per_device(): got = lax.ppermute(send, 'tp', swap)  1.74 us
    unnamed x16, local copies, waits for them, and re-layouts  1.5 us
    ppermute x1, waiting for transfers between devices, per_device(): other = lax.ppermute(packed, 'tp', swap)  0.99 us
  transfers between devices with their start and end apart: 11, of which 9 were waited for; matrix products, arithmetic and copies ran while one was open for 0% of the time, Pallas kernels for 2%

profile of v6, /device:TPU:0, one launch (start us, length us, event | category | flops | bytes accessed | tf_op | source)
XLA Modules:
  0.0 28.2 jit_solution(9735664097893233050)
XLA Ops:
  0.0 0.9 %copy-done.3 = bf16[2,8,3584]{2,1,0:T(8,128)(2,1)S(1)} copy-done((bf16[2,8,3584]{2,1,0:T(8,128)(2,1)S(1)}, bf16[2,8,3584]{2,1,0:T(8,128)(2,1)}, u32[]{:S(2)}) %copy-start.3) | copy-done | bytes 114712
  0.9 0.3 %shard_map.84 = (bf16[8,3584]{1,0:T(8,128)(2,1)S(1)}, bf16[8,3584]{1,0:T(8,128)(2,1)S(1)}) custom-call(s32[16,8]{1,0:T(8,128)S(1)} %shard_map.82.slot_ref, bf16[2,8,3584]{2,1,0:T(8,128)(2,1)S(1)} %copy-done.3, bf16[3584]{0:T(1024)(128)(2,1)S(1)} %copy-done.7, s32[2,1,8]{2,1,0:T(1,128)S(1)} %bitcast.9, s32[2,1,8]{2,1,0:T(1,128)S(1)} %bitcast.11), custom_call_target="tpu_custom_call" | custom-call | flops 20000000000 | bytes 40000000 | tf_op jit(solution)/shard_map/pallas_call | solution.py:237
  1.2 4.1 %collective-permute-start = (bf16[8,3584]{1,0:T(8,128)(2,1)S(1)}, bf16[8,3584]{1,0:T(8,128)(2,1)S(1)}, u32[]{:S(2)}, u32[]{:S(2)}) collective-permute-start(bf16[8,3584]{1,0:T(8,128)(2,1)S(1)} %get-tuple-element.18), channel_id=1, source_target_pairs={{0,8},{1,13},{2,10},{3,15},{4,12},{5,9},{6,14},{7,11},{8,0},{9,5},... | collective-permute-start | bytes 172040 | tf_op jit(solution)/shard_map/ppermute | solution.py:289
  5.3 1.6 %collective-permute-start.3 = (bf16[8,3584]{1,0:T(8,128)(2,1)S(1)}, bf16[8,3584]{1,0:T(8,128)(2,1)S(1)}, u32[]{:S(2)}, u32[]{:S(2)}) collective-permute-start(bf16[8,3584]{1,0:T(8,128)(2,1)S(1)} %get-tuple-element.19.refs_0_), channel_id=1, source_target_pairs={{0,4},{2,6},{4,0},{6,2},{8,12},{10,14},{12,8},{14,10},{1,5},{3,7},... | collective-permute-start | bytes 172040 | tf_op jit(solution)/shard_map/ppermute | solution.py:247
  6.9 1.5 %collective-permute-start.2 = (bf16[8,3584]{1,0:T(8,128)(2,1)S(1)}, bf16[8,3584]{1,0:T(8,128)(2,1)S(1)}, u32[]{:S(2)}, u32[]{:S(2)}) collective-permute-start(bf16[8,3584]{1,0:T(8,128)(2,1)S(1)} %get-tuple-element.19.refs_0_), channel_id=1, source_target_pairs={{0,2},{1,7},{2,0},{3,5},{4,6},{5,3},{6,4},{7,1},{8,10},{9,15},{10,... | collective-permute-start | bytes 172040 | tf_op jit(solution)/shard_map/ppermute | solution.py:289
  8.4 1.4 %collective-permute-start.1 = (bf16[8,3584]{1,0:T(8,128)(2,1)S(1)}, bf16[8,3584]{1,0:T(8,128)(2,1)S(1)}, u32[]{:S(2)}, u32[]{:S(2)}) collective-permute-start(bf16[8,3584]{1,0:T(8,128)(2,1)S(1)} %collective-permute-done.hop_ref), channel_id=1, source_target_pairs={{0,2},{2,0},{4,6},{6,4},{8,10},{10,8},{12,14},{14,12},{1,3},{3,1},... | collective-permute-start | bytes 172040 | tf_op jit(solution)/shard_map/ppermute | solution.py:247
  9.8 0.2 collective-permute-done.3.unread_ref.refs_1_
  10.0 2.0 %collective-permute-done.2.side_ref.refs_2_ = bf16[8,3584]{1,0:T(8,128)(2,1)S(1)} collective-permute-done((bf16[8,3584]{1,0:T(8,128)(2,1)S(1)}, bf16[8,3584]{1,0:T(8,128)(2,1)S(1)}, u32[]{:S(2)}, u32[]{:S(2)}) %collective-permute-start.2) | collective-permute-done | bytes 57376 | tf_op jit(solution)/shard_map/ppermute | solution.py:289
  12.0 0.8 %collective-permute-done.1.pass_ref = bf16[8,3584]{1,0:T(8,128)(2,1)S(1)} collective-permute-done((bf16[8,3584]{1,0:T(8,128)(2,1)S(1)}, bf16[8,3584]{1,0:T(8,128)(2,1)S(1)}, u32[]{:S(2)}, u32[]{:S(2)}) %collective-permute-start.1) | collective-permute-done | bytes 57376 | tf_op jit(solution)/shard_map/ppermute | solution.py:247
  13.0 0.4 %shard_map.86.early_ref = f32[24,128]{1,0:T(8,128)S(1)} custom-call(bf16[8,3584]{1,0:T(8,128)(2,1)S(1)} %get-tuple-element.19.refs_0_, bf16[8,3584]{1,0:T(8,128)(2,1)S(1)} %collective-permute-done.3.unread_ref.refs_1_, bf16[8,3584]{1,0:T(8,128)(2,1)S(1)} %collective-permute-done.2.side_ref.refs_2_, bf16[3584,128]{1,0:T(8,128)(2,1)S(1)} %copy-done, ...), custom_call_target="tpu_custom_call" | custom-call | flops 4000000000 | bytes 8000000 | tf_op jit(solution)/shard_map/pallas_call | solution.py:237
  13.4 1.0 %collective-permute-done.4.other_ref = bf16[24,3584]{1,0:T(8,128)(2,1)S(1)} collective-permute-done((bf16[24,3584]{1,0:T(8,128)(2,1)S(1)}, bf16[24,3584]{1,0:T(8,128)(2,1)S(1)}, u32[]{:S(2)}, u32[]{:S(2)}) %collective-permute-start.4) | collective-permute-done | bytes 172064 | tf_op jit(solution)/shard_map/ppermute | solution.py:298
  14.4 0.7 %shard_map.87 = (f32[24,3584]{1,0:T(8,128)S(1)}, f32[16,1792]{1,0:T(8,128)S(1)}, bf16[64,1792]{1,0:T(8,128)(2,1)S(1)}) custom-call(bf16[8,3584]{1,0:T(8,128)(2,1)S(1)} %collective-permute-done.hop_ref, bf16[8,3584]{1,0:T(8,128)(2,1)S(1)} %collective-permute-done.1.pass_ref, bf16[24,3584]{1,0:T(8,128)(2,1)S(1)} %collective-permute-done.4.other_ref, ...), custom_call_target="tpu_custom_call" | custom-call | flops 1000000 | bytes 2000 | tf_op jit(solution)/shard_map/pallas_call | solution.py:237
  15.0 0.2 collective-permute-start.5
  15.3 1.3 %collective-permute-done.5.got_ref = bf16[64,1792]{1,0:T(8,128)(2,1)S(1)} collective-permute-done((bf16[64,1792]{1,0:T(8,128)(2,1)S(1)}, bf16[64,1792]{1,0:T(8,128)(2,1)S(1)}, u32[]{:S(2)}, u32[]{:S(2)}) %collective-permute-start.5) | collective-permute-done | bytes 229408 | tf_op jit(solution)/shard_map/ppermute | solution.py:316
  16.7 1.2 %collective-permute-start.8 = (bf16[8,3584]{1,0:T(8,128)(2,1)S(1)}, bf16[8,3584]{1,0:T(8,128)(2,1)S(1)}, u32[]{:S(2)}, u32[]{:S(2)}) collective-permute-start(bf16[8,3584]{1,0:T(8,128)(2,1)S(1)} %get-tuple-element.27), channel_id=1, source_target_pairs={{0,2},{2,0},{4,6},{6,4},{8,10},{10,8},{12,14},{14,12},{1,3},{3,1},... | collective-permute-start | bytes 172040 | tf_op jit(solution)/shard_map/ppermute | solution.py:247
  17.8 1.5 %collective-permute-start.6 = (f32[8,1792]{1,0:T(8,128)S(1)}, f32[8,1792]{1,0:T(8,128)S(1)}, u32[]{:S(2)}, u32[]{:S(2)}) collective-permute-start(f32[8,1792]{1,0:T(8,128)S(1)} %get-tuple-element.24), channel_id=1, source_target_pairs={{0,4},{2,6},{4,0},{6,2},{8,12},{10,14},{12,8},{14,10},{1,5},{3,7},... | collective-permute-start | bytes 172040 | tf_op jit(solution)/shard_map/ppermute | solution.py:247
  19.3 0.4 %collective-permute-start.7 = (bf16[8,3584]{1,0:T(8,128)(2,1)S(1)}, bf16[8,3584]{1,0:T(8,128)(2,1)S(1)}, u32[]{:S(2)}, u32[]{:S(2)}) collective-permute-start(bf16[8,3584]{1,0:T(8,128)(2,1)S(1)} %get-tuple-element.25), channel_id=1, source_target_pairs={{0,2},{1,7},{2,0},{3,5},{4,6},{5,3},{6,4},{7,1},{8,10},{9,15},{10,... | collective-permute-start | bytes 172040 | tf_op jit(solution)/shard_map/ppermute | solution.py:289
  19.7 1.2 %collective-permute-done.8.refs_1_ = bf16[8,3584]{1,0:T(8,128)(2,1)S(1)} collective-permute-done((bf16[8,3584]{1,0:T(8,128)(2,1)S(1)}, bf16[8,3584]{1,0:T(8,128)(2,1)S(1)}, u32[]{:S(2)}, u32[]{:S(2)}) %collective-permute-start.8) | collective-permute-done | bytes 57376 | tf_op jit(solution)/shard_map/ppermute | solution.py:247
  20.9 2.4 %collective-permute-start.9 = (bf16[8,3584]{1,0:T(8,128)(2,1)S(1)}, bf16[8,3584]{1,0:T(8,128)(2,1)S(1)}, u32[]{:S(2)}, u32[]{:S(2)}) collective-permute-start(bf16[8,3584]{1,0:T(8,128)(2,1)S(1)} %shard_map.89), channel_id=1, source_target_pairs={{0,8},{1,13},{2,10},{3,15},{4,12},{5,9},{6,14},{7,11},{8,0},{9,5},... | collective-permute-start | bytes 172040 | tf_op jit(solution)/shard_map/ppermute | solution.py:289
  23.3 0.3 %collective-permute-done.7.side_ref = bf16[8,3584]{1,0:T(8,128)(2,1)S(1)} collective-permute-done((bf16[8,3584]{1,0:T(8,128)(2,1)S(1)}, bf16[8,3584]{1,0:T(8,128)(2,1)S(1)}, u32[]{:S(2)}, u32[]{:S(2)}) %collective-permute-start.7) | collective-permute-done | bytes 57376 | tf_op jit(solution)/shard_map/ppermute | solution.py:289
  23.6 2.4 %collective-permute-done.9.back_ref = bf16[8,3584]{1,0:T(8,128)(2,1)S(1)} collective-permute-done((bf16[8,3584]{1,0:T(8,128)(2,1)S(1)}, bf16[8,3584]{1,0:T(8,128)(2,1)S(1)}, u32[]{:S(2)}, u32[]{:S(2)}) %collective-permute-start.9) | collective-permute-done | bytes 57376 | tf_op jit(solution)/shard_map/ppermute | solution.py:289
  26.2 0.6 %copy-done.6 = f32[2,8,1]{1,2,0:T(1,128)S(1)} copy-done((f32[2,8,1]{1,2,0:T(1,128)S(1)}, f32[2,8,1]{1,2,0:T(1,128)}, u32[]{:S(2)}) %copy-start.6) | copy-done | bytes 88
  27.0 0.4 %collective-permute-done.10.got_ref = bf16[16,1792]{1,0:T(8,128)(2,1)S(1)} collective-permute-done((bf16[16,1792]{1,0:T(8,128)(2,1)S(1)}, bf16[16,1792]{1,0:T(8,128)(2,1)S(1)}, u32[]{:S(2)}, u32[]{:S(2)}) %collective-permute-start.10) | collective-permute-done | bytes 57376 | tf_op jit(solution)/shard_map/ppermute | solution.py:336
  27.4 0.8 %shard_map.92 = bf16[2,8,1792]{2,1,0:T(8,128)(2,1)} custom-call(f32[2,8,1792]{2,1,0:T(8,128)S(1)} %shard_map.91.base_ref, f32[2,8,16]{2,1,0:T(8,128)S(1)} %shard_map.83.table_ref, bf16[16,1792]{1,0:T(8,128)(2,1)S(1)} %collective-permute-done.10.got_ref), custom_call_target="tpu_custom_call" | custom-call | tf_op jit(solution)/shard_map/pallas_call | solution.py:237
  (25 shorter events, 0.5 us)
Async XLA Ops:
  0.0 0.9 %copy-start.3 = (bf16[2,8,3584]{2,1,0:T(8,128)(2,1)S(1)}, bf16[2,8,3584]{2,1,0:T(8,128)(2,1)}, u32[]{:S(2)}) copy-start(bf16[2,8,3584]{2,1,0:T(8,128)(2,1)} %hidden_ref.3) | copy-start | bytes 344068
  0.0 0.9 %copy-start.7 = (bf16[3584]{0:T(1024)(128)(2,1)S(1)}, bf16[3584]{0:T(1024)(128)(2,1)}, u32[]{:S(2)}) copy-start(bf16[3584]{0:T(1024)(128)(2,1)} %gain_ref.1) | copy-start | bytes 21508
  0.0 0.9 %copy-start.5 = (s32[2,8,1]{1,2,0:T(1,128)S(1)}, s32[2,8,1]{1,2,0:T(1,128)}, u32[]{:S(2)}) copy-start(s32[2,8,1]{1,2,0:T(1,128)} %param.12) | copy-start | bytes 196
  0.0 0.9 %copy-start.4 = (s32[2,8,1]{1,2,0:T(1,128)S(1)}, s32[2,8,1]{1,2,0:T(1,128)}, u32[]{:S(2)}) copy-start(s32[2,8,1]{1,2,0:T(1,128)} %param.10) | copy-start | bytes 196
  0.9 12.1 %copy-start = (bf16[3584,128]{1,0:T(8,128)(2,1)S(1)}, bf16[3584,128]{1,0:T(8,128)(2,1)}, u32[]{:S(2)}) copy-start(bf16[3584,128]{1,0:T(8,128)(2,1)} %gate_ref.1) | copy-start | bytes 2752516
  0.9 12.1 %copy-start.1 = (bf16[3584,128]{1,0:T(8,128)(2,1)S(1)}, bf16[3584,128]{1,0:T(8,128)(2,1)}, u32[]{:S(2)}) copy-start(bf16[3584,128]{1,0:T(8,128)(2,1)} %up_ref.1) | copy-start | bytes 2752516
  1.2 7.2 %collective-permute-start = (bf16[8,3584]{1,0:T(8,128)(2,1)S(1)}, bf16[8,3584]{1,0:T(8,128)(2,1)S(1)}, u32[]{:S(2)}, u32[]{:S(2)}) collective-permute-start(bf16[8,3584]{1,0:T(8,128)(2,1)S(1)} %get-tuple-element.18), channel_id=1, source_target_pairs={{0,8},{1,13},{2,10},{3,15},{4,12},{5,9},{6,14},{7,11},{8,0},{9,5},... | collective-permute-start | bytes 172040 | tf_op jit(solution)/shard_map/ppermute | solution.py:289
  5.3 4.7 %collective-permute-start.3 = (bf16[8,3584]{1,0:T(8,128)(2,1)S(1)}, bf16[8,3584]{1,0:T(8,128)(2,1)S(1)}, u32[]{:S(2)}, u32[]{:S(2)}) collective-permute-start(bf16[8,3584]{1,0:T(8,128)(2,1)S(1)} %get-tuple-element.19.refs_0_), channel_id=1, source_target_pairs={{0,4},{2,6},{4,0},{6,2},{8,12},{10,14},{12,8},{14,10},{1,5},{3,7},... | collective-permute-start | bytes 172040 | tf_op jit(solution)/shard_map/ppermute | solution.py:247
  6.9 5.1 %collective-permute-start.2 = (bf16[8,3584]{1,0:T(8,128)(2,1)S(1)}, bf16[8,3584]{1,0:T(8,128)(2,1)S(1)}, u32[]{:S(2)}, u32[]{:S(2)}) collective-permute-start(bf16[8,3584]{1,0:T(8,128)(2,1)S(1)} %get-tuple-element.19.refs_0_), channel_id=1, source_target_pairs={{0,2},{1,7},{2,0},{3,5},{4,6},{5,3},{6,4},{7,1},{8,10},{9,15},{10,... | collective-permute-start | bytes 172040 | tf_op jit(solution)/shard_map/ppermute | solution.py:289
  8.4 4.5 %collective-permute-start.1 = (bf16[8,3584]{1,0:T(8,128)(2,1)S(1)}, bf16[8,3584]{1,0:T(8,128)(2,1)S(1)}, u32[]{:S(2)}, u32[]{:S(2)}) collective-permute-start(bf16[8,3584]{1,0:T(8,128)(2,1)S(1)} %collective-permute-done.hop_ref), channel_id=1, source_target_pairs={{0,2},{2,0},{4,6},{6,4},{8,10},{10,8},{12,14},{14,12},{1,3},{3,1},... | collective-permute-start | bytes 172040 | tf_op jit(solution)/shard_map/ppermute | solution.py:247
  12.9 1.5 %copy-start.2 = (bf16[128,3584]{1,0:T(8,128)(2,1)S(1)}, bf16[128,3584]{1,0:T(8,128)(2,1)}, u32[]{:S(2)}) copy-start(bf16[128,3584]{1,0:T(8,128)(2,1)} %down_ref.1) | copy-start | bytes 2752516
  12.9 1.5 %collective-permute-start.4 = (bf16[24,3584]{1,0:T(8,128)(2,1)S(1)}, bf16[24,3584]{1,0:T(8,128)(2,1)S(1)}, u32[]{:S(2)}, u32[]{:S(2)}) collective-permute-start(bf16[24,3584]{1,0:T(8,128)(2,1)S(1)} %shard_map.85), channel_id=1, source_target_pairs={{0,1},{1,0},{2,3},{3,2},{4,5},{5,4},{6,7},{7,6},{8,9},{9,8},{10,11... | collective-permute-start | bytes 516104 | tf_op jit(solution)/shard_map/ppermute | solution.py:298
  15.0 1.6 %collective-permute-start.5 = (bf16[64,1792]{1,0:T(8,128)(2,1)S(1)}, bf16[64,1792]{1,0:T(8,128)(2,1)S(1)}, u32[]{:S(2)}, u32[]{:S(2)}) collective-permute-start(bf16[64,1792]{1,0:T(8,128)(2,1)S(1)} %get-tuple-element.22), channel_id=1, source_target_pairs={{0,1},{1,0},{2,3},{3,2},{4,5},{5,4},{6,7},{7,6},{8,9},{9,8},{10,11... | collective-permute-start | bytes 688136 | tf_op jit(solution)/shard_map/ppermute | solution.py:316
  16.7 4.2 %collective-permute-start.8 = (bf16[8,3584]{1,0:T(8,128)(2,1)S(1)}, bf16[8,3584]{1,0:T(8,128)(2,1)S(1)}, u32[]{:S(2)}, u32[]{:S(2)}) collective-permute-start(bf16[8,3584]{1,0:T(8,128)(2,1)S(1)} %get-tuple-element.27), channel_id=1, source_target_pairs={{0,2},{2,0},{4,6},{6,4},{8,10},{10,8},{12,14},{14,12},{1,3},{3,1},... | collective-permute-start | bytes 172040 | tf_op jit(solution)/shard_map/ppermute | solution.py:247
  17.8 5.5 %collective-permute-start.6 = (f32[8,1792]{1,0:T(8,128)S(1)}, f32[8,1792]{1,0:T(8,128)S(1)}, u32[]{:S(2)}, u32[]{:S(2)}) collective-permute-start(f32[8,1792]{1,0:T(8,128)S(1)} %get-tuple-element.24), channel_id=1, source_target_pairs={{0,4},{2,6},{4,0},{6,2},{8,12},{10,14},{12,8},{14,10},{1,5},{3,7},... | collective-permute-start | bytes 172040 | tf_op jit(solution)/shard_map/ppermute | solution.py:247
  19.3 4.3 %collective-permute-start.7 = (bf16[8,3584]{1,0:T(8,128)(2,1)S(1)}, bf16[8,3584]{1,0:T(8,128)(2,1)S(1)}, u32[]{:S(2)}, u32[]{:S(2)}) collective-permute-start(bf16[8,3584]{1,0:T(8,128)(2,1)S(1)} %get-tuple-element.25), channel_id=1, source_target_pairs={{0,2},{1,7},{2,0},{3,5},{4,6},{5,3},{6,4},{7,1},{8,10},{9,15},{10,... | collective-permute-start | bytes 172040 | tf_op jit(solution)/shard_map/ppermute | solution.py:289
  20.9 5.1 %collective-permute-start.9 = (bf16[8,3584]{1,0:T(8,128)(2,1)S(1)}, bf16[8,3584]{1,0:T(8,128)(2,1)S(1)}, u32[]{:S(2)}, u32[]{:S(2)}) collective-permute-start(bf16[8,3584]{1,0:T(8,128)(2,1)S(1)} %shard_map.89), channel_id=1, source_target_pairs={{0,8},{1,13},{2,10},{3,15},{4,12},{5,9},{6,14},{7,11},{8,0},{9,5},... | collective-permute-start | bytes 172040 | tf_op jit(solution)/shard_map/ppermute | solution.py:289
  26.1 0.7 %copy-start.6 = (f32[2,8,1]{1,2,0:T(1,128)S(1)}, f32[2,8,1]{1,2,0:T(1,128)}, u32[]{:S(2)}) copy-start(f32[2,8,1]{1,2,0:T(1,128)} %param.11) | copy-start | bytes 196
  26.1 1.3 %collective-permute-start.10 = (bf16[16,1792]{1,0:T(8,128)(2,1)S(1)}, bf16[16,1792]{1,0:T(8,128)(2,1)S(1)}, u32[]{:S(2)}, u32[]{:S(2)}) collective-permute-start(bf16[16,1792]{1,0:T(8,128)(2,1)S(1)} %get-tuple-element.30), channel_id=1, source_target_pairs={{0,1},{1,0},{2,3},{3,2},{4,5},{5,4},{6,7},{7,6},{8,9},{9,8},{10,11... | collective-permute-start | bytes 172040 | tf_op jit(solution)/shard_map/ppermute | solution.py:336

commit v7 on v6

--- a/solution.py
+++ b/solution.py
@@ -89,70 +89,53 @@
     down_halves(active, down_ref, keep_ref, send_ref)
 
 
-def pack_kernel(hop_ref, pass_ref, side_ref, unread_ref, out_ref):
-    out_ref[...] = jnp.concatenate(
-        [ref[...].astype(F32) for ref in (hop_ref, pass_ref, side_ref)], 0
-    ).astype(BF16)
-
-
-def shared_expert_kernel(
-    count,
-    hop_ref,
-    pass_ref,
-    other_ref,
-    gate_ref,
-    up_ref,
-    early_ref,
-    down_ref,
-    keep_ref,
-    keep_own_ref,
-    send_ref,
-    own_ref,
-):
-    core = lax.axis_index("tp")
-    half = keep_own_ref.shape[1]
-    late = hidden_units((hop_ref, pass_ref, other_ref), gate_ref, up_ref)
-    early = early_ref[...]
-    active = jnp.concatenate([late[: 2 * count], early[2 * count :], late[2 * count :]], 0)
-    active = jnp.concatenate([active, early[: 2 * count]], 0).astype(BF16)
-    product = jnp.dot(active, down_ref[...], preferred_element_type=F32)
-    keep_ref[...] = product[: 3 * count]
-    own_ref[...] = product[6 * count :]
-    keep_own_ref[...] = own_ref[:, pl.ds(pl.multiple_of(core * half, 128), half)]
-    own = own_ref[:, pl.ds(pl.multiple_of((1 - core) * half, 128), half)]
-    send = product[3 * count : 6 * count]
-    send_ref[...] = jnp.concatenate([send[:, :half], send[:, half:], own], 0).astype(BF16)
-
-
-def shared_sums_kernel(
-    keep_ref, keep_own_ref, got_ref, hop_ref, pass_ref, side_ref, own_ref, two_ref
-):
-    count, half = own_ref.shape
-    got = got_ref[...].astype(F32)
-    total = keep_ref[...] + jnp.concatenate([got[: 3 * count], got[3 * count : 6 * count]], 1)
-    hop_ref[...] = total[:count]
-    pass_ref[...] = total[count : 2 * count].astype(BF16)
-    side_ref[...] = total[2 * count :].astype(BF16)
-    own = keep_own_ref[...] + got[6 * count :]
-    own_ref[...] = own[:count]
-    two_ref[...] = own[count:]
+def own_or_rest(own, rest):
+    return jnp.where(lax.axis_index("tp") == 0, own, rest)
+
+
+def chip_product(rows, weight_refs):
+    total = 0.0
+    for gate_ref, up_ref, down_ref in (weight_refs[:3], weight_refs[3:]):
+        gate_val = jnp.dot(rows, gate_ref[...], preferred_element_type=F32)
+        up_val = jnp.dot(rows, up_ref[...], preferred_element_type=F32)
+        active = (gate_val / (1.0 + jnp.exp(-gate_val)) * up_val).astype(BF16)
+        total = total + jnp.dot(active, down_ref[...], preferred_element_type=F32)
+    return total
+
+
+def chip_early_kernel(rows_ref, *refs):
+    refs[-1][...] = chip_product(rows_ref[...], refs[:6]).astype(BF16)
+
+
+def chip_late_kernel(early_ref, hop_ref, passed_ref, own_ref, two_ref, *refs):
+    weight_refs, (hop_out, passed_out, own_out, two_out) = refs[:6], refs[6:]
+    count = hop_ref.shape[0]
+    hop, passed, own, two = (
+        ref[...].astype(F32) for ref in (hop_ref, passed_ref, own_ref, two_ref)
+    )
+    rows = jnp.concatenate([hop, passed, own_or_rest(own, two)], 0).astype(BF16)
+    total = chip_product(rows, weight_refs)
+    hop_out[...] = total[:count]
+    passed_out[...] = total[count : 2 * count].astype(BF16)
+    own_out[...] = total[2 * count :]
+    two_out[...] = total[2 * count :].astype(BF16)
 
 
 def halves_kernel(own_ref, two_ref, side_ref, back_ref, own_out, back_out, send_ref):
     core = lax.axis_index("tp")
     half = back_out.shape[1]
-    mine = pl.ds(pl.multiple_of(core * half, 128), half)
-    other = pl.ds(pl.multiple_of((1 - core) * half, 128), half)
-    own_out[...] = own_ref[...] + two_ref[...] + side_ref[:, mine].astype(F32)
-    back_out[...] = back_ref[:, mine]
-    send_ref[...] = jnp.concatenate(
-        [side_ref[:, other].astype(F32), back_ref[:, other].astype(F32)], 0
-    ).astype(BF16)
+
+    def columns(which):
+        block = pl.ds(pl.multiple_of(which * half, 128), half)
+        own = own_or_rest(own_ref[:, block], two_ref[:, block].astype(F32))
+        return own + side_ref[:, block].astype(F32), back_ref[:, block].astype(F32)
+
+    own_out[...], back_out[...] = columns(core)
+    send_ref[...] = jnp.concatenate(columns(1 - core), 0).astype(BF16)
 
 
 def base_kernel(sizes, hidden_ref, table_ref, own_ref, back_ref, out_ref):
-    own = own_ref[...]
-    back = back_ref[...].astype(F32)
+    own, back = own_ref[...], back_ref[...]
     half = out_ref.shape[2]
     columns = pl.ds(pl.multiple_of(lax.axis_index("tp") * half, 128), half)
     for m in range(hidden_ref.shape[0]):
@@ -274,10 +257,10 @@
         weights,
     )
     block = (node_size * all_rows, half)
-    hidden_block = ((3 * per_node, w_gate.shape[1]), F32)
 
     def early_rows(*pieces):
-        (early,) = call(early_kernel, [hidden_block], *pieces, w_gate, w_up, cost=4 * 10**9)
+        shape = (sum(piece.shape[0] for piece in pieces), w_gate.shape[1])
+        (early,) = call(early_kernel, [(shape, F32)], *pieces, w_gate, w_up, cost=4 * 10**9)
         return early
 
     if nodes == 2 and node_size == 4 and share_count == 2:
@@ -290,36 +273,22 @@
 
         swap = [(0, 1), (1, 0)]
         full, narrow = (per_node, model_width), (per_node, half)
+        weights = [w_gate, w_up, w_down]
+        weights += [lax.ppermute(array, "tp", swap) for array in weights]
         hop = by_core(rest, node_size, node_size ^ 2)
-        own_two, own_side = to_member(own, 2), by_core(own, 1, 3)
+        two, side = to_member(own, 2), by_core(own, 1, 3)
         passed = to_member(hop, 1)
-        early = early_rows(own, own_two, own_side)
-        (packed,) = call(pack_kernel, [((3 * per_node, model_width), BF16)], hop, passed, own_side, own_two)
-        other = lax.ppermute(packed, "tp", swap)
-        keep, keep_own, send = call(
-            functools.partial(shared_expert_kernel, per_node),
-            [
-                ((3 * per_node, model_width), F32),
-                ((2 * per_node, half), F32),
-                ((8 * per_node, half), BF16),
-            ],
+        (side,) = call(chip_early_kernel, [(full, BF16)], side, *weights, cost=4 * 10**9)
+        hop, passed, own, two = call(
+            chip_late_kernel,
+            [(full, F32), (full, BF16), (full, F32), (full, BF16)],
+            side,
             hop,
             passed,
-            other,
-            w_gate,
-            w_up,
-            early,
-            w_down,
-            scratch=[pltpu.VMEM((2 * per_node, model_width), F32)],
+            own,
+            two,
+            *weights,
             cost=10**6,
-        )
-        got = lax.ppermute(send, "tp", swap)
-        hop, passed, side, own, two = call(
-            shared_sums_kernel,
-            [(full, F32), (full, BF16), (full, BF16), (narrow, F32), (narrow, F32)],
-            keep,
-            keep_own,
-            got,
         )
         passed = to_member(passed, 1)
         side, two = by_core(side, 1, 3), to_member(two, 2)
@@ -327,7 +296,7 @@
         back = by_core(outbox, node_size, node_size ^ 2)
         own, back, send = call(
             halves_kernel,
-            [(narrow, F32), (narrow, BF16), ((2 * per_node, half), BF16)],
+            [(narrow, F32), (narrow, F32), ((2 * per_node, half), BF16)],
             own,
             two,
             side,

time: 28.3 us -> 27.4 us (0.968)
  waiting for transfers between devices: 9.74 us -> 7.78 us
  Pallas kernels: 2.47 us -> 3.24 us
  starting transfers between devices: 14.3 us -> 14.9 us
    ppermute x2 -> x1, waiting for transfers between devices: 1.74 us -> 0.41 us  [per_device(): got = lax.ppermute(send, 'tp', swap)]
    ppermute x1 -> x3, waiting for transfers between devices: 0.99 us -> 0.01 us  [per_device(): weights += [lax.ppermute(array, 'tp', swap) for array in weights]]
    ppermute x1 -> x3, starting transfers between devices: 0.07 us -> 0.96 us  [per_device(): weights += [lax.ppermute(array, 'tp', swap) for array in weights]]
    pallas_call x11 -> x9, Pallas kernels: 2.47 us -> 3.24 us  [call(): pl.pallas_call(kernel, out_shape=[jax.ShapeDtypeStruct(shape, kind) for s...]
    ppermute x4, starting transfers between devices: 5.59 us -> 4.95 us  [to_member(): return lax.ppermute(array, 'ep', pairs)]
    ppermute x4, waiting for transfers between devices: 2.27 us -> 2.8 us  [to_member(): return lax.ppermute(array, 'ep', pairs)]
    ppermute x4, starting transfers between devices: 8.4 us -> 8.88 us  [by_core(): return lax.ppermute(array, ('ep', 'tp'), pairs)]
  transfers between devices with their start and end apart: 11 -> 12, of which waited for: 9 -> 6; matrix products, arithmetic and copies ran while one was open for 0% -> 0% of each run, Pallas kernels for 2% -> 5%
where the time goes in v7:
time: 27.4 us; the launch traced here: 27.3 us
  starting transfers between devices  14.9 us (54%)
  waiting for transfers between devices  7.78 us (28%)
  Pallas kernels  3.24 us (12%)
  local copies, waits for them, and re-layouts  1.29 us (5%)
    ppermute x4, starting transfers between devices, by_core(): return lax.ppermute(array, ('ep', 'tp'), pairs)  8.88 us
    ppermute x4, starting transfers between devices, to_member(): return lax.ppermute(array, 'ep', pairs)  4.95 us
    ppermute x4, waiting for transfers between devices, by_core(): return lax.ppermute(array, ('ep', 'tp'), pairs)  4.56 us
    pallas_call x9, Pallas kernels, call(): pl.pallas_call(kernel, out_shape=[jax.ShapeDtypeStruct(shape, kind) for s...  3.24 us
    ppermute x4, waiting for transfers between devices, to_member(): return lax.ppermute(array, 'ep', pairs)  2.8 us
    unnamed x16, local copies, waits for them, and re-layouts  1.29 us
    ppermute x3, starting transfers between devices, per_device(): weights += [lax.ppermute(array, 'tp', swap) for array in weights]  0.96 us
  transfers between devices with their start and end apart: 12, of which 6 were waited for; matrix products, arithmetic and copies ran while one was open for 0% of the time, Pallas kernels for 5%

profile of v7, /device:TPU:0, one launch (start us, length us, event | category | flops | bytes accessed | tf_op | source)
XLA Modules:
  0.0 27.3 jit_solution(15786590946628522483)
XLA Ops:
  0.0 0.5 %collective-permute-start.1 = (bf16[3584,128]{1,0:T(8,128)(2,1)}, bf16[3584,128]{1,0:T(8,128)(2,1)S(1)}, u32[]{:S(2)}, u32[]{:S(2)}) collective-permute-start(bf16[3584,128]{1,0:T(8,128)(2,1)} %refs_0_.3), channel_id=1, source_target_pairs={{0,1},{1,0},{2,3},{3,2},{4,5},{5,4},{6,7},{7,6},{8,9},{9,8},{10,11... | collective-permute-start | bytes 2752520 | tf_op jit(solution)/shard_map/ppermute | solution.py:277
  0.5 0.4 %collective-permute-start.3 = (bf16[128,3584]{1,0:T(8,128)(2,1)}, bf16[128,3584]{1,0:T(8,128)(2,1)S(1)}, u32[]{:S(2)}, u32[]{:S(2)}) collective-permute-start(bf16[128,3584]{1,0:T(8,128)(2,1)} %refs_2_.3), channel_id=1, source_target_pairs={{0,1},{1,0},{2,3},{3,2},{4,5},{5,4},{6,7},{7,6},{8,9},{9,8},{10,11... | collective-permute-start | bytes 2752520 | tf_op jit(solution)/shard_map/ppermute | solution.py:277
  1.0 0.7 %copy-done.5 = s32[2,8,1]{1,2,0:T(1,128)S(1)} copy-done((s32[2,8,1]{1,2,0:T(1,128)S(1)}, s32[2,8,1]{1,2,0:T(1,128)}, u32[]{:S(2)}) %copy-start.5) | copy-done | bytes 88
  1.7 0.3 %shard_map.84 = (bf16[8,3584]{1,0:T(8,128)(2,1)S(1)}, bf16[8,3584]{1,0:T(8,128)(2,1)S(1)}) custom-call(s32[16,8]{1,0:T(8,128)S(1)} %shard_map.82.slot_ref, bf16[2,8,3584]{2,1,0:T(8,128)(2,1)S(1)} %copy-done.3, bf16[3584]{0:T(1024)(128)(2,1)S(1)} %copy-done.7, s32[2,1,8]{2,1,0:T(1,128)S(1)} %bitcast.9, s32[2,1,8]{2,1,0:T(1,128)S(1)} %bitcast.11), custom_call_target="tpu_custom_call" | custom-call | flops 20000000000 | bytes 40000000 | tf_op jit(solution)/shard_map/pallas_call | solution.py:220
  2.0 3.7 %collective-permute-start.4 = (bf16[8,3584]{1,0:T(8,128)(2,1)S(1)}, bf16[8,3584]{1,0:T(8,128)(2,1)S(1)}, u32[]{:S(2)}, u32[]{:S(2)}) collective-permute-start(bf16[8,3584]{1,0:T(8,128)(2,1)S(1)} %get-tuple-element.15), channel_id=1, source_target_pairs={{0,8},{1,13},{2,10},{3,15},{4,12},{5,9},{6,14},{7,11},{8,0},{9,5},... | collective-permute-start | bytes 172040 | tf_op jit(solution)/shard_map/ppermute | solution.py:272
  5.7 1.5 %collective-permute-start = (bf16[8,3584]{1,0:T(8,128)(2,1)S(1)}, bf16[8,3584]{1,0:T(8,128)(2,1)S(1)}, u32[]{:S(2)}, u32[]{:S(2)}) collective-permute-start(bf16[8,3584]{1,0:T(8,128)(2,1)S(1)} %get-tuple-element.14.own_ref), channel_id=1, source_target_pairs={{0,2},{1,7},{2,0},{3,5},{4,6},{5,3},{6,4},{7,1},{8,10},{9,15},{10,... | collective-permute-start | bytes 172040 | tf_op jit(solution)/shard_map/ppermute | solution.py:272
  7.2 2.4 %collective-permute-done.4.hop_ref = bf16[8,3584]{1,0:T(8,128)(2,1)S(1)} collective-permute-done((bf16[8,3584]{1,0:T(8,128)(2,1)S(1)}, bf16[8,3584]{1,0:T(8,128)(2,1)S(1)}, u32[]{:S(2)}, u32[]{:S(2)}) %collective-permute-start.4) | collective-permute-done | bytes 57376 | tf_op jit(solution)/shard_map/ppermute | solution.py:272
  9.6 0.5 %collective-permute-start.6 = (bf16[8,3584]{1,0:T(8,128)(2,1)S(1)}, bf16[8,3584]{1,0:T(8,128)(2,1)S(1)}, u32[]{:S(2)}, u32[]{:S(2)}) collective-permute-start(bf16[8,3584]{1,0:T(8,128)(2,1)S(1)} %get-tuple-element.14.own_ref), channel_id=1, source_target_pairs={{0,4},{2,6},{4,0},{6,2},{8,12},{10,14},{12,8},{14,10},{1,5},{3,7},... | collective-permute-start | bytes 172040 | tf_op jit(solution)/shard_map/ppermute | solution.py:230
  10.1 1.7 %collective-permute-start.5 = (bf16[8,3584]{1,0:T(8,128)(2,1)S(1)}, bf16[8,3584]{1,0:T(8,128)(2,1)S(1)}, u32[]{:S(2)}, u32[]{:S(2)}) collective-permute-start(bf16[8,3584]{1,0:T(8,128)(2,1)S(1)} %collective-permute-done.4.hop_ref), channel_id=1, source_target_pairs={{0,2},{2,0},{4,6},{6,4},{8,10},{10,8},{12,14},{14,12},{1,3},{3,1},... | collective-permute-start | bytes 172040 | tf_op jit(solution)/shard_map/ppermute | solution.py:230
  11.9 0.9 %shard_map.85.early_ref = bf16[8,3584]{1,0:T(8,128)(2,1)S(1)} custom-call(bf16[8,3584]{1,0:T(8,128)(2,1)S(1)} %collective-permute-done.rows_ref, bf16[3584,128]{1,0:T(8,128)(2,1)S(1)} %copy-done, bf16[3584,128]{1,0:T(8,128)(2,1)S(1)} %copy-done.1, bf16[128,3584]{1,0:T(8,128)(2,1)S(1)} %copy-done.2, bf16[3584,128]{1,0:T(8,128)(2,1)S(1)} %collective-permute-done.1.refs_3_, ...), custom_call_target="tpu_custom_call" | custom-call | flops 4000000000 | bytes 8000000 | tf_op jit(solution)/shard_map/pallas_call | solution.py:220
  12.8 1.0 %collective-permute-done.6.two_ref = bf16[8,3584]{1,0:T(8,128)(2,1)S(1)} collective-permute-done((bf16[8,3584]{1,0:T(8,128)(2,1)S(1)}, bf16[8,3584]{1,0:T(8,128)(2,1)S(1)}, u32[]{:S(2)}, u32[]{:S(2)}) %collective-permute-start.6) | collective-permute-done | bytes 57376 | tf_op jit(solution)/shard_map/ppermute | solution.py:230
  13.8 0.8 %collective-permute-done.5.passed_ref = bf16[8,3584]{1,0:T(8,128)(2,1)S(1)} collective-permute-done((bf16[8,3584]{1,0:T(8,128)(2,1)S(1)}, bf16[8,3584]{1,0:T(8,128)(2,1)S(1)}, u32[]{:S(2)}, u32[]{:S(2)}) %collective-permute-start.5) | collective-permute-done | bytes 57376 | tf_op jit(solution)/shard_map/ppermute | solution.py:230
  14.6 1.0 %shard_map.86 = (f32[8,3584]{1,0:T(8,128)S(1)}, bf16[8,3584]{1,0:T(8,128)(2,1)S(1)}, f32[8,3584]{1,0:T(8,128)S(1)}, bf16[8,3584]{1,0:T(8,128)(2,1)S(1)}) custom-call(bf16[8,3584]{1,0:T(8,128)(2,1)S(1)} %shard_map.85.early_ref, bf16[8,3584]{1,0:T(8,128)(2,1)S(1)} %collective-permute-done.4.hop_ref, bf16[8,3584]{1,0:T(8,128)(2,1)S(1)} %collective-permute-done.5.passed_ref, ...), custom_call_target="tpu_custom_call" | custom-call | flops 1000000 | bytes 2000 | tf_op jit(solution)/shard_map/pallas_call | solution.py:220
  15.6 1.5 %collective-permute-start.9 = (bf16[8,3584]{1,0:T(8,128)(2,1)S(1)}, bf16[8,3584]{1,0:T(8,128)(2,1)S(1)}, u32[]{:S(2)}, u32[]{:S(2)}) collective-permute-start(bf16[8,3584]{1,0:T(8,128)(2,1)S(1)} %get-tuple-element.19), channel_id=1, source_target_pairs={{0,2},{2,0},{4,6},{6,4},{8,10},{10,8},{12,14},{14,12},{1,3},{3,1},... | collective-permute-start | bytes 172040 | tf_op jit(solution)/shard_map/ppermute | solution.py:230
  17.2 0.5 %collective-permute-start.8 = (bf16[8,3584]{1,0:T(8,128)(2,1)S(1)}, bf16[8,3584]{1,0:T(8,128)(2,1)S(1)}, u32[]{:S(2)}, u32[]{:S(2)}) collective-permute-start(bf16[8,3584]{1,0:T(8,128)(2,1)S(1)} %shard_map.85.early_ref), channel_id=1, source_target_pairs={{0,2},{1,7},{2,0},{3,5},{4,6},{5,3},{6,4},{7,1},{8,10},{9,15},{10,... | collective-permute-start | bytes 172040 | tf_op jit(solution)/shard_map/ppermute | solution.py:272
  17.7 1.2 %collective-permute-start.7 = (bf16[8,3584]{1,0:T(8,128)(2,1)S(1)}, bf16[8,3584]{1,0:T(8,128)(2,1)S(1)}, u32[]{:S(2)}, u32[]{:S(2)}) collective-permute-start(bf16[8,3584]{1,0:T(8,128)(2,1)S(1)} %get-tuple-element.17), channel_id=1, source_target_pairs={{0,4},{2,6},{4,0},{6,2},{8,12},{10,14},{12,8},{14,10},{1,5},{3,7},... | collective-permute-start | bytes 172040 | tf_op jit(solution)/shard_map/ppermute | solution.py:230
  18.9 1.0 %collective-permute-done.9.refs_1_ = bf16[8,3584]{1,0:T(8,128)(2,1)S(1)} collective-permute-done((bf16[8,3584]{1,0:T(8,128)(2,1)S(1)}, bf16[8,3584]{1,0:T(8,128)(2,1)S(1)}, u32[]{:S(2)}, u32[]{:S(2)}) %collective-permute-start.9) | collective-permute-done | bytes 57376 | tf_op jit(solution)/shard_map/ppermute | solution.py:230
  19.9 3.1 %collective-permute-start.10 = (bf16[8,3584]{1,0:T(8,128)(2,1)S(1)}, bf16[8,3584]{1,0:T(8,128)(2,1)S(1)}, u32[]{:S(2)}, u32[]{:S(2)}) collective-permute-start(bf16[8,3584]{1,0:T(8,128)(2,1)S(1)} %shard_map.87), channel_id=1, source_target_pairs={{0,8},{1,13},{2,10},{3,15},{4,12},{5,9},{6,14},{7,11},{8,0},{9,5},... | collective-permute-start | bytes 172040 | tf_op jit(solution)/shard_map/ppermute | solution.py:272
  23.0 2.2 %collective-permute-done.10.back_ref = bf16[8,3584]{1,0:T(8,128)(2,1)S(1)} collective-permute-done((bf16[8,3584]{1,0:T(8,128)(2,1)S(1)}, bf16[8,3584]{1,0:T(8,128)(2,1)S(1)}, u32[]{:S(2)}, u32[]{:S(2)}) %collective-permute-start.10) | collective-permute-done | bytes 57376 | tf_op jit(solution)/shard_map/ppermute | solution.py:272
  25.3 0.6 %copy-done.6 = f32[2,8,1]{1,2,0:T(1,128)S(1)} copy-done((f32[2,8,1]{1,2,0:T(1,128)S(1)}, f32[2,8,1]{1,2,0:T(1,128)}, u32[]{:S(2)}) %copy-start.6) | copy-done | bytes 88
  25.8 0.1 shard_map.83.table_ref
  25.9 0.1 shard_map.89.base_ref
  26.1 0.4 %collective-permute-done.11.got_ref = bf16[16,1792]{1,0:T(8,128)(2,1)S(1)} collective-permute-done((bf16[16,1792]{1,0:T(8,128)(2,1)S(1)}, bf16[16,1792]{1,0:T(8,128)(2,1)S(1)}, u32[]{:S(2)}, u32[]{:S(2)}) %collective-permute-start.11) | collective-permute-done | bytes 57376 | tf_op jit(solution)/shard_map/ppermute | solution.py:305
  26.5 0.8 %shard_map.90 = bf16[2,8,1792]{2,1,0:T(8,128)(2,1)} custom-call(f32[2,8,1792]{2,1,0:T(8,128)S(1)} %shard_map.89.base_ref, f32[2,8,16]{2,1,0:T(8,128)S(1)} %shard_map.83.table_ref, bf16[16,1792]{1,0:T(8,128)(2,1)S(1)} %collective-permute-done.11.got_ref), custom_call_target="tpu_custom_call" | custom-call | tf_op jit(solution)/shard_map/pallas_call | solution.py:220
  (25 shorter events, 0.3 us)
Async XLA Ops:
  0.0 1.0 %copy-start.3 = (bf16[2,8,3584]{2,1,0:T(8,128)(2,1)S(1)}, bf16[2,8,3584]{2,1,0:T(8,128)(2,1)}, u32[]{:S(2)}) copy-start(bf16[2,8,3584]{2,1,0:T(8,128)(2,1)} %hidden_ref.3) | copy-start | bytes 344068
  0.0 1.0 %copy-start.7 = (bf16[3584]{0:T(1024)(128)(2,1)S(1)}, bf16[3584]{0:T(1024)(128)(2,1)}, u32[]{:S(2)}) copy-start(bf16[3584]{0:T(1024)(128)(2,1)} %gain_ref.1) | copy-start | bytes 21508
  0.0 11.8 %collective-permute-start.1 = (bf16[3584,128]{1,0:T(8,128)(2,1)}, bf16[3584,128]{1,0:T(8,128)(2,1)S(1)}, u32[]{:S(2)}, u32[]{:S(2)}) collective-permute-start(bf16[3584,128]{1,0:T(8,128)(2,1)} %refs_0_.3), channel_id=1, source_target_pairs={{0,1},{1,0},{2,3},{3,2},{4,5},{5,4},{6,7},{7,6},{8,9},{9,8},{10,11... | collective-permute-start | bytes 2752520 | tf_op jit(solution)/shard_map/ppermute | solution.py:277
  0.5 11.4 %collective-permute-start.2 = (bf16[3584,128]{1,0:T(8,128)(2,1)}, bf16[3584,128]{1,0:T(8,128)(2,1)S(1)}, u32[]{:S(2)}, u32[]{:S(2)}) collective-permute-start(bf16[3584,128]{1,0:T(8,128)(2,1)} %refs_1_.3), channel_id=1, source_target_pairs={{0,1},{1,0},{2,3},{3,2},{4,5},{5,4},{6,7},{7,6},{8,9},{9,8},{10,11... | collective-permute-start | bytes 2752520 | tf_op jit(solution)/shard_map/ppermute | solution.py:277
  0.5 11.3 %collective-permute-start.3 = (bf16[128,3584]{1,0:T(8,128)(2,1)}, bf16[128,3584]{1,0:T(8,128)(2,1)S(1)}, u32[]{:S(2)}, u32[]{:S(2)}) collective-permute-start(bf16[128,3584]{1,0:T(8,128)(2,1)} %refs_2_.3), channel_id=1, source_target_pairs={{0,1},{1,0},{2,3},{3,2},{4,5},{5,4},{6,7},{7,6},{8,9},{9,8},{10,11... | collective-permute-start | bytes 2752520 | tf_op jit(solution)/shard_map/ppermute | solution.py:277
  1.0 0.7 %copy-start.5 = (s32[2,8,1]{1,2,0:T(1,128)S(1)}, s32[2,8,1]{1,2,0:T(1,128)}, u32[]{:S(2)}) copy-start(s32[2,8,1]{1,2,0:T(1,128)} %param.12) | copy-start | bytes 196
  1.0 0.7 %copy-start.4 = (s32[2,8,1]{1,2,0:T(1,128)S(1)}, s32[2,8,1]{1,2,0:T(1,128)}, u32[]{:S(2)}) copy-start(s32[2,8,1]{1,2,0:T(1,128)} %param.10) | copy-start | bytes 196
  1.7 10.2 %copy-start = (bf16[3584,128]{1,0:T(8,128)(2,1)S(1)}, bf16[3584,128]{1,0:T(8,128)(2,1)}, u32[]{:S(2)}) copy-start(bf16[3584,128]{1,0:T(8,128)(2,1)} %refs_0_.3) | copy-start | bytes 2752516
  1.7 10.2 %copy-start.1 = (bf16[3584,128]{1,0:T(8,128)(2,1)S(1)}, bf16[3584,128]{1,0:T(8,128)(2,1)}, u32[]{:S(2)}) copy-start(bf16[3584,128]{1,0:T(8,128)(2,1)} %refs_1_.3) | copy-start | bytes 2752516
  1.7 10.2 %copy-start.2 = (bf16[128,3584]{1,0:T(8,128)(2,1)S(1)}, bf16[128,3584]{1,0:T(8,128)(2,1)}, u32[]{:S(2)}) copy-start(bf16[128,3584]{1,0:T(8,128)(2,1)} %refs_2_.3) | copy-start | bytes 2752516
  2.0 7.6 %collective-permute-start.4 = (bf16[8,3584]{1,0:T(8,128)(2,1)S(1)}, bf16[8,3584]{1,0:T(8,128)(2,1)S(1)}, u32[]{:S(2)}, u32[]{:S(2)}) collective-permute-start(bf16[8,3584]{1,0:T(8,128)(2,1)S(1)} %get-tuple-element.15), channel_id=1, source_target_pairs={{0,8},{1,13},{2,10},{3,15},{4,12},{5,9},{6,14},{7,11},{8,0},{9,5},... | collective-permute-start | bytes 172040 | tf_op jit(solution)/shard_map/ppermute | solution.py:272
  5.7 4.4 %collective-permute-start = (bf16[8,3584]{1,0:T(8,128)(2,1)S(1)}, bf16[8,3584]{1,0:T(8,128)(2,1)S(1)}, u32[]{:S(2)}, u32[]{:S(2)}) collective-permute-start(bf16[8,3584]{1,0:T(8,128)(2,1)S(1)} %get-tuple-element.14.own_ref), channel_id=1, source_target_pairs={{0,2},{1,7},{2,0},{3,5},{4,6},{5,3},{6,4},{7,1},{8,10},{9,15},{10,... | collective-permute-start | bytes 172040 | tf_op jit(solution)/shard_map/ppermute | solution.py:272
  9.6 4.2 %collective-permute-start.6 = (bf16[8,3584]{1,0:T(8,128)(2,1)S(1)}, bf16[8,3584]{1,0:T(8,128)(2,1)S(1)}, u32[]{:S(2)}, u32[]{:S(2)}) collective-permute-start(bf16[8,3584]{1,0:T(8,128)(2,1)S(1)} %get-tuple-element.14.own_ref), channel_id=1, source_target_pairs={{0,4},{2,6},{4,0},{6,2},{8,12},{10,14},{12,8},{14,10},{1,5},{3,7},... | collective-permute-start | bytes 172040 | tf_op jit(solution)/shard_map/ppermute | solution.py:230
  10.1 4.5 %collective-permute-start.5 = (bf16[8,3584]{1,0:T(8,128)(2,1)S(1)}, bf16[8,3584]{1,0:T(8,128)(2,1)S(1)}, u32[]{:S(2)}, u32[]{:S(2)}) collective-permute-start(bf16[8,3584]{1,0:T(8,128)(2,1)S(1)} %collective-permute-done.4.hop_ref), channel_id=1, source_target_pairs={{0,2},{2,0},{4,6},{6,4},{8,10},{10,8},{12,14},{14,12},{1,3},{3,1},... | collective-permute-start | bytes 172040 | tf_op jit(solution)/shard_map/ppermute | solution.py:230
  15.6 4.2 %collective-permute-start.9 = (bf16[8,3584]{1,0:T(8,128)(2,1)S(1)}, bf16[8,3584]{1,0:T(8,128)(2,1)S(1)}, u32[]{:S(2)}, u32[]{:S(2)}) collective-permute-start(bf16[8,3584]{1,0:T(8,128)(2,1)S(1)} %get-tuple-element.19), channel_id=1, source_target_pairs={{0,2},{2,0},{4,6},{6,4},{8,10},{10,8},{12,14},{14,12},{1,3},{3,1},... | collective-permute-start | bytes 172040 | tf_op jit(solution)/shard_map/ppermute | solution.py:230
  17.2 5.8 %collective-permute-start.8 = (bf16[8,3584]{1,0:T(8,128)(2,1)S(1)}, bf16[8,3584]{1,0:T(8,128)(2,1)S(1)}, u32[]{:S(2)}, u32[]{:S(2)}) collective-permute-start(bf16[8,3584]{1,0:T(8,128)(2,1)S(1)} %shard_map.85.early_ref), channel_id=1, source_target_pairs={{0,2},{1,7},{2,0},{3,5},{4,6},{5,3},{6,4},{7,1},{8,10},{9,15},{10,... | collective-permute-start | bytes 172040 | tf_op jit(solution)/shard_map/ppermute | solution.py:272
  17.7 5.3 %collective-permute-start.7 = (bf16[8,3584]{1,0:T(8,128)(2,1)S(1)}, bf16[8,3584]{1,0:T(8,128)(2,1)S(1)}, u32[]{:S(2)}, u32[]{:S(2)}) collective-permute-start(bf16[8,3584]{1,0:T(8,128)(2,1)S(1)} %get-tuple-element.17), channel_id=1, source_target_pairs={{0,4},{2,6},{4,0},{6,2},{8,12},{10,14},{12,8},{14,10},{1,5},{3,7},... | collective-permute-start | bytes 172040 | tf_op jit(solution)/shard_map/ppermute | solution.py:230
  19.9 5.3 %collective-permute-start.10 = (bf16[8,3584]{1,0:T(8,128)(2,1)S(1)}, bf16[8,3584]{1,0:T(8,128)(2,1)S(1)}, u32[]{:S(2)}, u32[]{:S(2)}) collective-permute-start(bf16[8,3584]{1,0:T(8,128)(2,1)S(1)} %shard_map.87), channel_id=1, source_target_pairs={{0,8},{1,13},{2,10},{3,15},{4,12},{5,9},{6,14},{7,11},{8,0},{9,5},... | collective-permute-start | bytes 172040 | tf_op jit(solution)/shard_map/ppermute | solution.py:272
  25.2 0.7 %copy-start.6 = (f32[2,8,1]{1,2,0:T(1,128)S(1)}, f32[2,8,1]{1,2,0:T(1,128)}, u32[]{:S(2)}) copy-start(f32[2,8,1]{1,2,0:T(1,128)} %param.11) | copy-start | bytes 196
  25.2 1.3 %collective-permute-start.11 = (bf16[16,1792]{1,0:T(8,128)(2,1)S(1)}, bf16[16,1792]{1,0:T(8,128)(2,1)S(1)}, u32[]{:S(2)}, u32[]{:S(2)}) collective-permute-start(bf16[16,1792]{1,0:T(8,128)(2,1)S(1)} %get-tuple-element.22), channel_id=1, source_target_pairs={{0,1},{1,0},{2,3},{3,2},{4,5},{5,4},{6,7},{7,6},{8,9},{9,8},{10,11... | collective-permute-start | bytes 172040 | tf_op jit(solution)/shard_map/ppermute | solution.py:305

commit v8 on v7

--- a/solution.py
+++ b/solution.py
@@ -23,6 +23,10 @@
 
 def slots_kernel(slot_ref):
     slot_ref[...] = lax.broadcasted_iota(jnp.int32, slot_ref.shape, 0)
+
+
+def pass_kernel(in_ref, out_ref):
+    out_ref[...] = in_ref[...]
 
 
 def dispatch_kernel(
@@ -103,22 +107,19 @@
     return total
 
 
-def chip_early_kernel(rows_ref, *refs):
-    refs[-1][...] = chip_product(rows_ref[...], refs[:6]).astype(BF16)
-
-
-def chip_late_kernel(early_ref, hop_ref, passed_ref, own_ref, two_ref, *refs):
-    weight_refs, (hop_out, passed_out, own_out, two_out) = refs[:6], refs[6:]
+def chip_kernel(hop_ref, passed_ref, side_ref, own_ref, two_ref, *refs):
+    weight_refs, (hop_out, passed_out, side_out, own_out, two_out) = refs[:6], refs[6:]
     count = hop_ref.shape[0]
-    hop, passed, own, two = (
-        ref[...].astype(F32) for ref in (hop_ref, passed_ref, own_ref, two_ref)
-    )
-    rows = jnp.concatenate([hop, passed, own_or_rest(own, two)], 0).astype(BF16)
+    hop, passed, side, own, two = (
+        ref[...].astype(F32) for ref in (hop_ref, passed_ref, side_ref, own_ref, two_ref)
+    )
+    rows = jnp.concatenate([hop, passed, side, own_or_rest(own, two)], 0).astype(BF16)
     total = chip_product(rows, weight_refs)
     hop_out[...] = total[:count]
     passed_out[...] = total[count : 2 * count].astype(BF16)
-    own_out[...] = total[2 * count :]
-    two_out[...] = total[2 * count :].astype(BF16)
+    side_out[...] = total[2 * count : 3 * count].astype(BF16)
+    own_out[...] = total[3 * count :]
+    two_out[...] = total[3 * count :].astype(BF16)
 
 
 def halves_kernel(own_ref, two_ref, side_ref, back_ref, own_out, back_out, send_ref):
@@ -277,14 +278,14 @@
         weights += [lax.ppermute(array, "tp", swap) for array in weights]
         hop = by_core(rest, node_size, node_size ^ 2)
         two, side = to_member(own, 2), by_core(own, 1, 3)
+        (hop,) = call(pass_kernel, [(full, BF16)], hop, cost=20 * 10**9)
         passed = to_member(hop, 1)
-        (side,) = call(chip_early_kernel, [(full, BF16)], side, *weights, cost=4 * 10**9)
-        hop, passed, own, two = call(
-            chip_late_kernel,
-            [(full, F32), (full, BF16), (full, F32), (full, BF16)],
-            side,
+        hop, passed, side, own, two = call(
+            chip_kernel,
+            [(full, F32), (full, BF16), (full, BF16), (full, F32), (full, BF16)],
             hop,
             passed,
+            side,
             own,
             two,
             *weights,

time: 27.4 us -> 27.5 us (level)
  waiting for transfers between devices: 7.78 us -> 10 us
  starting transfers between devices: 14.9 us -> 13.4 us
  Pallas kernels: 3.24 us -> 2.34 us
    ppermute x4, starting transfers between devices: 8.88 us -> 6.39 us  [by_core(): return lax.ppermute(array, ('ep', 'tp'), pairs)]
    ppermute x4, waiting for transfers between devices: 2.8 us -> 5.21 us  [to_member(): return lax.ppermute(array, 'ep', pairs)]
    ppermute x4, starting transfers between devices: 4.95 us -> 6.38 us  [to_member(): return lax.ppermute(array, 'ep', pairs)]
    pallas_call x9, Pallas kernels: 3.24 us -> 2.34 us  [call(): pl.pallas_call(kernel, out_shape=[jax.ShapeDtypeStruct(shape, kind) for s...]
    ppermute x3, starting transfers between devices: 0.96 us -> 0.59 us  [per_device(): weights += [lax.ppermute(array, 'tp', swap) for array in weights]]
  transfers between devices with their start and end apart: 12 -> 12, of which waited for: 6 -> 8; matrix products, arithmetic and copies ran while one was open for 0% -> 0% of each run, Pallas kernels for 5% -> 1%
where the time goes in v8:
time: 27.5 us; the launch traced here: 27.4 us
  starting transfers between devices  13.4 us (49%)
  waiting for transfers between devices  10 us (36%)
  Pallas kernels  2.34 us (9%)
  local copies, waits for them, and re-layouts  1.5 us (5%)
    ppermute x4, starting transfers between devices, by_core(): return lax.ppermute(array, ('ep', 'tp'), pairs)  6.39 us
    ppermute x4, starting transfers between devices, to_member(): return lax.ppermute(array, 'ep', pairs)  6.38 us
    ppermute x4, waiting for transfers between devices, to_member(): return lax.ppermute(array, 'ep', pairs)  5.21 us
    ppermute x4, waiting for transfers between devices, by_core(): return lax.ppermute(array, ('ep', 'tp'), pairs)  4.38 us
    pallas_call x9, Pallas kernels, call(): pl.pallas_call(kernel, out_shape=[jax.ShapeDtypeStruct(shape, kind) for s...  2.34 us
    unnamed x16, local copies, waits for them, and re-layouts  1.5 us
    ppermute x3, starting transfers between devices, per_device(): weights += [lax.ppermute(array, 'tp', swap) for array in weights]  0.59 us
  transfers between devices with their start and end apart: 12, of which 8 were waited for; matrix products, arithmetic and copies ran while one was open for 0% of the time, Pallas kernels for 1%

profile of v8, /device:TPU:0, one launch (start us, length us, event | category | flops | bytes accessed | tf_op | source)
XLA Modules:
  0.0 27.4 jit_solution(6839976878375276037)
XLA Ops:
  0.0 0.9 %copy-done.3 = bf16[2,8,3584]{2,1,0:T(8,128)(2,1)S(1)} copy-done((bf16[2,8,3584]{2,1,0:T(8,128)(2,1)S(1)}, bf16[2,8,3584]{2,1,0:T(8,128)(2,1)}, u32[]{:S(2)}) %copy-start.3) | copy-done | bytes 114712
  0.9 0.3 %shard_map.84 = (bf16[8,3584]{1,0:T(8,128)(2,1)S(1)}, bf16[8,3584]{1,0:T(8,128)(2,1)S(1)}) custom-call(s32[16,8]{1,0:T(8,128)S(1)} %shard_map.82.slot_ref, bf16[2,8,3584]{2,1,0:T(8,128)(2,1)S(1)} %copy-done.3, bf16[3584]{0:T(1024)(128)(2,1)S(1)} %copy-done.7, s32[2,1,8]{2,1,0:T(1,128)S(1)} %bitcast.9, s32[2,1,8]{2,1,0:T(1,128)S(1)} %bitcast.11), custom_call_target="tpu_custom_call" | custom-call | flops 20000000000 | bytes 40000000 | tf_op jit(solution)/shard_map/pallas_call | solution.py:221
  1.3 4.1 %collective-permute-start = (bf16[8,3584]{1,0:T(8,128)(2,1)S(1)}, bf16[8,3584]{1,0:T(8,128)(2,1)S(1)}, u32[]{:S(2)}, u32[]{:S(2)}) collective-permute-start(bf16[8,3584]{1,0:T(8,128)(2,1)S(1)} %get-tuple-element.15), channel_id=1, source_target_pairs={{0,8},{1,13},{2,10},{3,15},{4,12},{5,9},{6,14},{7,11},{8,0},{9,5},... | collective-permute-start | bytes 172040 | tf_op jit(solution)/shard_map/ppermute | solution.py:273
  5.4 1.6 %collective-permute-start.3 = (bf16[8,3584]{1,0:T(8,128)(2,1)S(1)}, bf16[8,3584]{1,0:T(8,128)(2,1)S(1)}, u32[]{:S(2)}, u32[]{:S(2)}) collective-permute-start(bf16[8,3584]{1,0:T(8,128)(2,1)S(1)} %get-tuple-element.16.own_ref), channel_id=1, source_target_pairs={{0,4},{2,6},{4,0},{6,2},{8,12},{10,14},{12,8},{14,10},{1,5},{3,7},... | collective-permute-start | bytes 172040 | tf_op jit(solution)/shard_map/ppermute | solution.py:231
  6.9 1.5 %collective-permute-start.2 = (bf16[8,3584]{1,0:T(8,128)(2,1)S(1)}, bf16[8,3584]{1,0:T(8,128)(2,1)S(1)}, u32[]{:S(2)}, u32[]{:S(2)}) collective-permute-start(bf16[8,3584]{1,0:T(8,128)(2,1)S(1)} %get-tuple-element.16.own_ref), channel_id=1, source_target_pairs={{0,2},{1,7},{2,0},{3,5},{4,6},{5,3},{6,4},{7,1},{8,10},{9,15},{10,... | collective-permute-start | bytes 172040 | tf_op jit(solution)/shard_map/ppermute | solution.py:273
  8.4 0.5 %collective-permute-start.5 = (bf16[3584,128]{1,0:T(8,128)(2,1)S(1)}, bf16[3584,128]{1,0:T(8,128)(2,1)S(1)}, u32[]{:S(2)}, u32[]{:S(2)}) collective-permute-start(bf16[3584,128]{1,0:T(8,128)(2,1)S(1)} %copy-done.1), channel_id=1, source_target_pairs={{0,1},{1,0},{2,3},{3,2},{4,5},{5,4},{6,7},{7,6},{8,9},{9,8},{10,11... | collective-permute-start | bytes 2752520 | tf_op jit(solution)/shard_map/ppermute | solution.py:278
  9.0 1.0 %collective-permute-done.3.two_ref = bf16[8,3584]{1,0:T(8,128)(2,1)S(1)} collective-permute-done((bf16[8,3584]{1,0:T(8,128)(2,1)S(1)}, bf16[8,3584]{1,0:T(8,128)(2,1)S(1)}, u32[]{:S(2)}, u32[]{:S(2)}) %collective-permute-start.3) | collective-permute-done | bytes 57376 | tf_op jit(solution)/shard_map/ppermute | solution.py:231
  10.0 1.5 %collective-permute-start.1 = (bf16[8,3584]{1,0:T(8,128)(2,1)S(1)}, bf16[8,3584]{1,0:T(8,128)(2,1)S(1)}, u32[]{:S(2)}, u32[]{:S(2)}) collective-permute-start(bf16[8,3584]{1,0:T(8,128)(2,1)S(1)} %shard_map.85.hop_ref), channel_id=1, source_target_pairs={{0,2},{2,0},{4,6},{6,4},{8,10},{10,8},{12,14},{14,12},{1,3},{3,1},... | collective-permute-start | bytes 172040 | tf_op jit(solution)/shard_map/ppermute | solution.py:231
  11.5 0.1 collective-permute-done.2.side_ref
  11.7 2.6 %collective-permute-done.1.passed_ref = bf16[8,3584]{1,0:T(8,128)(2,1)S(1)} collective-permute-done((bf16[8,3584]{1,0:T(8,128)(2,1)S(1)}, bf16[8,3584]{1,0:T(8,128)(2,1)S(1)}, u32[]{:S(2)}, u32[]{:S(2)}) %collective-permute-start.1) | collective-permute-done | bytes 57376 | tf_op jit(solution)/shard_map/ppermute | solution.py:231
  14.2 1.0 %shard_map.86 = (f32[8,3584]{1,0:T(8,128)S(1)}, bf16[8,3584]{1,0:T(8,128)(2,1)S(1)}, bf16[8,3584]{1,0:T(8,128)(2,1)S(1)}, f32[8,3584]{1,0:T(8,128)S(1)}, bf16[8,3584]{1,0:T(8,128)(2,1)S(1)}) custom-call(bf16[8,3584]{1,0:T(8,128)(2,1)S(1)} %shard_map.85.hop_ref, bf16[8,3584]{1,0:T(8,128)(2,1)S(1)} %collective-permute-done.1.passed_ref, ...), custom_call_target="tpu_custom_call" | custom-call | flops 1000000 | bytes 2000 | tf_op jit(solution)/shard_map/pallas_call | solution.py:221
  15.2 1.6 %collective-permute-start.9 = (bf16[8,3584]{1,0:T(8,128)(2,1)S(1)}, bf16[8,3584]{1,0:T(8,128)(2,1)S(1)}, u32[]{:S(2)}, u32[]{:S(2)}) collective-permute-start(bf16[8,3584]{1,0:T(8,128)(2,1)S(1)} %get-tuple-element.21), channel_id=1, source_target_pairs={{0,2},{2,0},{4,6},{6,4},{8,10},{10,8},{12,14},{14,12},{1,3},{3,1},... | collective-permute-start | bytes 172040 | tf_op jit(solution)/shard_map/ppermute | solution.py:231
  16.8 1.7 %collective-permute-start.7 = (bf16[8,3584]{1,0:T(8,128)(2,1)S(1)}, bf16[8,3584]{1,0:T(8,128)(2,1)S(1)}, u32[]{:S(2)}, u32[]{:S(2)}) collective-permute-start(bf16[8,3584]{1,0:T(8,128)(2,1)S(1)} %get-tuple-element.18), channel_id=1, source_target_pairs={{0,4},{2,6},{4,0},{6,2},{8,12},{10,14},{12,8},{14,10},{1,5},{3,7},... | collective-permute-start | bytes 172040 | tf_op jit(solution)/shard_map/ppermute | solution.py:231
  18.5 0.1 collective-permute-start.8
  18.6 1.4 %collective-permute-done.9.refs_1_ = bf16[8,3584]{1,0:T(8,128)(2,1)S(1)} collective-permute-done((bf16[8,3584]{1,0:T(8,128)(2,1)S(1)}, bf16[8,3584]{1,0:T(8,128)(2,1)S(1)}, u32[]{:S(2)}, u32[]{:S(2)}) %collective-permute-start.9) | collective-permute-done | bytes 57376 | tf_op jit(solution)/shard_map/ppermute | solution.py:231
  20.1 0.7 %collective-permute-start.10 = (bf16[8,3584]{1,0:T(8,128)(2,1)S(1)}, bf16[8,3584]{1,0:T(8,128)(2,1)S(1)}, u32[]{:S(2)}, u32[]{:S(2)}) collective-permute-start(bf16[8,3584]{1,0:T(8,128)(2,1)S(1)} %shard_map.87), channel_id=1, source_target_pairs={{0,8},{1,13},{2,10},{3,15},{4,12},{5,9},{6,14},{7,11},{8,0},{9,5},... | collective-permute-start | bytes 172040 | tf_op jit(solution)/shard_map/ppermute | solution.py:273
  20.8 0.2 collective-permute-done.7.two_ref
  21.0 1.7 %collective-permute-done.8.side_ref = bf16[8,3584]{1,0:T(8,128)(2,1)S(1)} collective-permute-done((bf16[8,3584]{1,0:T(8,128)(2,1)S(1)}, bf16[8,3584]{1,0:T(8,128)(2,1)S(1)}, u32[]{:S(2)}, u32[]{:S(2)}) %collective-permute-start.8) | collective-permute-done | bytes 57376 | tf_op jit(solution)/shard_map/ppermute | solution.py:273
  22.7 2.5 %collective-permute-done.10.back_ref = bf16[8,3584]{1,0:T(8,128)(2,1)S(1)} collective-permute-done((bf16[8,3584]{1,0:T(8,128)(2,1)S(1)}, bf16[8,3584]{1,0:T(8,128)(2,1)S(1)}, u32[]{:S(2)}, u32[]{:S(2)}) %collective-permute-start.10) | collective-permute-done | bytes 57376 | tf_op jit(solution)/shard_map/ppermute | solution.py:273
  25.4 0.6 %copy-done.6 = f32[2,8,1]{1,2,0:T(1,128)S(1)} copy-done((f32[2,8,1]{1,2,0:T(1,128)S(1)}, f32[2,8,1]{1,2,0:T(1,128)}, u32[]{:S(2)}) %copy-start.6) | copy-done | bytes 88
  25.9 0.1 shard_map.83.table_ref
  26.0 0.1 shard_map.89.base_ref
  26.2 0.4 %collective-permute-done.11.got_ref = bf16[16,1792]{1,0:T(8,128)(2,1)S(1)} collective-permute-done((bf16[16,1792]{1,0:T(8,128)(2,1)S(1)}, bf16[16,1792]{1,0:T(8,128)(2,1)S(1)}, u32[]{:S(2)}, u32[]{:S(2)}) %collective-permute-start.11) | collective-permute-done | bytes 57376 | tf_op jit(solution)/shard_map/ppermute | solution.py:306
  26.6 0.8 %shard_map.90 = bf16[2,8,1792]{2,1,0:T(8,128)(2,1)} custom-call(f32[2,8,1792]{2,1,0:T(8,128)S(1)} %shard_map.89.base_ref, f32[2,8,16]{2,1,0:T(8,128)S(1)} %shard_map.83.table_ref, bf16[16,1792]{1,0:T(8,128)(2,1)S(1)} %collective-permute-done.11.got_ref), custom_call_target="tpu_custom_call" | custom-call | tf_op jit(solution)/shard_map/pallas_call | solution.py:221
  (25 shorter events, 0.3 us)
Async XLA Ops:
  0.0 0.9 %copy-start.3 = (bf16[2,8,3584]{2,1,0:T(8,128)(2,1)S(1)}, bf16[2,8,3584]{2,1,0:T(8,128)(2,1)}, u32[]{:S(2)}) copy-start(bf16[2,8,3584]{2,1,0:T(8,128)(2,1)} %hidden_ref.3) | copy-start | bytes 344068
  0.0 0.9 %copy-start.7 = (bf16[3584]{0:T(1024)(128)(2,1)S(1)}, bf16[3584]{0:T(1024)(128)(2,1)}, u32[]{:S(2)}) copy-start(bf16[3584]{0:T(1024)(128)(2,1)} %gain_ref.1) | copy-start | bytes 21508
  0.0 0.9 %copy-start.5 = (s32[2,8,1]{1,2,0:T(1,128)S(1)}, s32[2,8,1]{1,2,0:T(1,128)}, u32[]{:S(2)}) copy-start(s32[2,8,1]{1,2,0:T(1,128)} %param.12) | copy-start | bytes 196
  0.0 0.9 %copy-start.4 = (s32[2,8,1]{1,2,0:T(1,128)S(1)}, s32[2,8,1]{1,2,0:T(1,128)}, u32[]{:S(2)}) copy-start(s32[2,8,1]{1,2,0:T(1,128)} %param.10) | copy-start | bytes 196
  0.9 7.5 %copy-start = (bf16[3584,128]{1,0:T(8,128)(2,1)S(1)}, bf16[3584,128]{1,0:T(8,128)(2,1)}, u32[]{:S(2)}) copy-start(bf16[3584,128]{1,0:T(8,128)(2,1)} %refs_0_.1) | copy-start | bytes 2752516
  0.9 7.5 %copy-start.1 = (bf16[3584,128]{1,0:T(8,128)(2,1)S(1)}, bf16[3584,128]{1,0:T(8,128)(2,1)}, u32[]{:S(2)}) copy-start(bf16[3584,128]{1,0:T(8,128)(2,1)} %refs_1_.1) | copy-start | bytes 2752516
  0.9 8.0 %copy-start.2 = (bf16[128,3584]{1,0:T(8,128)(2,1)S(1)}, bf16[128,3584]{1,0:T(8,128)(2,1)}, u32[]{:S(2)}) copy-start(bf16[128,3584]{1,0:T(8,128)(2,1)} %refs_2_.1) | copy-start | bytes 2752516
  1.3 7.7 %collective-permute-start = (bf16[8,3584]{1,0:T(8,128)(2,1)S(1)}, bf16[8,3584]{1,0:T(8,128)(2,1)S(1)}, u32[]{:S(2)}, u32[]{:S(2)}) collective-permute-start(bf16[8,3584]{1,0:T(8,128)(2,1)S(1)} %get-tuple-element.15), channel_id=1, source_target_pairs={{0,8},{1,13},{2,10},{3,15},{4,12},{5,9},{6,14},{7,11},{8,0},{9,5},... | collective-permute-start | bytes 172040 | tf_op jit(solution)/shard_map/ppermute | solution.py:273
  5.4 4.7 %collective-permute-start.3 = (bf16[8,3584]{1,0:T(8,128)(2,1)S(1)}, bf16[8,3584]{1,0:T(8,128)(2,1)S(1)}, u32[]{:S(2)}, u32[]{:S(2)}) collective-permute-start(bf16[8,3584]{1,0:T(8,128)(2,1)S(1)} %get-tuple-element.16.own_ref), channel_id=1, source_target_pairs={{0,4},{2,6},{4,0},{6,2},{8,12},{10,14},{12,8},{14,10},{1,5},{3,7},... | collective-permute-start | bytes 172040 | tf_op jit(solution)/shard_map/ppermute | solution.py:231
  6.9 4.7 %collective-permute-start.2 = (bf16[8,3584]{1,0:T(8,128)(2,1)S(1)}, bf16[8,3584]{1,0:T(8,128)(2,1)S(1)}, u32[]{:S(2)}, u32[]{:S(2)}) collective-permute-start(bf16[8,3584]{1,0:T(8,128)(2,1)S(1)} %get-tuple-element.16.own_ref), channel_id=1, source_target_pairs={{0,2},{1,7},{2,0},{3,5},{4,6},{5,3},{6,4},{7,1},{8,10},{9,15},{10,... | collective-permute-start | bytes 172040 | tf_op jit(solution)/shard_map/ppermute | solution.py:273
  8.4 5.8 %collective-permute-start.4 = (bf16[3584,128]{1,0:T(8,128)(2,1)S(1)}, bf16[3584,128]{1,0:T(8,128)(2,1)S(1)}, u32[]{:S(2)}, u32[]{:S(2)}) collective-permute-start(bf16[3584,128]{1,0:T(8,128)(2,1)S(1)} %copy-done), channel_id=1, source_target_pairs={{0,1},{1,0},{2,3},{3,2},{4,5},{5,4},{6,7},{7,6},{8,9},{9,8},{10,11... | collective-permute-start | bytes 2752520 | tf_op jit(solution)/shard_map/ppermute | solution.py:278
  8.4 5.8 %collective-permute-start.5 = (bf16[3584,128]{1,0:T(8,128)(2,1)S(1)}, bf16[3584,128]{1,0:T(8,128)(2,1)S(1)}, u32[]{:S(2)}, u32[]{:S(2)}) collective-permute-start(bf16[3584,128]{1,0:T(8,128)(2,1)S(1)} %copy-done.1), channel_id=1, source_target_pairs={{0,1},{1,0},{2,3},{3,2},{4,5},{5,4},{6,7},{7,6},{8,9},{9,8},{10,11... | collective-permute-start | bytes 2752520 | tf_op jit(solution)/shard_map/ppermute | solution.py:278
  8.9 5.3 %collective-permute-start.6 = (bf16[128,3584]{1,0:T(8,128)(2,1)S(1)}, bf16[128,3584]{1,0:T(8,128)(2,1)S(1)}, u32[]{:S(2)}, u32[]{:S(2)}) collective-permute-start(bf16[128,3584]{1,0:T(8,128)(2,1)S(1)} %copy-done.2), channel_id=1, source_target_pairs={{0,1},{1,0},{2,3},{3,2},{4,5},{5,4},{6,7},{7,6},{8,9},{9,8},{10,11... | collective-permute-start | bytes 2752520 | tf_op jit(solution)/shard_map/ppermute | solution.py:278
  10.0 4.2 %collective-permute-start.1 = (bf16[8,3584]{1,0:T(8,128)(2,1)S(1)}, bf16[8,3584]{1,0:T(8,128)(2,1)S(1)}, u32[]{:S(2)}, u32[]{:S(2)}) collective-permute-start(bf16[8,3584]{1,0:T(8,128)(2,1)S(1)} %shard_map.85.hop_ref), channel_id=1, source_target_pairs={{0,2},{2,0},{4,6},{6,4},{8,10},{10,8},{12,14},{14,12},{1,3},{3,1},... | collective-permute-start | bytes 172040 | tf_op jit(solution)/shard_map/ppermute | solution.py:231
  15.2 4.9 %collective-permute-start.9 = (bf16[8,3584]{1,0:T(8,128)(2,1)S(1)}, bf16[8,3584]{1,0:T(8,128)(2,1)S(1)}, u32[]{:S(2)}, u32[]{:S(2)}) collective-permute-start(bf16[8,3584]{1,0:T(8,128)(2,1)S(1)} %get-tuple-element.21), channel_id=1, source_target_pairs={{0,2},{2,0},{4,6},{6,4},{8,10},{10,8},{12,14},{14,12},{1,3},{3,1},... | collective-permute-start | bytes 172040 | tf_op jit(solution)/shard_map/ppermute | solution.py:231
  16.8 4.2 %collective-permute-start.7 = (bf16[8,3584]{1,0:T(8,128)(2,1)S(1)}, bf16[8,3584]{1,0:T(8,128)(2,1)S(1)}, u32[]{:S(2)}, u32[]{:S(2)}) collective-permute-start(bf16[8,3584]{1,0:T(8,128)(2,1)S(1)} %get-tuple-element.18), channel_id=1, source_target_pairs={{0,4},{2,6},{4,0},{6,2},{8,12},{10,14},{12,8},{14,10},{1,5},{3,7},... | collective-permute-start | bytes 172040 | tf_op jit(solution)/shard_map/ppermute | solution.py:231
  18.5 4.2 %collective-permute-start.8 = (bf16[8,3584]{1,0:T(8,128)(2,1)S(1)}, bf16[8,3584]{1,0:T(8,128)(2,1)S(1)}, u32[]{:S(2)}, u32[]{:S(2)}) collective-permute-start(bf16[8,3584]{1,0:T(8,128)(2,1)S(1)} %get-tuple-element.19), channel_id=1, source_target_pairs={{0,2},{1,7},{2,0},{3,5},{4,6},{5,3},{6,4},{7,1},{8,10},{9,15},{10,... | collective-permute-start | bytes 172040 | tf_op jit(solution)/shard_map/ppermute | solution.py:273
  20.1 5.1 %collective-permute-start.10 = (bf16[8,3584]{1,0:T(8,128)(2,1)S(1)}, bf16[8,3584]{1,0:T(8,128)(2,1)S(1)}, u32[]{:S(2)}, u32[]{:S(2)}) collective-permute-start(bf16[8,3584]{1,0:T(8,128)(2,1)S(1)} %shard_map.87), channel_id=1, source_target_pairs={{0,8},{1,13},{2,10},{3,15},{4,12},{5,9},{6,14},{7,11},{8,0},{9,5},... | collective-permute-start | bytes 172040 | tf_op jit(solution)/shard_map/ppermute | solution.py:273
  25.3 0.7 %copy-start.6 = (f32[2,8,1]{1,2,0:T(1,128)S(1)}, f32[2,8,1]{1,2,0:T(1,128)}, u32[]{:S(2)}) copy-start(f32[2,8,1]{1,2,0:T(1,128)} %param.11) | copy-start | bytes 196
  25.3 1.3 %collective-permute-start.11 = (bf16[16,1792]{1,0:T(8,128)(2,1)S(1)}, bf16[16,1792]{1,0:T(8,128)(2,1)S(1)}, u32[]{:S(2)}, u32[]{:S(2)}) collective-permute-start(bf16[16,1792]{1,0:T(8,128)(2,1)S(1)} %get-tuple-element.24), channel_id=1, source_target_pairs={{0,1},{1,0},{2,3},{3,2},{4,5},{5,4},{6,7},{7,6},{8,9},{9,8},{10,11... | collective-permute-start | bytes 172040 | tf_op jit(solution)/shard_map/ppermute | solution.py:306
